TPU v7x, 32 devices: a whole 2x2x4 slice. The times are simulated.
32 devices in a mesh: grp: 2 (over x), orbit: 16 (over z, y, core).
Axes of the slice: x: 2, y: 2, z: 4, core: 2. Of those that a mesh axis runs over, the one named last changes fastest.
Arguments:
- solution: float32 [256, 8, 16, 128], P(('grp', 'orbit')), parts along dimension 0, may hold values from -6 to 6
- residual: float32 [256, 8, 16, 128], P(('grp', 'orbit')), parts along dimension 0, may hold values from -9 to 9
- direction: float32 [256, 8, 16, 128], P(('grp', 'orbit')), parts along dimension 0, may hold values from -9 to 9
- jacobian: bfloat16 [256, 24, 128, 128], P(('grp', 'orbit')), parts along dimension 0, may hold values from -0.109375 to 0.109375
- crossing: int32 [256, 24], P(('grp', 'orbit')), parts along dimension 0, may hold values from 0 to 127
- tile_count: int32 [32], P(('grp', 'orbit')), parts along dimension 0, may hold values from 1 to 8, as said below
- sightline_weight: float32 [256, 128], P(('grp', 'orbit')), parts along dimension 0, may hold values from 1 to 8
- length_class: int32 [256], P('grp'), parts along dimension 0, may hold values from 0 to 3
- smooth_weight: float32 [8, 128], replicated, may hold values from 0.2 to 2
Outputs:
- solution_next: float32 [256, 8, 16, 128], P(('grp', 'orbit')), parts along dimension 0
- residual_next: float32 [256, 8, 16, 128], P(('grp', 'orbit')), parts along dimension 0
- step_length: float32 [32], P('grp'), parts along dimension 0
There are 2 independent parts, one for each index of `grp`. A program takes and returns all parts, laid end to end along the dimension named above; an argument that names none is the same for every part. Nothing has to cross between parts.
Inputs may be any that keep to these rules, and one draw needn't show every extreme that they name: `tile_count`: slots at or above this count hold padding that carries no weight; in every draw some device has 8 live tiles. `crossing`: the window of a device starts 4 columns before its own block and covers 2 * 8 columns.
All inputs are finite; a program needn't handle non-finite values.
Results may differ from a plain program's by a relative error of at most 0.00075.
Values may be sent and summed in bfloat16 or wider, within the bound.
No kernel may reach another device: no remote copies, remote signals or barrier semaphores. Data moves between devices by JAX's collectives and lax.ppermute only.
A program may use at most 64 MiB of HBM per device.

v0:
```python
import jax
import jax.numpy as jnp
from jax import lax
from jax.sharding import PartitionSpec as P

LEVELS = 120
CLASSES = 4
REACH = 8


epsilon = 1e-06


def extended(array, sides, width):
    for axis, dim in sides:
        count, length = (lax.axis_size(axis), array.shape[dim])
        up = [(i, (i + 1) % count) for i in range(count)]
        down = [(j, i) for i, j in up]
        last = lax.slice_in_dim(array, length - width, length, axis=dim)
        leading = lax.slice_in_dim(array, 0, width, axis=dim)
        before = lax.ppermute(last, axis, up)
        after = lax.ppermute(leading, axis, down)
        array = jnp.concatenate([before, array, after], axis=dim)
    return array


def shifted(array, axis, by):
    count = lax.axis_size(axis)
    return lax.ppermute(array, axis, [(i, (i + by) % count) for i in range(count)])


def banded_matrix(window_lengths, out_cols, reach):
    width = out_cols + 2 * reach
    out_index = jnp.arange(out_cols)[:, None]
    position = jnp.arange(width)[None, :]
    offset = position - out_index - reach
    distance = jnp.abs(offset)
    safe = jnp.maximum(distance, 1).astype(jnp.float32)
    reciprocal = 1.0 / (safe * safe)
    own_lengths = lax.dynamic_slice_in_dim(window_lengths, reach, out_cols)[:, None]
    back_lengths = window_lengths[None, :]
    live_forward = (offset > 0) & (distance <= reach) & (distance <= own_lengths)
    live_back = (offset < 0) & (distance <= reach) & (distance <= back_lengths)
    beside = jnp.where(live_forward | live_back, -reciprocal, 0.0)
    centre = -jnp.sum(beside, axis=1)
    return beside + jnp.where(offset == 0, centre[:, None], 0.0)


def rim_stencil(padded, flat_dir, length_class, block_cols):
    first_col = lax.axis_index("orbit") * block_cols
    total_cols = length_class.shape[0]
    doubled = jnp.concatenate([length_class, length_class])
    nearby = lax.dynamic_slice_in_dim(
        doubled, (first_col - REACH) % total_cols, block_cols + 2 * REACH
    )
    lengths = (nearby + 1) * REACH // CLASSES
    stencil = banded_matrix(lengths, block_cols, REACH)
    result = jnp.dot(
        stencil,
        padded.reshape(block_cols + 2 * REACH, -1),
        precision=lax.Precision.HIGHEST,
        preferred_element_type=jnp.float32,
    )
    return result.reshape(flat_dir.shape)


def local(
    solution,
    residual,
    direction,
    jacobian,
    crossing,
    tile_count,
    sightline_weight,
    length_class,
    smooth_weight,
):
    block_cols, species, probes, tile_width = direction.shape
    rim_cols = block_cols // 2
    level_mask = (jnp.arange(tile_width) < LEVELS).astype(jnp.float32)
    masked_dir = direction * level_mask
    masked_res = residual * level_mask
    flat_dir = masked_dir.reshape(block_cols, species * probes, tile_width)
    rounded_dir = masked_dir.astype(jnp.bfloat16)
    window = extended(rounded_dir, (("orbit", 0),), rim_cols)
    flattened = window.reshape(2 * block_cols * species, probes, tile_width)
    window_tiles = flattened.shape[0]
    tile_slots, crossings = crossing.shape
    live_count = tile_count[0]
    gathered = jnp.take(flattened, crossing, axis=0)
    integrals = jnp.einsum("tjrl,tjnl->tnr", jacobian, gathered, preferred_element_type=jnp.float32)
    alive = (jnp.arange(tile_slots) < live_count).astype(jnp.float32)
    row_weight = alive[:, None] * sightline_weight
    weighted = (row_weight[:, None, :] * integrals).astype(jnp.bfloat16)
    contribution = jnp.einsum(
        "tjrl,tnr->tjnl", jacobian, weighted, preferred_element_type=jnp.float32
    )
    selector = (crossing.reshape(-1)[:, None] == jnp.arange(window_tiles)[None, :]).astype(
        jnp.float32
    )
    window_back = jnp.dot(
        selector.T,
        contribution.reshape(tile_slots * crossings, probes * tile_width),
        precision=lax.Precision.HIGHEST,
        preferred_element_type=jnp.float32,
    )
    window_back = window_back.reshape(2 * block_cols, species, probes, tile_width)
    left_rim = window_back[:rim_cols]
    own_part = window_back[rim_cols : rim_cols + block_cols]
    right_rim = window_back[rim_cols + block_cols :]
    arrivals = []
    for outgoing, offset in ((right_rim, 1), (left_rim, -1)):
        arrivals.append(
            shifted(outgoing.astype(jnp.bfloat16), "orbit", offset).astype(outgoing.dtype)
        )
    projected = own_part + jnp.concatenate(arrivals, axis=0)
    deep = extended(flat_dir, (("orbit", 0),), REACH)
    smoothing = rim_stencil(deep, flat_dir, length_class, block_cols)
    smoothing = smoothing.reshape(block_cols, species, probes, tile_width)
    image = level_mask * (projected + smooth_weight[None, :, None, :] * (masked_dir + smoothing))
    residual_norm, curvature = lax.psum(
        (
            jnp.sum(masked_res * masked_res, axis=(0, 1, 3)),
            jnp.sum(masked_dir * image, axis=(0, 1, 3)),
        ),
        "orbit",
    )
    step_length = residual_norm / (curvature + epsilon)
    expand = step_length[None, None, :, None]
    solution_next = level_mask * (solution + expand * masked_dir)
    residual_next = masked_res - expand * image
    return (solution_next, residual_next, step_length)


def solution(mesh):
    placed = (
        P(("grp", "orbit"), None, None, None),
        P(("grp", "orbit"), None, None, None),
        P(("grp", "orbit"), None, None, None),
        P(("grp", "orbit"), None, None, None),
        P(("grp", "orbit"), None),
        P(("grp", "orbit")),
        P(("grp", "orbit"), None),
        P("grp"),
        P(),
    )
    return jax.shard_map(
        local,
        mesh=mesh,
        in_specs=placed,
        out_specs=(
            P(("grp", "orbit"), None, None, None),
            P(("grp", "orbit"), None, None, None),
            P("grp"),
        ),
        check_vma=False,
    )
```

profile of v0, /device:TPU:0, one launch (start us, length us, event | category | flops | bytes accessed | tf_op | source)
XLA Modules:
  0.0 72.7 jit_solution(13729497194905772035)
XLA Ops:
  0.7 1.9 %fusion.57 = (bf16[8,8,16,128]{3,0,2,1:T(8,128)(2,1)S(1)}, f32[8,8,16,128]{3,0,2,1:T(8,128)S(1)}, f32[16]{0:T(128)S(1)}) fusion(f32[128]{0:T(128)S(1)} %compare_convert_fusion.1, f32[8,8,16,128]{3,2,1,0:T(8,128)} %param.11, f32[8,8,16,128]{3,2,1,0:T(8,128)} %param.10), kind=kLoop, calls=%fused_computation.75 | loop fusion | flops 655344 | bytes 1835584 | tf_op jit(solution)/shard_map/convert_element_type | solution.py:84
  2.6 5.5 %collective-permute-start.5 = (f32[8,128,128]{2,0,1:T(8,128)S(1)}, f32[8,128,128]{2,0,1:T(8,128)S(1)}, u32[]{:S(2)}, u32[]{:S(2)}) collective-permute-start(f32[8,128,128]{2,0,1:T(8,128)S(1)} %bitcast.55), channel_id=1, source_target_pairs={{1,0},{2,1},{3,2},{4,3},{5,4},{6,5},{7,6},{8,7},{9,8},{10,9},{11,1... | collective-permute-start | bytes 1572872 | tf_op jit(solution)/shard_map/ppermute | solution.py:22
  8.1 0.0 collective-permute-start.4
  8.1 0.1 fusion.58
  8.2 0.1 collective-permute-start
  8.3 4.5 %collective-permute-start.1 = (bf16[4,8,16,128]{3,0,2,1:T(4,128)(2,1)S(1)}, bf16[4,8,16,128]{3,0,2,1:T(4,128)(2,1)S(1)}, u32[]{:S(2)}, u32[]{:S(2)}) collective-permute-start(bf16[4,8,16,128]{3,0,2,1:T(4,128)(2,1)S(1)} %get-tuple-element.16), channel_id=1, source_target_pairs={{1,0},{2,1},{3,2},{4,3},{5,4},{6,5},{7,6},{8,7},{9,8},{10,9},{11,1... | collective-permute-start | bytes 393224 | tf_op jit(solution)/shard_map/ppermute | solution.py:22
  13.5 0.1 and_select_fusion
  13.6 0.1 dynamic_slice.7
  13.6 0.1 broadcast_multiply_fusion
  13.7 0.2 fusion.48
  13.9 0.1 eq.20
  14.0 0.1 reshape.56
  14.1 6.8 %collective-permute-done = bf16[4,8,16,128]{3,0,2,1:T(4,128)(2,1)S(1)} collective-permute-done((bf16[4,8,16,128]{3,0,2,1:T(4,128)(2,1)S(1)}, bf16[4,8,16,128]{3,0,2,1:T(4,128)(2,1)S(1)}, u32[]{:S(2)}, u32[]{:S(2)}) %collective-permute-start) | collective-permute-done | bytes 131104 | tf_op jit(solution)/shard_map/ppermute | solution.py:21
  20.9 0.3 pad_maximum_fusion
  21.2 0.1 copy.22
  21.3 0.8 %gather_fusion = bf16[192,16,128]{2,1,0:T(8,128)(2,1)S(1)} fusion(bf16[128,16,128]{2,1,0:T(8,128)(2,1)S(1)} %bitcast.60, s32[1024]{0:T(1024)S(1)} %pad_clamp_fusion), kind=kCustom, calls=%fused_computation | custom fusion | bytes 1573632 | tf_op jit(solution)/shard_map/jit(_take)/gather | solution.py:90
  22.1 7.2 %fusion.14 = f32[8,16,24,128]{3,1,2,0:T(8,128)S(1)} fusion(bf16[8,24,128,128]{3,2,1,0:T(8,128)(2,1)} %param.12, bf16[8,24,16,128]{3,2,1,0:T(8,128)(2,1)S(1)} %bitcast.61, pred[8,24]{1,0:T(8,128)(4,1)S(1)} %compare_and_fusion, f32[8,128]{1,0:T(8,128)S(1)} %broadcast_multiply_fusion), kind=kOutput, calls=%fused_computation.13 | convolution fusion | flops 201752576 | bytes 8655040 | tf_op jit(solution)/shard_map/tjrl,tnr->tjnl/dot_general | solution.py:95
  29.3 1.2 %fusion.59 = (bf16[128,2048]{1,0:T(8,128)(2,1)S(1)}, f32[128,2048]{1,0:T(8,128)S(1)}) fusion(f32[24,8,16,128]{3,2,1,0:T(8,128)S(1)} %bitcast.59, s32[192]{0:T(256)S(1)} %eq.20), kind=kOutput, calls=%fused_computation.77 | convolution fusion | flops 604266496 | bytes 3146496 | tf_op jit(solution)/shard_map/dot_general | solution.py:101
  30.6 0.1 copy.23
  30.7 0.1 copy.24
  30.8 0.1 collective-permute-start.3
  30.9 0.5 collective-permute-start.2
  31.4 1.1 %maximum_bitcast_fusion = f32[3,8,128,128]{3,1,2,0:T(8,128)S(1)} fusion(f32[8,16384]{1,0:T(8,128)S(1)} %bitcast.62, f32[8,16384]{1,0:T(8,128)S(1)} %bitcast.57, f32[8,16384]{1,0:T(8,128)} %bitcast.14), kind=kLoop, calls=%fused_computation.4 | loop fusion | flops 786432 | bytes 3145728
  32.6 0.0 copy-start.3
  32.6 0.3 copy.34
  32.9 0.5 collective-permute-done.3
  33.4 5.1 %collective-permute-done.2 = bf16[4,8,16,128]{3,0,2,1:T(4,128)(2,1)S(1)} collective-permute-done((bf16[4,8,16,128]{3,0,2,1:T(4,128)(2,1)S(1)}, bf16[4,8,16,128]{3,0,2,1:T(4,128)(2,1)S(1)}, u32[]{:S(2)}, u32[]{:S(2)}) %collective-permute-start.2) | collective-permute-done | bytes 131104 | tf_op jit(solution)/shard_map/ppermute | solution.py:29
  38.5 2.2 %multiply_reduce_fusion = (f32[16]{0:T(128)S(1)}, f32[8,8,16,128]{3,0,2,1:T(8,128)S(1)}) fusion(f32[8,8,16,128]{3,0,2,1:T(8,128)S(1)} %get-tuple-element.12, f32[8,16,128,24]{2,1,0,3:T(8,128)S(1)} %bitcast.58, f32[8]{0:T(128)S(1)} %neg.11, s32[24]{0:T(128)S(1)} %and_select_fusion, s32[8]{0:T(128)S(1)} %dynamic_slice.7, f32[8,128]{1,0:T(8,128)S(1)} %copy-done.3, ...), kind=kOutput, calls=%fused_computation.26 | convolution fusion | flops 39194736 | bytes 3412704 | tf_op jit(solution)/shard_map/dot_general | solution.py:58
  40.7 29.5 %all-reduce = (f32[16]{0:T(128)S(1)}, f32[16]{0:T(128)S(1)}) all-reduce(f32[16]{0:T(128)S(1)} %get-tuple-element.19, f32[16]{0:T(128)S(1)} %get-tuple-element.22), channel_id=1, replica_groups=mesh['grp'=2,'orbit'=16] {'orbit'}, use_global_device_ids=true, to_apply=%region_1.2 | all-reduce | flops 32 | bytes 256 | tf_op jit(solution)/shard_map/psum | solution.py:121
  70.2 0.6 multiply_subtract_fusion
  70.9 0.9 %copy.29 = f32[8,8,16,128]{3,2,1,0:T(8,128)} copy(f32[8,8,16,128]{3,0,2,1:T(8,128)S(1)} %get-tuple-element.17) | data formatting | bytes 1048576
  71.8 0.9 %copy.28 = f32[8,8,16,128]{3,2,1,0:T(8,128)} copy(f32[8,8,16,128]{3,0,2,1:T(8,128)S(1)} %get-tuple-element.18) | data formatting | bytes 1048576
  (26 shorter events, 0.1 us)
Async XLA Ops:
  0.6 12.1 %copy-start.2 = (s32[8,24]{1,0:T(8,128)S(1)}, s32[8,24]{1,0:T(8,128)}, u32[]{:S(2)}) copy-start(s32[8,24]{1,0:T(8,128)} %param.13) | copy-start | bytes 2308
  0.6 12.8 %copy-start.6 = (s32[128]{0:T(128)S(1)}, s32[128]{0:T(128)}, u32[]{:S(2)}) copy-start(s32[128]{0:T(128)} %param.16) | copy-start | bytes 1540
  0.7 13.0 %copy-start.4 = (f32[8,128]{1,0:T(8,128)S(1)}, f32[8,128]{1,0:T(8,128)}, u32[]{:S(2)}) copy-start(f32[8,128]{1,0:T(8,128)} %param.15) | copy-start | bytes 12292
  2.6 28.8 %collective-permute-start.5 = (f32[8,128,128]{2,0,1:T(8,128)S(1)}, f32[8,128,128]{2,0,1:T(8,128)S(1)}, u32[]{:S(2)}, u32[]{:S(2)}) collective-permute-start(f32[8,128,128]{2,0,1:T(8,128)S(1)} %bitcast.55), channel_id=1, source_target_pairs={{1,0},{2,1},{3,2},{4,3},{5,4},{6,5},{7,6},{8,7},{9,8},{10,9},{11,1... | collective-permute-start | bytes 1572872 | tf_op jit(solution)/shard_map/ppermute | solution.py:22
  8.1 23.4 %collective-permute-start.4 = (f32[8,128,128]{2,0,1:T(8,128)S(1)}, f32[8,128,128]{2,0,1:T(8,128)}, u32[]{:S(2)}, u32[]{:S(2)}) collective-permute-start(f32[8,128,128]{2,0,1:T(8,128)S(1)} %bitcast.56), channel_id=1, source_target_pairs={{0,1},{1,2},{2,3},{3,4},{4,5},{5,6},{6,7},{7,8},{8,9},{9,10},{10,1... | collective-permute-start | bytes 1572872 | tf_op jit(solution)/shard_map/ppermute | solution.py:21
  8.2 12.7 %collective-permute-start = (bf16[4,8,16,128]{3,0,2,1:T(4,128)(2,1)S(1)}, bf16[4,8,16,128]{3,0,2,1:T(4,128)(2,1)S(1)}, u32[]{:S(2)}, u32[]{:S(2)}) collective-permute-start(bf16[4,8,16,128]{3,0,2,1:T(4,128)(2,1)S(1)} %get-tuple-element.15), channel_id=1, source_target_pairs={{0,1},{1,2},{2,3},{3,4},{4,5},{5,6},{6,7},{7,8},{8,9},{9,10},{10,1... | collective-permute-start | bytes 393224 | tf_op jit(solution)/shard_map/ppermute | solution.py:21
  8.3 12.6 %collective-permute-start.1 = (bf16[4,8,16,128]{3,0,2,1:T(4,128)(2,1)S(1)}, bf16[4,8,16,128]{3,0,2,1:T(4,128)(2,1)S(1)}, u32[]{:S(2)}, u32[]{:S(2)}) collective-permute-start(bf16[4,8,16,128]{3,0,2,1:T(4,128)(2,1)S(1)} %get-tuple-element.16), channel_id=1, source_target_pairs={{1,0},{2,1},{3,2},{4,3},{5,4},{6,5},{7,6},{8,7},{9,8},{10,9},{11,1... | collective-permute-start | bytes 393224 | tf_op jit(solution)/shard_map/ppermute | solution.py:22
  30.8 2.6 %collective-permute-start.3 = (bf16[4,8,16,128]{3,0,2,1:T(4,128)(2,1)S(1)}, bf16[4,8,16,128]{3,0,2,1:T(4,128)(2,1)S(1)}, u32[]{:S(2)}, u32[]{:S(2)}) collective-permute-start(bf16[4,8,16,128]{3,0,2,1:T(4,128)(2,1)S(1)} %copy.24), channel_id=1, source_target_pairs={{0,15},{1,0},{2,1},{3,2},{4,3},{5,4},{6,5},{7,6},{8,7},{9,8},{10,9... | collective-permute-start | bytes 393224 | tf_op jit(solution)/shard_map/ppermute | solution.py:29
  30.9 7.6 %collective-permute-start.2 = (bf16[4,8,16,128]{3,0,2,1:T(4,128)(2,1)S(1)}, bf16[4,8,16,128]{3,0,2,1:T(4,128)(2,1)S(1)}, u32[]{:S(2)}, u32[]{:S(2)}) collective-permute-start(bf16[4,8,16,128]{3,0,2,1:T(4,128)(2,1)S(1)} %copy.23), channel_id=1, source_target_pairs={{0,1},{1,2},{2,3},{3,4},{4,5},{5,6},{6,7},{7,8},{8,9},{9,10},{10,1... | collective-permute-start | bytes 393224 | tf_op jit(solution)/shard_map/ppermute | solution.py:29
  32.6 5.9 %copy-start.3 = (f32[8,128]{1,0:T(8,128)S(1)}, f32[8,128]{1,0:T(8,128)}, u32[]{:S(2)}) copy-start(f32[8,128]{1,0:T(8,128)} %param.17) | copy-start | bytes 12292
  38.5 31.7 %copy-start = (f32[8,8,16,128]{3,2,1,0:T(8,128)S(1)}, f32[8,8,16,128]{3,2,1,0:T(8,128)}, u32[]{:S(2)}) copy-start(f32[8,8,16,128]{3,2,1,0:T(8,128)} %param.10) | copy-start | bytes 1572868
  38.5 31.7 %copy-start.1 = (f32[8,8,16,128]{3,2,1,0:T(8,128)S(1)}, f32[8,8,16,128]{3,2,1,0:T(8,128)}, u32[]{:S(2)}) copy-start(f32[8,8,16,128]{3,2,1,0:T(8,128)} %param.9) | copy-start | bytes 1572868
  70.2 0.7 copy-start.5
where the time goes:
time: 72.9 us; the launch traced here: 72.7 us
  blocking collectives  29.5 us (40%)
  waiting for transfers between devices  12.4 us (17%)
  matrix products  10.7 us (15%)
  starting transfers between devices  10.6 us (15%)
  other arithmetic  4.39 us (6%)
  local copies, waits for them, and re-layouts  3.61 us (5%)
  between operations  1.51 us (2%)
    psum x1, blocking collectives, local(): lax.psum((jnp.sum(masked_res * masked_res, axis=(0, 1, 3)), jnp.sum(maske...  29.5 us
    ppermute x2, starting transfers between devices, extended(): after = lax.ppermute(leading, axis, down)  9.97 us
    dot_general x1, matrix products, local(): jnp.einsum('tjrl,tnr->tjnl', jacobian, weighted, preferred_element_type=j...  7.2 us
    ppermute x2, waiting for transfers between devices, extended(): before = lax.ppermute(last, axis, up)  6.81 us
    ppermute x2, waiting for transfers between devices, shifted(): lax.ppermute(array, axis, [(i, (i + by) % count) for i in range(count)])  5.6 us
    dot_general x1, matrix products, rim_stencil(): jnp.dot(stencil, padded.reshape(block_cols + 2 * REACH, -1), precision=la...  2.24 us
    unnamed x17, local copies, waits for them, and re-layouts  2.08 us
    convert_element_type x1, other arithmetic, local(): rounded_dir = masked_dir.astype(jnp.bfloat16)  1.92 us
  transfers between devices with their start and end apart: 6, of which 3 were waited for; matrix products, arithmetic and copies ran while one was open for 17% of the time, Pallas kernels for 0%

commit v1 on v0

v1 whole, which is shorter than its diff:
```python
import functools

import jax
import jax.numpy as jnp
from jax import lax
from jax.experimental import pallas as pl
from jax.experimental.pallas import tpu as pltpu
from jax.sharding import PartitionSpec as P

LEVELS = 120
CLASSES = 4
REACH = 8
EPSILON = 1e-06
VMEM_LIMIT = 40 * 1024 * 1024

SMEM = functools.partial(pl.BlockSpec, memory_space=pltpu.SMEM)
VMEM = functools.partial(pl.BlockSpec, memory_space=pltpu.VMEM)
ANY = functools.partial(pl.BlockSpec, memory_space=pl.ANY)


def live_lanes(shape):
    return lax.broadcasted_iota(jnp.int32, shape, len(shape) - 1) < LEVELS


def masked(values):
    return jnp.where(live_lanes(values.shape), values, 0.0)


def call(kernel, out_shape, in_specs, flops, moved, scratch=()):
    return pl.pallas_call(
        kernel,
        out_shape=out_shape,
        in_specs=in_specs,
        out_specs=jax.tree.map(lambda _: VMEM(), out_shape),
        scratch_shapes=list(scratch),
        compiler_params=pltpu.CompilerParams(vmem_limit_bytes=VMEM_LIMIT),
        cost_estimate=pl.CostEstimate(flops=flops, bytes_accessed=moved, transcendentals=0),
    )


def rounding_kernel(rim, direction, near_low, near_high, far_up, far_down):
    cols = direction.shape[0]
    for c in range(cols):
        value = masked(direction[c])
        high = value.astype(jnp.bfloat16)
        if c < rim:
            near_low[c] = high
            far_up[c] = high
        else:
            near_high[c - rim] = high
            far_down[c - rim] = high
        if c == 0:
            far_down[rim] = (value - high.astype(jnp.float32)).astype(jnp.bfloat16)
        if c == cols - 1:
            far_up[rim] = (value - high.astype(jnp.float32)).astype(jnp.bfloat16)


def coupling(classes, cols):
    total = classes.shape[0]
    first = lax.axis_index("orbit") * cols
    table = {}
    for c in range(-REACH, cols):
        length = (classes[lax.rem(first + c + total, total)] + 1) * REACH // CLASSES
        for k in range(1, REACH + 1):
            table[c, k] = jnp.where(k <= length, jnp.float32(1.0 / (k * k)), jnp.float32(0.0))
    return table


def between(table, c, other):
    return table[c, other - c] if other > c else table[other, c - other]


def inner_kernel(direction, residual, classes, inner, norm):
    cols = direction.shape[0]
    table = coupling(classes, cols)
    squares = jnp.zeros(norm.shape, jnp.float32)
    for c in range(cols):
        centre = jnp.float32(0.0)
        for k in range(1, REACH + 1):
            centre = centre + (table[c, k] + table[c - k, k])
        result = centre * masked(direction[c])
        for other in range(cols):
            if other != c and abs(other - c) <= REACH:
                result = result - between(table, c, other) * masked(direction[other])
        inner[c] = result
        mres = masked(residual[c])
        squares = squares + jnp.sum(mres * mres, axis=0)
    norm[...] = squares


def outer_kernel(
    rim, direction, inner, left_near, right_near, left_far, right_far, classes, smooth, norm, curved,
    base, sums, sides,
):
    cols = direction.shape[0]
    table = coupling(classes, cols)
    for c in range(rim):
        sides[c] = left_far[c].astype(jnp.float32)
        sides[rim + c] = left_near[c].astype(jnp.float32)
        sides[cols + c] = right_near[c].astype(jnp.float32)
        sides[cols + rim + c] = right_far[c].astype(jnp.float32)
    sides[cols - 1] += left_far[rim].astype(jnp.float32)
    sides[cols] += right_far[rim].astype(jnp.float32)
    total = curved[...]
    weight = smooth[...][:, None, :]
    for c in range(cols):
        result = inner[c]
        for other in list(range(-cols, 0)) + list(range(cols, 2 * cols)):
            if abs(other - c) <= REACH:
                place = other + cols if other < 0 else other
                result = result - between(table, c, other) * sides[place]
        value = masked(direction[c])
        result = weight * (value + result)
        base[c] = result
        total = total + jnp.sum(value * result, axis=0)
    lane = lax.broadcasted_iota(jnp.int32, sums.shape, 1)
    sums[...] = jnp.where(
        lane == 0,
        jnp.sum(norm[...], axis=1, keepdims=True),
        jnp.where(lane == 1, jnp.sum(total, axis=1, keepdims=True), 0.0),
    )


def forward_kernel(
    crossing, count, sight, left, low, high, right, jac_hbm, weighted, curved, window, jac, sems
):
    slots, crossings = crossing.shape
    copies = [pltpu.make_async_copy(jac_hbm.at[i], jac.at[i], sems.at[i]) for i in range(slots)]
    for copy in copies:
        copy.start()
    rim_tiles = left.shape[0]
    for place, part in enumerate((left, low, high, right)):
        window[pl.ds(place * rim_tiles, rim_tiles)] = part[...]
    total = jnp.zeros(curved.shape, jnp.float32)
    for i in range(slots):
        copies[i].wait()
        picked = jnp.concatenate([window[crossing[i, j]] for j in range(crossings)], axis=1)
        tiles = jnp.concatenate([jac[i, j] for j in range(crossings)], axis=1)
        integrals = lax.dot_general(
            picked, tiles, (((1,), (1,)), ((), ())), preferred_element_type=jnp.float32
        )
        row = sight[pl.ds(i, 1), :] * jnp.where(i < count[0], 1.0, 0.0)
        product = (row * integrals).astype(jnp.bfloat16)
        weighted[i] = product
        total = total + product.astype(jnp.float32) * integrals
    curved[...] = total


def backward_kernel(crossing, weighted, jac_hbm, own, left, right, sums, jac, sems):
    slots, crossings = crossing.shape
    copies = [pltpu.make_async_copy(jac_hbm.at[i], jac.at[i], sems.at[i]) for i in range(slots)]
    for copy in copies:
        copy.start()
    sums[...] = jnp.zeros(sums.shape, jnp.float32)
    tile = jac.shape[-1]
    for i in range(slots):
        copies[i].wait()
        tiles = jnp.concatenate([jac[i, j] for j in range(crossings)], axis=1)
        terms = jnp.dot(weighted[i], tiles, preferred_element_type=jnp.float32)
        for j in range(crossings):
            sums[crossing[i, j]] += terms[:, j * tile : (j + 1) * tile]
    rim_tiles, own_tiles = left.shape[0], own.shape[0]
    left[...] = sums[pl.ds(0, rim_tiles)].astype(left.dtype)
    right[...] = sums[pl.ds(rim_tiles + own_tiles, rim_tiles)].astype(right.dtype)
    own[...] = sums[pl.ds(rim_tiles, own_tiles)]


def final_kernel(
    rim, solution, residual, direction, base, own, from_left, from_right, sums,
    solution_next, residual_next, step_length,
):
    norm = sums[:, 0:1]
    curvature = sums[:, 1:2]
    step = norm / (curvature + EPSILON)
    step_length[...] = step
    cols = direction.shape[0]
    wide = jnp.broadcast_to(step, direction.shape[2:])[None]
    for c in range(cols):
        arrived = from_left[c] if c < rim else from_right[c - rim]
        image = masked(base[c] + (own[c] + arrived.astype(jnp.float32)))
        solution_next[c] = masked(solution[c] + wide * direction[c])
        residual_next[c] = masked(residual[c]) - wide * image


def shifted(array, by):
    count = lax.axis_size("orbit")
    return lax.ppermute(array, "orbit", [(i, (i + by) % count) for i in range(count)])


def summed(array):
    count = lax.axis_size("orbit")
    if count & (count - 1):
        return lax.psum(array, "orbit")
    bit = 1
    while bit < count:
        array = array + lax.ppermute(array, "orbit", [(i, i ^ bit) for i in range(count)])
        bit *= 2
    return array


def local(
    solution, residual, direction, jacobian, crossing, tile_count, sightline_weight,
    length_class, smooth_weight,
):
    cols, species, probes, width = direction.shape
    rim = cols // 2
    slots, crossings = crossing.shape
    f32, bf16 = jnp.float32, jnp.bfloat16
    shape = jax.ShapeDtypeStruct
    column = (species, probes, width)
    elements = direction.size
    scratch_jac = [pltpu.VMEM(jacobian.shape, bf16), pltpu.SemaphoreType.DMA((slots,))]
    dot_flops = 2 * jacobian.size * probes

    near = shape((rim,) + column, bf16)
    far = shape((rim + 1,) + column, bf16)
    near_low, near_high, far_up, far_down = call(
        functools.partial(rounding_kernel, rim),
        (near, near, far, far),
        [VMEM()],
        2 * elements,
        9 * elements,
    )(direction)
    left_near = shifted(near_high, 1)
    right_near = shifted(near_low, -1)
    left_far = shifted(far_up, 1)
    right_far = shifted(far_down, -1)

    inner, norm = call(
        inner_kernel,
        (shape(direction.shape, f32), shape((probes, width), f32)),
        [VMEM(), VMEM(), SMEM()],
        20 * elements,
        12 * elements,
    )(direction, residual, length_class)

    flat = (rim * species, probes, width)
    weighted, curved = call(
        forward_kernel,
        (shape((slots, probes, width), bf16), shape((probes, width), f32)),
        [SMEM(), SMEM()] + [VMEM()] * 5 + [ANY()],
        dot_flops,
        2 * jacobian.size,
        [pltpu.VMEM((4 * rim * species, probes, width), bf16)] + scratch_jac,
    )(
        crossing, tile_count, sightline_weight, left_near.reshape(flat), near_low.reshape(flat),
        near_high.reshape(flat), right_near.reshape(flat), jacobian,
    )

    base, sums = call(
        functools.partial(outer_kernel, rim),
        (shape(direction.shape, f32), shape((probes, width), f32)),
        [VMEM()] * 6 + [SMEM()] + [VMEM()] * 3,
        20 * elements,
        16 * elements,
        [pltpu.VMEM((2 * cols,) + column, f32)],
    )(
        direction, inner, left_near, right_near, left_far, right_far, length_class, smooth_weight,
        norm, curved,
    )
    sums = summed(sums)

    own, to_left, to_right = call(
        backward_kernel,
        (
            shape((cols * species, probes, width), f32),
            shape(flat, bf16),
            shape(flat, bf16),
        ),
        [SMEM(), VMEM(), ANY()],
        dot_flops,
        2 * jacobian.size,
        [pltpu.VMEM((4 * rim * species, probes, width), f32)] + scratch_jac,
    )(crossing, weighted, jacobian)
    from_left = shifted(to_right, 1)
    from_right = shifted(to_left, -1)

    solution_next, residual_next, step_length = call(
        functools.partial(final_kernel, rim),
        (
            shape(direction.shape, f32),
            shape(direction.shape, f32),
            shape((probes, 1), f32),
        ),
        [VMEM()] * 8,
        8 * elements,
        28 * elements,
    )(
        solution, residual, direction, base, own.reshape(direction.shape),
        from_left.reshape(near.shape), from_right.reshape(near.shape), sums,
    )
    return solution_next, residual_next, step_length.reshape(probes)


def solution(mesh):
    wide = P(("grp", "orbit"), None, None, None)
    placed = (
        wide, wide, wide, wide,
        P(("grp", "orbit"), None),
        P(("grp", "orbit")),
        P(("grp", "orbit"), None),
        P("grp"),
        P(),
    )
    return jax.shard_map(
        local, mesh=mesh, in_specs=placed, out_specs=(wide, wide, P("grp")), check_vma=False
    )
```

time: 72.9 us -> 47 us (0.64)
  blocking collectives: 29.5 us -> 0 us
  Pallas kernels: 0 us -> 12 us
  matrix products: 10.7 us -> 0 us
  starting transfers between devices: 10.6 us -> 14.5 us
  other arithmetic: 4.39 us -> 0.64 us
  local copies, waits for them, and re-layouts: 3.61 us -> 5.22 us
    psum x1 -> x0, blocking collectives: 29.5 us -> none  [local(): lax.psum((jnp.sum(masked_res * masked_res, axis=(0, 1, 3)), jnp.sum(maske...]
    pallas_call x0 -> x6, Pallas kernels: none -> 12 us  [the longest x1 5.34 us: local(): call(forward_kernel, (shape((slots, probes, width), bf16), shape((probes,...]
    dot_general x3 -> x0, matrix products: 10.7 us -> none  [the longest x1 7.2 us: local(): jnp.einsum('tjrl,tnr->tjnl', jacobian, weighted, preferred_element_type=j...]
    ppermute x6 -> x10, starting transfers between devices: 10.6 us -> 14.5 us  [the longest x6 14.5 us: shifted(): lax.ppermute(array, 'orbit', [(i, (i + by) % count) for i in range(count)])]
    unnamed x17 -> x22, local copies, waits for them, and re-layouts: 2.08 us -> 5.22 us
    convert_element_type x3 -> x0, other arithmetic: 1.93 us -> none  [the longest x1 1.92 us: local(): rounded_dir = masked_dir.astype(jnp.bfloat16)]
    unnamed x1 -> x0, other arithmetic: 1.14 us -> none
    gather x1 -> x0, local copies, waits for them, and re-layouts: 0.78 us -> none  [local(): gathered = jnp.take(flattened, crossing, axis=0)]
  transfers between devices with their start and end apart: 6 -> 10, of which waited for: 3 -> 4; matrix products, arithmetic and copies ran while one was open for 17% -> 0% of each run, Pallas kernels for 0% -> 23%
where the time goes in v1:
time: 47 us; the launch traced here: 46.8 us
  starting transfers between devices  14.5 us (31%)
  waiting for transfers between devices  13 us (28%)
  Pallas kernels  12 us (26%)
  local copies, waits for them, and re-layouts  5.22 us (11%)
  between operations  1.43 us (3%)
  other arithmetic  0.64 us (1%)
    ppermute x6, starting transfers between devices, shifted(): lax.ppermute(array, 'orbit', [(i, (i + by) % count) for i in range(count)])  14.5 us
    ppermute x4, waiting for transfers between devices, summed(): lax.ppermute(array, 'orbit', [(i, i ^ bit) for i in range(count)])  13 us
    pallas_call x1, Pallas kernels, local(): call(forward_kernel, (shape((slots, probes, width), bf16), shape((probes,...  5.34 us
    unnamed x22, local copies, waits for them, and re-layouts  5.22 us
    pallas_call x1, Pallas kernels, local(): call(backward_kernel, (shape((cols * species, probes, width), f32), shape...  3.1 us
    pallas_call x1, Pallas kernels, local(): call(functools.partial(final_kernel, rim), (shape(direction.shape, f32),...  1.25 us
    pallas_call x1, Pallas kernels, local(): call(functools.partial(outer_kernel, rim), (shape(direction.shape, f32),...  1.16 us
    pallas_call x1, Pallas kernels, local(): call(inner_kernel, (shape(direction.shape, f32), shape((probes, width), f...  1.05 us
  transfers between devices with their start and end apart: 10, of which 4 were waited for; matrix products, arithmetic and copies ran while one was open for 0% of the time, Pallas kernels for 23%

profile of v1, /device:TPU:0, one launch (start us, length us, event | category | flops | bytes accessed | tf_op | source)
XLA Modules:
  0.0 46.8 jit_solution(9466528334445177901)
XLA Ops:
  0.6 0.0 copy-start.2
  0.6 1.0 %copy-done.2 = f32[8,8,16,128]{3,2,1,0:T(8,128)S(1)} copy-done((f32[8,8,16,128]{3,2,1,0:T(8,128)S(1)}, f32[8,8,16,128]{3,2,1,0:T(8,128)}, u32[]{:S(2)}) %copy-start.2) | copy-done | bytes 524312
  1.7 0.5 %collective-permute-start = (bf16[4,8,16,128]{3,2,1,0:T(8,128)(2,1)S(1)}, bf16[4,8,16,128]{3,2,1,0:T(8,128)(2,1)S(1)}, u32[]{:S(2)}, u32[]{:S(2)}) collective-permute-start(bf16[4,8,16,128]{3,2,1,0:T(8,128)(2,1)S(1)} %get-tuple-element.20), channel_id=1, source_target_pairs={{0,1},{1,2},{2,3},{3,4},{4,5},{5,6},{6,7},{7,8},{8,9},{9,10},{10,1... | collective-permute-start | bytes 393224 | tf_op jit(solution)/shard_map/ppermute | solution.py:187
  2.2 5.1 %collective-permute-start.1 = (bf16[4,8,16,128]{3,2,1,0:T(8,128)(2,1)S(1)}, bf16[4,8,16,128]{3,2,1,0:T(8,128)(2,1)S(1)}, u32[]{:S(2)}, u32[]{:S(2)}) collective-permute-start(bf16[4,8,16,128]{3,2,1,0:T(8,128)(2,1)S(1)} %get-tuple-element.21), channel_id=1, source_target_pairs={{0,15},{1,0},{2,1},{3,2},{4,3},{5,4},{6,5},{7,6},{8,7},{9,8},{10,9... | collective-permute-start | bytes 393224 | tf_op jit(solution)/shard_map/ppermute | solution.py:187
  7.3 0.0 collective-permute-start.2
  7.3 4.4 %collective-permute-start.3 = (bf16[5,8,16,128]{3,2,1,0:T(8,128)(2,1)S(1)}, bf16[5,8,16,128]{3,2,1,0:T(8,128)(2,1)S(1)}, u32[]{:S(2)}, u32[]{:S(2)}) collective-permute-start(bf16[5,8,16,128]{3,2,1,0:T(8,128)(2,1)S(1)} %get-tuple-element.23), channel_id=1, source_target_pairs={{0,15},{1,0},{2,1},{3,2},{4,3},{5,4},{6,5},{7,6},{8,7},{9,8},{10,9... | collective-permute-start | bytes 491528 | tf_op jit(solution)/shard_map/ppermute | solution.py:187
  12.4 0.0 collective-permute-done.left_near
  12.4 0.0 collective-permute-done.1.right_near
  12.4 0.0 copy-start
  12.4 2.8 %copy-done = bf16[8,24,128,128]{3,2,1,0:T(8,128)(2,1)S(1)} copy-done((bf16[8,24,128,128]{3,2,1,0:T(8,128)(2,1)S(1)}, bf16[8,24,128,128]{3,2,1,0:T(8,128)(2,1)}, u32[]{:S(2)}) %copy-start) | copy-done | bytes 6291480
  15.2 0.7 %copy-done.6 = s32[8,24]{1,0:T(8,128)S(1)} copy-done((s32[8,24]{1,0:T(8,128)S(1)}, s32[8,24]{1,0:T(8,128)}, u32[]{:S(2)}) %copy-start.6) | copy-done | bytes 792
  15.9 0.7 %copy-done.9 = f32[8,128]{1,0:T(8,128)S(1)} copy-done((f32[8,128]{1,0:T(8,128)S(1)}, f32[8,128]{1,0:T(8,128)}, u32[]{:S(2)}) %copy-start.9) | copy-done | bytes 4120
  16.6 0.0 copy-start.8
  16.6 0.0 copy-start.5
  16.6 5.3 %shard_map.114 = (bf16[8,16,128]{2,1,0:T(8,128)(2,1)S(1)}, f32[16,128]{1,0:T(8,128)S(1)}) custom-call(s32[8,24]{1,0:T(8,128)S(1)} %copy-done.6, s32[1]{0:T(128)S(6)} %copy.12.count, f32[8,128]{1,0:T(8,128)S(1)} %copy-done.9, bf16[32,16,128]{2,1,0:T(8,128)(2,1)S(1)} %bitcast.7, bf16[32,16,128]{2,1,0:T(8,128)(2,1)S(1)} %bitcast.12, ...), custom_call_target="tpu_custom_call" | custom-call | flops 100663296 | bytes 6291456 | tf_op jit(solution)/shard_map/pallas_call | solution.py:238
  22.0 3.1 %shard_map.116 = (f32[64,16,128]{2,1,0:T(8,128)S(1)}, bf16[32,16,128]{2,1,0:T(8,128)(2,1)S(1)}, bf16[32,16,128]{2,1,0:T(8,128)(2,1)S(1)}) custom-call(s32[8,24]{1,0:T(8,128)S(1)} %copy-done.7, bf16[8,16,128]{2,1,0:T(8,128)(2,1)S(1)} %get-tuple-element.27.weighted, bf16[8,24,128,128]{3,2,1,0:T(8,128)(2,1)S(1)} %copy-done.1), custom_call_target="tpu_custom_call" | custom-call | flops 100663296 | bytes 6291456 | tf_op jit(solution)/shard_map/pallas_call | solution.py:263
  25.1 0.1 collective-permute-start.4
  25.1 4.4 %collective-permute-start.5 = (bf16[32,16,128]{2,1,0:T(8,128)(2,1)S(1)}, bf16[32,16,128]{2,1,0:T(8,128)(2,1)S(1)}, u32[]{:S(2)}, u32[]{:S(2)}) collective-permute-start(bf16[32,16,128]{2,1,0:T(8,128)(2,1)S(1)} %get-tuple-element.30), channel_id=1, source_target_pairs={{0,15},{1,0},{2,1},{3,2},{4,3},{5,4},{6,5},{7,6},{8,7},{9,8},{10,9... | collective-permute-start | bytes 393224 | tf_op jit(solution)/shard_map/ppermute | solution.py:187
  29.6 1.1 %shard_map.112 = (f32[8,8,16,128]{3,2,1,0:T(8,128)S(1)}, f32[16,128]{1,0:T(8,128)S(1)}) custom-call(f32[8,8,16,128]{3,2,1,0:T(8,128)S(1)} %copy-done.3, f32[8,8,16,128]{3,2,1,0:T(8,128)S(1)} %copy-done.4, s32[128]{0:T(128)S(1)} %copy-done.10), custom_call_target="tpu_custom_call" | custom-call | flops 2621440 | bytes 1572864 | tf_op jit(solution)/shard_map/pallas_call | solution.py:229
  30.6 0.0 collective-permute-done.2.left_far
  30.7 0.0 collective-permute-done.3.right_far
  30.7 1.2 %shard_map.115 = (f32[8,8,16,128]{3,2,1,0:T(8,128)S(1)}, f32[16,128]{1,0:T(8,128)S(1)}) custom-call(f32[8,8,16,128]{3,2,1,0:T(8,128)S(1)} %copy-done.3, f32[8,8,16,128]{3,2,1,0:T(8,128)S(1)} %get-tuple-element.19.inner, bf16[4,8,16,128]{3,2,1,0:T(8,128)(2,1)S(1)} %collective-permute-done.left_near, ...), custom_call_target="tpu_custom_call" | custom-call | flops 2621440 | bytes 2097152 | tf_op jit(solution)/shard_map/pallas_call | solution.py:250
  31.8 0.0 collective-permute-start.6
  31.8 1.2 %collective-permute-done.6 = f32[16,128]{1,0:T(8,128)S(1)} collective-permute-done((f32[16,128]{1,0:T(8,128)S(1)}, f32[16,128]{1,0:T(8,128)S(1)}, u32[]{:S(2)}, u32[]{:S(2)}) %collective-permute-start.6) | collective-permute-done | bytes 8224 | tf_op jit(solution)/shard_map/ppermute | solution.py:196
  33.0 0.0 collective-permute-start.7
  33.0 3.6 %collective-permute-done.7 = f32[16,128]{1,0:T(8,128)S(1)} collective-permute-done((f32[16,128]{1,0:T(8,128)S(1)}, f32[16,128]{1,0:T(8,128)S(1)}, u32[]{:S(2)}, u32[]{:S(2)}) %collective-permute-start.7) | collective-permute-done | bytes 8224 | tf_op jit(solution)/shard_map/ppermute | solution.py:196
  36.7 0.0 collective-permute-start.8
  36.7 3.6 %collective-permute-done.8 = f32[16,128]{1,0:T(8,128)S(1)} collective-permute-done((f32[16,128]{1,0:T(8,128)S(1)}, f32[16,128]{1,0:T(8,128)S(1)}, u32[]{:S(2)}, u32[]{:S(2)}) %collective-permute-start.8) | collective-permute-done | bytes 8224 | tf_op jit(solution)/shard_map/ppermute | solution.py:196
  40.3 0.0 collective-permute-start.9
  40.3 4.5 %collective-permute-done.9 = f32[16,128]{1,0:T(8,128)S(1)} collective-permute-done((f32[16,128]{1,0:T(8,128)S(1)}, f32[16,128]{1,0:T(8,128)S(1)}, u32[]{:S(2)}, u32[]{:S(2)}) %collective-permute-start.9) | collective-permute-done | bytes 8224 | tf_op jit(solution)/shard_map/ppermute | solution.py:196
  44.9 1.3 %shard_map.117 = (f32[8,8,16,128]{3,2,1,0:T(8,128)}, f32[8,8,16,128]{3,2,1,0:T(8,128)}, f32[16,1]{1,0:T(8,128)S(1)}) custom-call(f32[8,8,16,128]{3,2,1,0:T(8,128)S(1)} %copy-done.5, f32[8,8,16,128]{3,2,1,0:T(8,128)S(1)} %copy-done.4, f32[8,8,16,128]{3,2,1,0:T(8,128)S(1)} %copy-done.3, f32[8,8,16,128]{3,2,1,0:T(8,128)S(1)} %get-tuple-element.26.base, ...), custom_call_target="tpu_custom_call" | custom-call | flops 1048576 | bytes 3670016 | tf_op jit(solution)/shard_map/pallas_call | solution.py:278
  46.1 0.6 %reduce = f32[16]{0:T(128)} reduce(f32[16,1]{1,0:T(8,128)S(1)} %get-tuple-element.34, f32[]{:T(128)} %constant.7), dimensions={1}, to_apply=%get-tuple-element.34.reduce_sub_computation | reduce | bytes 132 | tf_op jit(solution)/shard_map/pallas_call | solution.py:278
  (21 shorter events, 0.1 us)
Async XLA Ops:
  0.6 1.0 %copy-start.2 = (f32[8,8,16,128]{3,2,1,0:T(8,128)S(1)}, f32[8,8,16,128]{3,2,1,0:T(8,128)}, u32[]{:S(2)}) copy-start(f32[8,8,16,128]{3,2,1,0:T(8,128)} %direction.7) | copy-start | bytes 1572868
  1.7 20.3 %copy-start.7 = (s32[8,24]{1,0:T(8,128)S(1)}, s32[8,24]{1,0:T(8,128)}, u32[]{:S(2)}) copy-start(s32[8,24]{1,0:T(8,128)} %crossing.3) | copy-start | bytes 2308
  1.7 10.7 %collective-permute-start = (bf16[4,8,16,128]{3,2,1,0:T(8,128)(2,1)S(1)}, bf16[4,8,16,128]{3,2,1,0:T(8,128)(2,1)S(1)}, u32[]{:S(2)}, u32[]{:S(2)}) collective-permute-start(bf16[4,8,16,128]{3,2,1,0:T(8,128)(2,1)S(1)} %get-tuple-element.20), channel_id=1, source_target_pairs={{0,1},{1,2},{2,3},{3,4},{4,5},{5,6},{6,7},{7,8},{8,9},{9,10},{10,1... | collective-permute-start | bytes 393224 | tf_op jit(solution)/shard_map/ppermute | solution.py:187
  2.2 10.2 %collective-permute-start.1 = (bf16[4,8,16,128]{3,2,1,0:T(8,128)(2,1)S(1)}, bf16[4,8,16,128]{3,2,1,0:T(8,128)(2,1)S(1)}, u32[]{:S(2)}, u32[]{:S(2)}) collective-permute-start(bf16[4,8,16,128]{3,2,1,0:T(8,128)(2,1)S(1)} %get-tuple-element.21), channel_id=1, source_target_pairs={{0,15},{1,0},{2,1},{3,2},{4,3},{5,4},{6,5},{7,6},{8,7},{9,8},{10,9... | collective-permute-start | bytes 393224 | tf_op jit(solution)/shard_map/ppermute | solution.py:187
  7.3 23.4 %collective-permute-start.2 = (bf16[5,8,16,128]{3,2,1,0:T(8,128)(2,1)S(1)}, bf16[5,8,16,128]{3,2,1,0:T(8,128)(2,1)S(1)}, u32[]{:S(2)}, u32[]{:S(2)}) collective-permute-start(bf16[5,8,16,128]{3,2,1,0:T(8,128)(2,1)S(1)} %get-tuple-element.22), channel_id=1, source_target_pairs={{0,1},{1,2},{2,3},{3,4},{4,5},{5,6},{6,7},{7,8},{8,9},{9,10},{10,1... | collective-permute-start | bytes 491528 | tf_op jit(solution)/shard_map/ppermute | solution.py:187
  7.3 23.4 %collective-permute-start.3 = (bf16[5,8,16,128]{3,2,1,0:T(8,128)(2,1)S(1)}, bf16[5,8,16,128]{3,2,1,0:T(8,128)(2,1)S(1)}, u32[]{:S(2)}, u32[]{:S(2)}) collective-permute-start(bf16[5,8,16,128]{3,2,1,0:T(8,128)(2,1)S(1)} %get-tuple-element.23), channel_id=1, source_target_pairs={{0,15},{1,0},{2,1},{3,2},{4,3},{5,4},{6,5},{7,6},{8,7},{9,8},{10,9... | collective-permute-start | bytes 491528 | tf_op jit(solution)/shard_map/ppermute | solution.py:187
  12.4 2.8 %copy-start = (bf16[8,24,128,128]{3,2,1,0:T(8,128)(2,1)S(1)}, bf16[8,24,128,128]{3,2,1,0:T(8,128)(2,1)}, u32[]{:S(2)}) copy-start(bf16[8,24,128,128]{3,2,1,0:T(8,128)(2,1)} %jac_hbm.3) | copy-start | bytes 18874372
  15.2 0.7 %copy-start.6 = (s32[8,24]{1,0:T(8,128)S(1)}, s32[8,24]{1,0:T(8,128)}, u32[]{:S(2)}) copy-start(s32[8,24]{1,0:T(8,128)} %crossing.3) | copy-start | bytes 2308
  15.9 0.7 %copy-start.9 = (f32[8,128]{1,0:T(8,128)S(1)}, f32[8,128]{1,0:T(8,128)}, u32[]{:S(2)}) copy-start(f32[8,128]{1,0:T(8,128)} %sight.1) | copy-start | bytes 12292
  16.6 5.4 %copy-start.1 = (bf16[8,24,128,128]{3,2,1,0:T(8,128)(2,1)S(1)}, bf16[8,24,128,128]{3,2,1,0:T(8,128)(2,1)}, u32[]{:S(2)}) copy-start(bf16[8,24,128,128]{3,2,1,0:T(8,128)(2,1)} %jac_hbm.3) | copy-start | bytes 18874372
  16.6 13.0 %copy-start.3 = (f32[8,8,16,128]{3,2,1,0:T(8,128)S(1)}, f32[8,8,16,128]{3,2,1,0:T(8,128)}, u32[]{:S(2)}) copy-start(f32[8,8,16,128]{3,2,1,0:T(8,128)} %direction.7) | copy-start | bytes 1572868
  16.6 13.0 %copy-start.4 = (f32[8,8,16,128]{3,2,1,0:T(8,128)S(1)}, f32[8,8,16,128]{3,2,1,0:T(8,128)}, u32[]{:S(2)}) copy-start(f32[8,8,16,128]{3,2,1,0:T(8,128)} %residual.3) | copy-start | bytes 1572868
  16.6 13.0 %copy-start.10 = (s32[128]{0:T(128)S(1)}, s32[128]{0:T(128)}, u32[]{:S(2)}) copy-start(s32[128]{0:T(128)} %classes.3) | copy-start | bytes 1540
  16.6 14.1 %copy-start.8 = (f32[8,128]{1,0:T(8,128)S(1)}, f32[8,128]{1,0:T(8,128)}, u32[]{:S(2)}) copy-start(f32[8,128]{1,0:T(8,128)} %smooth.1) | copy-start | bytes 12292
  16.6 28.3 %copy-start.5 = (f32[8,8,16,128]{3,2,1,0:T(8,128)S(1)}, f32[8,8,16,128]{3,2,1,0:T(8,128)}, u32[]{:S(2)}) copy-start(f32[8,8,16,128]{3,2,1,0:T(8,128)} %solution.1) | copy-start | bytes 1572868
  25.1 19.8 %collective-permute-start.4 = (bf16[32,16,128]{2,1,0:T(8,128)(2,1)S(1)}, bf16[32,16,128]{2,1,0:T(8,128)(2,1)S(1)}, u32[]{:S(2)}, u32[]{:S(2)}) collective-permute-start(bf16[32,16,128]{2,1,0:T(8,128)(2,1)S(1)} %get-tuple-element.29), channel_id=1, source_target_pairs={{0,1},{1,2},{2,3},{3,4},{4,5},{5,6},{6,7},{7,8},{8,9},{9,10},{10,1... | collective-permute-start | bytes 393224 | tf_op jit(solution)/shard_map/ppermute | solution.py:187
  25.1 19.7 %collective-permute-start.5 = (bf16[32,16,128]{2,1,0:T(8,128)(2,1)S(1)}, bf16[32,16,128]{2,1,0:T(8,128)(2,1)S(1)}, u32[]{:S(2)}, u32[]{:S(2)}) collective-permute-start(bf16[32,16,128]{2,1,0:T(8,128)(2,1)S(1)} %get-tuple-element.30), channel_id=1, source_target_pairs={{0,15},{1,0},{2,1},{3,2},{4,3},{5,4},{6,5},{7,6},{8,7},{9,8},{10,9... | collective-permute-start | bytes 393224 | tf_op jit(solution)/shard_map/ppermute | solution.py:187
  31.8 1.2 %collective-permute-start.6 = (f32[16,128]{1,0:T(8,128)S(1)}, f32[16,128]{1,0:T(8,128)S(1)}, u32[]{:S(2)}, u32[]{:S(2)}) collective-permute-start(f32[16,128]{1,0:T(8,128)S(1)} %get-tuple-element.31), channel_id=1, source_target_pairs={{0,1},{1,0},{2,3},{3,2},{4,5},{5,4},{6,7},{7,6},{8,9},{9,8},{10,11... | collective-permute-start | bytes 24584 | tf_op jit(solution)/shard_map/ppermute | solution.py:196
  33.0 3.7 %collective-permute-start.7 = (f32[16,128]{1,0:T(8,128)S(1)}, f32[16,128]{1,0:T(8,128)S(1)}, u32[]{:S(2)}, u32[]{:S(2)}) collective-permute-start(f32[16,128]{1,0:T(8,128)S(1)} %add.12), channel_id=1, source_target_pairs={{0,2},{1,3},{2,0},{3,1},{4,6},{5,7},{6,4},{7,5},{8,10},{9,11},{10,... | collective-permute-start | bytes 24584 | tf_op jit(solution)/shard_map/ppermute | solution.py:196
  36.7 3.7 %collective-permute-start.8 = (f32[16,128]{1,0:T(8,128)S(1)}, f32[16,128]{1,0:T(8,128)S(1)}, u32[]{:S(2)}, u32[]{:S(2)}) collective-permute-start(f32[16,128]{1,0:T(8,128)S(1)} %add.13), channel_id=1, source_target_pairs={{0,4},{1,5},{2,6},{3,7},{4,0},{5,1},{6,2},{7,3},{8,12},{9,13},{10,... | collective-permute-start | bytes 24584 | tf_op jit(solution)/shard_map/ppermute | solution.py:196
  40.3 4.5 %collective-permute-start.9 = (f32[16,128]{1,0:T(8,128)S(1)}, f32[16,128]{1,0:T(8,128)S(1)}, u32[]{:S(2)}, u32[]{:S(2)}) collective-permute-start(f32[16,128]{1,0:T(8,128)S(1)} %add.14), channel_id=1, source_target_pairs={{0,8},{1,9},{2,10},{3,11},{4,12},{5,13},{6,14},{7,15},{8,0},{9,1},... | collective-permute-start | bytes 24584 | tf_op jit(solution)/shard_map/ppermute | solution.py:196

commit v2 on v1

v2 whole, which is shorter than its diff:
```python
import functools

import jax
import jax.numpy as jnp
from jax import lax
from jax.experimental import pallas as pl
from jax.experimental.pallas import tpu as pltpu
from jax.sharding import PartitionSpec as P

LEVELS = 120
CLASSES = 4
REACH = 8
EPSILON = 1e-06
VMEM_LIMIT = 24 * 1024 * 1024

SMEM = functools.partial(pl.BlockSpec, memory_space=pltpu.SMEM)
VMEM = functools.partial(pl.BlockSpec, memory_space=pltpu.VMEM)
HBM = functools.partial(pl.BlockSpec, memory_space=pltpu.HBM)


def in_hbm(array):
    return pltpu.with_memory_space_constraint(array, pltpu.HBM)


def live_lanes(shape):
    return lax.broadcasted_iota(jnp.int32, shape, len(shape) - 1) < LEVELS


def masked(values):
    return jnp.where(live_lanes(values.shape), values, 0.0)


def call(kernel, out_shape, in_specs, flops, moved, scratch=()):
    return pl.pallas_call(
        kernel,
        out_shape=out_shape,
        in_specs=in_specs,
        out_specs=jax.tree.map(lambda _: VMEM(), out_shape),
        scratch_shapes=list(scratch),
        compiler_params=pltpu.CompilerParams(vmem_limit_bytes=VMEM_LIMIT),
        cost_estimate=pl.CostEstimate(flops=flops, bytes_accessed=moved, transcendentals=0),
    )


def rounding_kernel(direction, low, high):
    rim = low.shape[0]
    for c in range(rim):
        low[c] = masked(direction[c]).astype(jnp.bfloat16)
        high[c] = masked(direction[rim + c]).astype(jnp.bfloat16)


def coupling(classes, cols, columns):
    total = classes.shape[0]
    first = lax.axis_index("orbit") * cols
    table = {}
    for c in columns:
        length = (classes[lax.rem(first + c + total, total)] + 1) * REACH // CLASSES
        for k in range(1, REACH + 1):
            table[c, k] = jnp.where(k <= length, jnp.float32(1.0 / (k * k)), jnp.float32(0.0))
    return table


def pull(table, to, values):
    result = None
    for c, value in values.items():
        if c != to and abs(c - to) <= REACH:
            term = table[min(c, to), abs(c - to)] * value
            result = term if result is None else result + term
    return -result


def inner_kernel(
    direction, residual_hbm, classes_hbm, smooth_hbm, jac_hbm, begun, norm, curved, jac,
    residual, classes, smooth, sems,
):
    pairs = (classes_hbm, classes), (smooth_hbm, smooth), (residual_hbm, residual), (jac_hbm, jac)
    copies = [pltpu.make_async_copy(*pair, sems.at[i]) for i, pair in enumerate(pairs)]
    for copy in copies:
        copy.start()
    copies[0].wait()
    copies[1].wait()
    cols = direction.shape[0]
    rim = cols // 2
    table = coupling(classes, cols, range(-REACH, cols))
    weight = smooth[...][:, None, :]
    total = jnp.zeros(norm.shape, jnp.float32)
    values = {c: masked(direction[c]) for c in range(cols)}
    rests = {c: v - v.astype(jnp.bfloat16).astype(jnp.float32) for c, v in values.items()}
    for c in range(cols):
        centre = jnp.float32(1.0)
        for k in range(1, REACH + 1):
            centre = centre + (table[c, k] + table[c - k, k])
        result = weight * (centre * values[c] + pull(table, c, values))
        begun[rim + c] = result
        total = total + jnp.sum(values[c] * result, axis=0)
    for q in range(rim):
        to_left = {c: values[c] if c >= rim else rests[c] for c in range(cols)}
        to_right = {c: values[c] if c < rim else rests[c] for c in range(cols)}
        begun[q] = weight * pull(table, q - rim, to_left)
        begun[rim + cols + q] = weight * pull(table, q + cols, to_right)
    curved[...] = total
    copies[2].wait()
    squares = jnp.zeros(norm.shape, jnp.float32)
    for c in range(cols):
        mres = masked(residual[c])
        squares = squares + jnp.sum(mres * mres, axis=0)
    norm[...] = squares
    copies[3].wait()


def forward_kernel(
    crossing, count, classes, sight, direction, smooth, left, low, high, right, begun, norm, curved,
    jac, weighted, own, sums, window,
):
    slots, crossings = crossing.shape
    cols, species = direction.shape[:2]
    rim = left.shape[0]
    rim_tiles = rim * species
    for place, part in enumerate((left, low, high, right)):
        window[pl.ds(place * rim_tiles, rim_tiles)] = part[...].reshape(rim_tiles, *part.shape[2:])
    total = curved[...]
    for i in range(slots):
        picked = jnp.concatenate([window[crossing[i, j]] for j in range(crossings)], axis=1)
        tiles = jnp.concatenate([jac[i, j] for j in range(crossings)], axis=1)
        integrals = lax.dot_general(
            tiles, picked, (((1,), (1,)), ((), ())), preferred_element_type=jnp.float32
        )
        integrals = jnp.transpose(integrals)
        row = sight[pl.ds(i, 1), :] * jnp.where(i < count[0], 1.0, 0.0)
        product = (row * integrals).astype(jnp.bfloat16)
        weighted[i] = product
        total = total + product.astype(jnp.float32) * integrals
    table = coupling(classes, cols, range(-rim, cols))
    weight = smooth[...][:, None, :]
    before = {c - rim: left[c].astype(jnp.float32) for c in range(rim)}
    after = {c + cols: right[c].astype(jnp.float32) for c in range(rim)}
    for c in range(cols):
        from_before = weight * pull(table, c, before)
        from_after = weight * pull(table, c, after)
        own[c] = begun[rim + c] + (from_before + from_after)
        edges = from_after if c < rim else from_after + from_before
        total = total + 2.0 * jnp.sum(masked(direction[c]) * edges, axis=0)
    lane = lax.broadcasted_iota(jnp.int32, sums.shape, 1)
    sums[...] = jnp.where(
        lane == 0,
        jnp.sum(norm[...], axis=1, keepdims=True),
        jnp.where(lane == 1, jnp.sum(total, axis=1, keepdims=True), 0.0),
    )


def backward_kernel(crossing, weighted, jac, begun, own, image, left, right, sums):
    slots, crossings = crossing.shape
    cols, species, probes, tile = own.shape
    rim = left.shape[0]
    rim_tiles, own_tiles = rim * species, cols * species
    spans = (pl.ds(0, rim_tiles), pl.ds(rim_tiles, own_tiles), pl.ds(rim_tiles + own_tiles, rim_tiles))
    sums[spans[0]] = begun[pl.ds(0, rim)].reshape(rim_tiles, probes, tile)
    sums[spans[1]] = own[...].reshape(own_tiles, probes, tile)
    sums[spans[2]] = begun[pl.ds(rim + cols, rim)].reshape(rim_tiles, probes, tile)
    for i in range(slots):
        tiles = jnp.concatenate([jac[i, j] for j in range(crossings)], axis=1)
        terms = jnp.dot(weighted[i], tiles, preferred_element_type=jnp.float32)
        for j in range(crossings):
            sums[crossing[i, j]] += terms[:, j * tile : (j + 1) * tile]
    left[...] = sums[spans[0]].astype(left.dtype).reshape(left.shape)
    right[...] = sums[spans[2]].astype(right.dtype).reshape(right.shape)
    image[...] = sums[spans[1]].reshape(image.shape)


def final_kernel(
    solution, residual, direction, image, from_left, from_right, sums,
    solution_next, residual_next, step_length,
):
    step = sums[:, 0:1] / (sums[:, 1:2] + EPSILON)
    cols = direction.shape[0]
    rim = from_left.shape[0]
    wide = jnp.broadcast_to(step, direction.shape[2:])
    step_length[...] = jnp.transpose(wide)[0:1]
    wide = wide[None]
    for c in range(cols):
        arrived = from_left[c] if c < rim else from_right[c - rim]
        whole = masked(image[c] + arrived.astype(jnp.float32))
        solution_next[c] = masked(solution[c] + wide * direction[c])
        residual_next[c] = masked(residual[c]) - wide * whole


def shifted(array, by):
    count = lax.axis_size("orbit")
    return lax.ppermute(array, "orbit", [(i, (i + by) % count) for i in range(count)])


def summed(array):
    count = lax.axis_size("orbit")
    if count & (count - 1):
        return lax.psum(array, "orbit")
    bits = [1 << b for b in range(count.bit_length() - 1)]
    for bit in bits[1:] + bits[:1]:
        array = array + lax.ppermute(array, "orbit", [(i, i ^ bit) for i in range(count)])
    return array


def local(
    solution, residual, direction, jacobian, crossing, tile_count, sightline_weight,
    length_class, smooth_weight,
):
    cols, species, probes, width = direction.shape
    assert REACH <= cols
    rim = cols // 2
    slots = crossing.shape[0]
    f32, bf16 = jnp.float32, jnp.bfloat16
    shape = jax.ShapeDtypeStruct
    column = (species, probes, width)
    elements = direction.size
    dot_flops = 2 * jacobian.size * probes
    near = shape((rim,) + column, bf16)
    whole = shape(direction.shape, f32)
    small = shape((probes, width), f32)

    low, high = call(rounding_kernel, (near, near), [VMEM()], 2 * elements, 6 * elements)(direction)
    left = shifted(high, 1)
    right = shifted(low, -1)

    begun, norm, curved, jac = call(
        inner_kernel,
        (shape((2 * cols,) + column, f32), small, small, shape(jacobian.shape, bf16)),
        [VMEM()] + [HBM()] * 4,
        60 * elements,
        4 * jacobian.size,
        [
            pltpu.VMEM(direction.shape, f32),
            pltpu.SMEM(length_class.shape, jnp.int32),
            pltpu.VMEM(smooth_weight.shape, f32),
            pltpu.SemaphoreType.DMA((4,)),
        ],
    )(direction, *map(in_hbm, (residual, length_class, smooth_weight, jacobian)))

    weighted, own, sums = call(
        forward_kernel,
        (shape((slots, probes, width), bf16), whole, small),
        [SMEM()] * 3 + [VMEM()] * 11,
        dot_flops,
        2 * jacobian.size,
        [pltpu.VMEM((2 * cols * species, probes, width), bf16)],
    )(
        crossing, tile_count, length_class, sightline_weight, direction, smooth_weight,
        left, low, high, right, begun, norm, curved, jac,
    )
    sums = summed(sums)

    image, to_left, to_right = call(
        backward_kernel,
        (whole, near, near),
        [SMEM()] + [VMEM()] * 4,
        dot_flops,
        2 * jacobian.size,
        [pltpu.VMEM((2 * cols * species, probes, width), f32)],
    )(crossing, weighted, jac, begun, own)
    from_left = shifted(to_right, 1)
    from_right = shifted(to_left, -1)

    solution_next, residual_next, step_length = call(
        final_kernel,
        (whole, whole, shape((1, probes), f32)),
        [VMEM()] * 7,
        8 * elements,
        28 * elements,
    )(solution, residual, direction, image, from_left, from_right, sums)
    return solution_next, residual_next, step_length.reshape(probes)


def solution(mesh):
    wide = P(("grp", "orbit"), None, None, None)
    placed = (
        wide, wide, wide, wide,
        P(("grp", "orbit"), None),
        P(("grp", "orbit")),
        P(("grp", "orbit"), None),
        P("grp"),
        P(),
    )
    return jax.shard_map(
        local, mesh=mesh, in_specs=placed, out_specs=(wide, wide, P("grp")), check_vma=False
    )
```

time: 47 us -> 34.7 us (0.74)
  starting transfers between devices: 14.5 us -> 10.1 us
  local copies, waits for them, and re-layouts: 5.22 us -> 1.07 us
  Pallas kernels: 12 us -> 8.89 us
  other arithmetic: 0.64 us -> 0.01 us
    ppermute x6 -> x4, starting transfers between devices: 14.5 us -> 10.1 us  [shifted(): lax.ppermute(array, 'orbit', [(i, (i + by) % count) for i in range(count)])]
    unnamed x22 -> x16, local copies, waits for them, and re-layouts: 5.22 us -> 1.07 us
    pallas_call x6 -> x5, Pallas kernels: 12 us -> 8.89 us  [the longest x1 3.02 us: local(): call(inner_kernel, (shape((2 * cols,) + column, f32), small, small, shape...]
    pallas_call x1 -> x0, other arithmetic: 0.63 us -> none  [local(): call(functools.partial(final_kernel, rim), (shape(direction.shape, f32),...]
  transfers between devices with their start and end apart: 10 -> 8, of which waited for: 4 -> 4; matrix products, arithmetic and copies ran while one was open for 0% -> 0% of each run, Pallas kernels for 23% -> 9%
where the time goes in v2:
time: 34.7 us; the launch traced here: 34.5 us
  waiting for transfers between devices  13 us (37%)
  starting transfers between devices  10.1 us (29%)
  Pallas kernels  8.89 us (26%)
  between operations  1.43 us (4%)
  local copies, waits for them, and re-layouts  1.07 us (3%)
    ppermute x4, waiting for transfers between devices, summed(): lax.ppermute(array, 'orbit', [(i, i ^ bit) for i in range(count)])  13 us
    ppermute x4, starting transfers between devices, shifted(): lax.ppermute(array, 'orbit', [(i, (i + by) % count) for i in range(count)])  10.1 us
    pallas_call x1, Pallas kernels, local(): call(inner_kernel, (shape((2 * cols,) + column, f32), small, small, shape...  3.02 us
    pallas_call x1, Pallas kernels, local(): call(forward_kernel, (shape((slots, probes, width), bf16), whole, small),...  2.86 us
    pallas_call x1, Pallas kernels, local(): call(backward_kernel, (whole, near, near), [SMEM()] + [VMEM()] * 4, dot_f...  1.79 us
    pallas_call x1, Pallas kernels, local(): call(final_kernel, (whole, whole, shape((1, probes), f32)), [VMEM()] * 7,...  1.18 us
    unnamed x16, local copies, waits for them, and re-layouts  1.07 us
  transfers between devices with their start and end apart: 8, of which 4 were waited for; matrix products, arithmetic and copies ran while one was open for 0% of the time, Pallas kernels for 9%

profile of v2, /device:TPU:0, one launch (start us, length us, event | category | flops | bytes accessed | tf_op | source)
XLA Modules:
  0.0 34.5 jit_solution(11138540856727369252)
XLA Ops:
  0.6 0.0 copy-start
  0.6 1.0 %copy-done = f32[8,8,16,128]{3,2,1,0:T(8,128)S(1)} copy-done((f32[8,8,16,128]{3,2,1,0:T(8,128)S(1)}, f32[8,8,16,128]{3,2,1,0:T(8,128)}, u32[]{:S(2)}) %copy-start) | copy-done | bytes 524312
  1.7 0.5 %collective-permute-start = (bf16[4,8,16,128]{3,2,1,0:T(8,128)(2,1)S(1)}, bf16[4,8,16,128]{3,2,1,0:T(8,128)(2,1)S(1)}, u32[]{:S(2)}, u32[]{:S(2)}) collective-permute-start(bf16[4,8,16,128]{3,2,1,0:T(8,128)(2,1)S(1)} %get-tuple-element.18.high), channel_id=1, source_target_pairs={{0,1},{1,2},{2,3},{3,4},{4,5},{5,6},{6,7},{7,8},{8,9},{9,10},{10,1... | collective-permute-start | bytes 393224 | tf_op jit(solution)/shard_map/ppermute | solution.py:189
  2.2 5.1 %collective-permute-start.1 = (bf16[4,8,16,128]{3,2,1,0:T(8,128)(2,1)S(1)}, bf16[4,8,16,128]{3,2,1,0:T(8,128)(2,1)S(1)}, u32[]{:S(2)}, u32[]{:S(2)}) collective-permute-start(bf16[4,8,16,128]{3,2,1,0:T(8,128)(2,1)S(1)} %get-tuple-element.19.low), channel_id=1, source_target_pairs={{0,15},{1,0},{2,1},{3,2},{4,3},{5,4},{6,5},{7,6},{8,7},{9,8},{10,9... | collective-permute-start | bytes 393224 | tf_op jit(solution)/shard_map/ppermute | solution.py:189
  7.9 3.0 %shard_map.113 = (f32[16,8,16,128]{3,2,1,0:T(8,128)S(1)}, f32[16,128]{1,0:T(8,128)S(1)}, f32[16,128]{1,0:T(8,128)S(1)}, bf16[8,24,128,128]{3,2,1,0:T(8,128)(2,1)S(1)}) custom-call(f32[8,8,16,128]{3,2,1,0:T(8,128)S(1)} %copy-done, f32[8,8,16,128]{3,2,1,0:T(8,128)} %residual.1, s32[128]{0:T(128)} %classes.1, f32[8,128]{1,0:T(8,128)} %smooth.1, ...), custom_call_target="tpu_custom_call" | custom-call | flops 7864320 | bytes 12582912 | tf_op jit(solution)/shard_map/pallas_call | solution.py:223
  11.0 0.0 collective-permute-done.left
  11.0 0.0 collective-permute-done.1.right
  11.0 0.0 copy-done.4
  11.0 0.0 copy-done.5
  11.0 0.0 copy-done.6
  11.0 0.0 copy-done.7
  11.0 0.0 copy-start.1
  11.0 0.0 copy-start.2
  11.1 0.0 copy-start.3
  11.1 2.9 %shard_map.114 = (bf16[8,16,128]{2,1,0:T(8,128)(2,1)S(1)}, f32[8,8,16,128]{3,2,1,0:T(8,128)S(1)}, f32[16,128]{1,0:T(8,128)S(1)}) custom-call(s32[8,24]{1,0:T(8,128)S(1)} %copy-done.5, s32[1]{0:T(128)S(6)} %copy.12.count, s32[128]{0:T(128)S(1)} %copy-done.7, f32[8,128]{1,0:T(8,128)S(1)} %copy-done.6, f32[8,8,16,128]{3,2,1,0:T(8,128)S(1)} %copy-done, ...), custom_call_target="tpu_custom_call" | custom-call | flops 100663296 | bytes 6291456 | tf_op jit(solution)/shard_map/pallas_call | solution.py:237
  13.9 1.8 %shard_map.115 = (f32[8,8,16,128]{3,2,1,0:T(8,128)S(1)}, bf16[4,8,16,128]{3,2,1,0:T(8,128)(2,1)S(1)}, bf16[4,8,16,128]{3,2,1,0:T(8,128)(2,1)S(1)}) custom-call(s32[8,24]{1,0:T(8,128)S(1)} %copy-done.5, bf16[8,16,128]{2,1,0:T(8,128)(2,1)S(1)} %get-tuple-element.24.weighted, bf16[8,24,128,128]{3,2,1,0:T(8,128)(2,1)S(1)} %get-tuple-element.23.jac, ...), custom_call_target="tpu_custom_call" | custom-call | flops 100663296 | bytes 6291456 | tf_op jit(solution)/shard_map/pallas_call | solution.py:250
  15.7 0.1 collective-permute-start.2
  15.8 4.4 %collective-permute-start.3 = (bf16[4,8,16,128]{3,2,1,0:T(8,128)(2,1)S(1)}, bf16[4,8,16,128]{3,2,1,0:T(8,128)(2,1)S(1)}, u32[]{:S(2)}, u32[]{:S(2)}) collective-permute-start(bf16[4,8,16,128]{3,2,1,0:T(8,128)(2,1)S(1)} %get-tuple-element.28), channel_id=1, source_target_pairs={{0,15},{1,0},{2,1},{3,2},{4,3},{5,4},{6,5},{7,6},{8,7},{9,8},{10,9... | collective-permute-start | bytes 393224 | tf_op jit(solution)/shard_map/ppermute | solution.py:189
  20.2 0.0 collective-permute-start.4
  20.2 3.6 %collective-permute-done.4 = f32[16,128]{1,0:T(8,128)S(1)} collective-permute-done((f32[16,128]{1,0:T(8,128)S(1)}, f32[16,128]{1,0:T(8,128)S(1)}, u32[]{:S(2)}, u32[]{:S(2)}) %collective-permute-start.4) | collective-permute-done | bytes 8224 | tf_op jit(solution)/shard_map/ppermute | solution.py:198
  23.9 0.0 collective-permute-start.5
  23.9 3.6 %collective-permute-done.5 = f32[16,128]{1,0:T(8,128)S(1)} collective-permute-done((f32[16,128]{1,0:T(8,128)S(1)}, f32[16,128]{1,0:T(8,128)S(1)}, u32[]{:S(2)}, u32[]{:S(2)}) %collective-permute-start.5) | collective-permute-done | bytes 8224 | tf_op jit(solution)/shard_map/ppermute | solution.py:198
  27.5 0.0 collective-permute-start.6
  27.5 4.5 %collective-permute-done.6 = f32[16,128]{1,0:T(8,128)S(1)} collective-permute-done((f32[16,128]{1,0:T(8,128)S(1)}, f32[16,128]{1,0:T(8,128)S(1)}, u32[]{:S(2)}, u32[]{:S(2)}) %collective-permute-start.6) | collective-permute-done | bytes 8224 | tf_op jit(solution)/shard_map/ppermute | solution.py:198
  32.1 0.0 collective-permute-start.7
  32.1 1.2 %collective-permute-done.7 = f32[16,128]{1,0:T(8,128)S(1)} collective-permute-done((f32[16,128]{1,0:T(8,128)S(1)}, f32[16,128]{1,0:T(8,128)S(1)}, u32[]{:S(2)}, u32[]{:S(2)}) %collective-permute-start.7) | collective-permute-done | bytes 8224 | tf_op jit(solution)/shard_map/ppermute | solution.py:198
  33.3 0.0 collective-permute-done.2.from_left
  33.3 0.0 collective-permute-done.3.from_right
  33.3 0.0 copy-done.1
  33.3 0.0 copy-done.2
  33.3 0.0 copy-done.3
  33.3 1.2 %shard_map.116 = (f32[8,8,16,128]{3,2,1,0:T(8,128)}, f32[8,8,16,128]{3,2,1,0:T(8,128)}, f32[1,16]{1,0:T(1,128)}) custom-call(f32[8,8,16,128]{3,2,1,0:T(8,128)S(1)} %copy-done.3, f32[8,8,16,128]{3,2,1,0:T(8,128)S(1)} %copy-done.2, f32[8,8,16,128]{3,2,1,0:T(8,128)S(1)} %copy-done.1, f32[8,8,16,128]{3,2,1,0:T(8,128)S(1)} %get-tuple-element.26.image, ...), custom_call_target="tpu_custom_call" | custom-call | flops 1048576 | bytes 3670016 | tf_op jit(solution)/shard_map/pallas_call | solution.py:261
  (9 shorter events, 0.1 us)
Async XLA Ops:
  0.6 1.0 %copy-start = (f32[8,8,16,128]{3,2,1,0:T(8,128)S(1)}, f32[8,8,16,128]{3,2,1,0:T(8,128)}, u32[]{:S(2)}) copy-start(f32[8,8,16,128]{3,2,1,0:T(8,128)} %direction.7) | copy-start | bytes 1572868
  1.7 9.3 %copy-start.4 = (f32[8,128]{1,0:T(8,128)S(1)}, f32[8,128]{1,0:T(8,128)}, u32[]{:S(2)}) copy-start(f32[8,128]{1,0:T(8,128)} %smooth.1) | copy-start | bytes 12292
  1.7 9.3 %copy-start.5 = (s32[8,24]{1,0:T(8,128)S(1)}, s32[8,24]{1,0:T(8,128)}, u32[]{:S(2)}) copy-start(s32[8,24]{1,0:T(8,128)} %crossing.3) | copy-start | bytes 2308
  1.7 9.3 %copy-start.6 = (f32[8,128]{1,0:T(8,128)S(1)}, f32[8,128]{1,0:T(8,128)}, u32[]{:S(2)}) copy-start(f32[8,128]{1,0:T(8,128)} %sight.1) | copy-start | bytes 12292
  1.7 9.3 %copy-start.7 = (s32[128]{0:T(128)S(1)}, s32[128]{0:T(128)}, u32[]{:S(2)}) copy-start(s32[128]{0:T(128)} %classes.1) | copy-start | bytes 1540
  1.7 9.2 %collective-permute-start = (bf16[4,8,16,128]{3,2,1,0:T(8,128)(2,1)S(1)}, bf16[4,8,16,128]{3,2,1,0:T(8,128)(2,1)S(1)}, u32[]{:S(2)}, u32[]{:S(2)}) collective-permute-start(bf16[4,8,16,128]{3,2,1,0:T(8,128)(2,1)S(1)} %get-tuple-element.18.high), channel_id=1, source_target_pairs={{0,1},{1,2},{2,3},{3,4},{4,5},{5,6},{6,7},{7,8},{8,9},{9,10},{10,1... | collective-permute-start | bytes 393224 | tf_op jit(solution)/shard_map/ppermute | solution.py:189
  2.2 8.8 %collective-permute-start.1 = (bf16[4,8,16,128]{3,2,1,0:T(8,128)(2,1)S(1)}, bf16[4,8,16,128]{3,2,1,0:T(8,128)(2,1)S(1)}, u32[]{:S(2)}, u32[]{:S(2)}) collective-permute-start(bf16[4,8,16,128]{3,2,1,0:T(8,128)(2,1)S(1)} %get-tuple-element.19.low), channel_id=1, source_target_pairs={{0,15},{1,0},{2,1},{3,2},{4,3},{5,4},{6,5},{7,6},{8,7},{9,8},{10,9... | collective-permute-start | bytes 393224 | tf_op jit(solution)/shard_map/ppermute | solution.py:189
  11.0 22.2 %copy-start.1 = (f32[8,8,16,128]{3,2,1,0:T(8,128)S(1)}, f32[8,8,16,128]{3,2,1,0:T(8,128)}, u32[]{:S(2)}) copy-start(f32[8,8,16,128]{3,2,1,0:T(8,128)} %direction.7) | copy-start | bytes 1572868
  11.0 22.2 %copy-start.2 = (f32[8,8,16,128]{3,2,1,0:T(8,128)S(1)}, f32[8,8,16,128]{3,2,1,0:T(8,128)}, u32[]{:S(2)}) copy-start(f32[8,8,16,128]{3,2,1,0:T(8,128)} %residual.1) | copy-start | bytes 1572868
  11.1 22.2 %copy-start.3 = (f32[8,8,16,128]{3,2,1,0:T(8,128)S(1)}, f32[8,8,16,128]{3,2,1,0:T(8,128)}, u32[]{:S(2)}) copy-start(f32[8,8,16,128]{3,2,1,0:T(8,128)} %solution.1) | copy-start | bytes 1572868
  15.7 17.5 %collective-permute-start.2 = (bf16[4,8,16,128]{3,2,1,0:T(8,128)(2,1)S(1)}, bf16[4,8,16,128]{3,2,1,0:T(8,128)(2,1)S(1)}, u32[]{:S(2)}, u32[]{:S(2)}) collective-permute-start(bf16[4,8,16,128]{3,2,1,0:T(8,128)(2,1)S(1)} %get-tuple-element.27), channel_id=1, source_target_pairs={{0,1},{1,2},{2,3},{3,4},{4,5},{5,6},{6,7},{7,8},{8,9},{9,10},{10,1... | collective-permute-start | bytes 393224 | tf_op jit(solution)/shard_map/ppermute | solution.py:189
  15.8 17.5 %collective-permute-start.3 = (bf16[4,8,16,128]{3,2,1,0:T(8,128)(2,1)S(1)}, bf16[4,8,16,128]{3,2,1,0:T(8,128)(2,1)S(1)}, u32[]{:S(2)}, u32[]{:S(2)}) collective-permute-start(bf16[4,8,16,128]{3,2,1,0:T(8,128)(2,1)S(1)} %get-tuple-element.28), channel_id=1, source_target_pairs={{0,15},{1,0},{2,1},{3,2},{4,3},{5,4},{6,5},{7,6},{8,7},{9,8},{10,9... | collective-permute-start | bytes 393224 | tf_op jit(solution)/shard_map/ppermute | solution.py:189
  20.2 3.7 %collective-permute-start.4 = (f32[16,128]{1,0:T(8,128)S(1)}, f32[16,128]{1,0:T(8,128)S(1)}, u32[]{:S(2)}, u32[]{:S(2)}) collective-permute-start(f32[16,128]{1,0:T(8,128)S(1)} %get-tuple-element.29), channel_id=1, source_target_pairs={{0,2},{1,3},{2,0},{3,1},{4,6},{5,7},{6,4},{7,5},{8,10},{9,11},{10,... | collective-permute-start | bytes 24584 | tf_op jit(solution)/shard_map/ppermute | solution.py:198
  23.9 3.7 %collective-permute-start.5 = (f32[16,128]{1,0:T(8,128)S(1)}, f32[16,128]{1,0:T(8,128)S(1)}, u32[]{:S(2)}, u32[]{:S(2)}) collective-permute-start(f32[16,128]{1,0:T(8,128)S(1)} %add.12), channel_id=1, source_target_pairs={{0,4},{1,5},{2,6},{3,7},{4,0},{5,1},{6,2},{7,3},{8,12},{9,13},{10,... | collective-permute-start | bytes 24584 | tf_op jit(solution)/shard_map/ppermute | solution.py:198
  27.5 4.5 %collective-permute-start.6 = (f32[16,128]{1,0:T(8,128)S(1)}, f32[16,128]{1,0:T(8,128)S(1)}, u32[]{:S(2)}, u32[]{:S(2)}) collective-permute-start(f32[16,128]{1,0:T(8,128)S(1)} %add.13), channel_id=1, source_target_pairs={{0,8},{1,9},{2,10},{3,11},{4,12},{5,13},{6,14},{7,15},{8,0},{9,1},... | collective-permute-start | bytes 24584 | tf_op jit(solution)/shard_map/ppermute | solution.py:198
  32.1 1.2 %collective-permute-start.7 = (f32[16,128]{1,0:T(8,128)S(1)}, f32[16,128]{1,0:T(8,128)S(1)}, u32[]{:S(2)}, u32[]{:S(2)}) collective-permute-start(f32[16,128]{1,0:T(8,128)S(1)} %add.14), channel_id=1, source_target_pairs={{0,1},{1,0},{2,3},{3,2},{4,5},{5,4},{6,7},{7,6},{8,9},{9,8},{10,11... | collective-permute-start | bytes 24584 | tf_op jit(solution)/shard_map/ppermute | solution.py:198

commit v3 on v2

v3 whole, which is shorter than its diff:
```python
import functools

import jax
import jax.numpy as jnp
from jax import lax
from jax.experimental import pallas as pl
from jax.experimental.pallas import tpu as pltpu
from jax.sharding import PartitionSpec as P

LEVELS = 120
CLASSES = 4
REACH = 8
EPSILON = 1e-06
VMEM_LIMIT = 24 * 1024 * 1024

SMEM = functools.partial(pl.BlockSpec, memory_space=pltpu.SMEM)
VMEM = functools.partial(pl.BlockSpec, memory_space=pltpu.VMEM)
HBM = functools.partial(pl.BlockSpec, memory_space=pltpu.HBM)


def in_hbm(array):
    return pltpu.with_memory_space_constraint(array, pltpu.HBM)


def live_lanes(shape):
    return lax.broadcasted_iota(jnp.int32, shape, len(shape) - 1) < LEVELS


def masked(values):
    return jnp.where(live_lanes(values.shape), values, 0.0)


def call(kernel, out_shape, in_specs, flops, moved, scratch=()):
    return pl.pallas_call(
        kernel,
        out_shape=out_shape,
        in_specs=in_specs,
        out_specs=jax.tree.map(lambda _: VMEM(), out_shape),
        scratch_shapes=list(scratch),
        compiler_params=pltpu.CompilerParams(vmem_limit_bytes=VMEM_LIMIT),
        cost_estimate=pl.CostEstimate(flops=flops, bytes_accessed=moved, transcendentals=0),
    )


def parity():
    return lax.rem(lax.axis_index("orbit"), 2)


def rounding_kernel(direction, across, within):
    rim = across.shape[0]
    odd = parity()
    for c in range(rim):
        across[c] = masked(direction[odd * rim + c]).astype(jnp.bfloat16)
        within[c] = masked(direction[(1 - odd) * rim + c]).astype(jnp.bfloat16)


def coupling(classes, cols, columns):
    total = classes.shape[0]
    first = lax.axis_index("orbit") * cols
    table = {}
    for c in columns:
        length = (classes[lax.rem(first + c + total, total)] + 1) * REACH // CLASSES
        for k in range(1, REACH + 1):
            table[c, k] = jnp.where(k <= length, jnp.float32(1.0 / (k * k)), jnp.float32(0.0))
    return table


def pull(table, to, values):
    result = None
    for c, value in values.items():
        if c != to and abs(c - to) <= REACH:
            term = table[min(c, to), abs(c - to)] * value
            result = term if result is None else result + term
    return -result


def inner_kernel(
    direction, count, residual_hbm, classes_hbm, smooth_hbm, sight_hbm, jac_hbm,
    begun, norm, curved, rows, jac, residual, classes, smooth, sight, sems,
):
    pairs = (
        (classes_hbm, classes), (smooth_hbm, smooth), (sight_hbm, sight),
        (residual_hbm, residual), (jac_hbm, jac),
    )
    copies = [pltpu.make_async_copy(*pair, sems.at[i]) for i, pair in enumerate(pairs)]
    for copy in copies:
        copy.start()
    copies[0].wait()
    copies[1].wait()
    cols = direction.shape[0]
    rim = cols // 2
    table = coupling(classes, cols, range(-REACH, cols))
    weight = smooth[...][:, None, :]
    total = jnp.zeros(norm.shape, jnp.float32)
    values = {c: masked(direction[c]) for c in range(cols)}
    rests = {c: v - v.astype(jnp.bfloat16).astype(jnp.float32) for c, v in values.items()}
    for c in range(cols):
        centre = jnp.float32(1.0)
        for k in range(1, REACH + 1):
            centre = centre + (table[c, k] + table[c - k, k])
        result = weight * (centre * values[c] + pull(table, c, values))
        begun[rim + c] = result
        total = total + jnp.sum(values[c] * result, axis=0)
    for q in range(rim):
        to_left = {c: values[c] if c >= rim else rests[c] for c in range(cols)}
        to_right = {c: values[c] if c < rim else rests[c] for c in range(cols)}
        begun[q] = weight * pull(table, q - rim, to_left)
        begun[rim + cols + q] = weight * pull(table, q + cols, to_right)
    curved[...] = total
    copies[2].wait()
    slot = lax.broadcasted_iota(jnp.int32, rows.shape, 0)
    rows[...] = jnp.where(slot < count[0], sight[...], 0.0)
    copies[3].wait()
    squares = jnp.zeros(norm.shape, jnp.float32)
    for c in range(cols):
        mres = masked(residual[c])
        squares = squares + jnp.sum(mres * mres, axis=0)
    norm[...] = squares
    copies[4].wait()


def forward_kernel(
    crossing, classes, rows, direction, smooth, across, within, from_across, from_within,
    begun, norm, curved, jac, weighted, own, sums, window,
):
    slots, crossings = crossing.shape
    cols, species = direction.shape[:2]
    rim = across.shape[0]
    span = rim * species
    odd = parity()
    places = (1 + odd, across), (2 - odd, within), (3 * odd, from_across), (3 - 3 * odd, from_within)
    for place, part in places:
        window[pl.ds(place * span, span)] = part[...].reshape(span, *part.shape[2:])
    total = curved[...]
    for i in range(slots):
        picked = jnp.concatenate([window[crossing[i, j]] for j in range(crossings)], axis=1)
        tiles = jnp.concatenate([jac[i, j] for j in range(crossings)], axis=1)
        integrals = lax.dot_general(
            tiles, picked, (((1,), (1,)), ((), ())), preferred_element_type=jnp.float32
        )
        integrals = jnp.transpose(integrals)
        product = (rows[pl.ds(i, 1), :] * integrals).astype(jnp.bfloat16)
        weighted[i] = product
        total = total + product.astype(jnp.float32) * integrals
    table = coupling(classes, cols, range(-rim, cols))
    weight = smooth[...][:, None, :]
    before, after = {}, {}
    for c in range(rim):
        before[c - rim] = window[pl.ds(c * species, species)].astype(jnp.float32)
        after[c + cols] = window[pl.ds(3 * span + c * species, species)].astype(jnp.float32)
    for c in range(cols):
        from_before = weight * pull(table, c, before)
        from_after = weight * pull(table, c, after)
        own[c] = begun[rim + c] + (from_before + from_after)
        edges = from_after if c < rim else from_after + from_before
        total = total + 2.0 * jnp.sum(masked(direction[c]) * edges, axis=0)
    half = sums.shape[1]
    parts = [jnp.sum(x, axis=1, keepdims=True) for x in (norm[...], total)]
    parts = [part[h * half : (h + 1) * half] for h in range(2) for part in parts]
    lane = lax.broadcasted_iota(jnp.int32, sums.shape[1:], 1)
    block = jnp.zeros(sums.shape[1:], jnp.float32)
    for k, part in enumerate(parts):
        block = jnp.where(lane == k, part, block)
    sums[...] = jnp.broadcast_to(block[None], sums.shape)


def backward_kernel(crossing, weighted, jac, begun, own, image, across, within, sums):
    slots, crossings = crossing.shape
    cols, species, probes, tile = own.shape
    rim = across.shape[0]
    span = rim * species
    middle = pl.ds(span, 2 * span)
    sums[pl.ds(0, span)] = begun[pl.ds(0, rim)].reshape(span, probes, tile)
    sums[middle] = own[...].reshape(2 * span, probes, tile)
    sums[pl.ds(3 * span, span)] = begun[pl.ds(rim + cols, rim)].reshape(span, probes, tile)
    for i in range(slots):
        tiles = jnp.concatenate([jac[i, j] for j in range(crossings)], axis=1)
        terms = jnp.dot(weighted[i], tiles, preferred_element_type=jnp.float32)
        for j in range(crossings):
            sums[crossing[i, j]] += terms[:, j * tile : (j + 1) * tile]
    odd = parity()
    for part, place in (across, 3 * odd), (within, 3 - 3 * odd):
        part[...] = sums[pl.ds(place * span, span)].astype(part.dtype).reshape(part.shape)
    image[...] = sums[middle].reshape(image.shape)


def final_kernel(
    solution, residual, direction, image, from_across, from_within, sums,
    solution_next, residual_next, step_length,
):
    whole = jnp.sum(sums[...], axis=0)
    norm = jnp.concatenate([whole[:, 0:1], whole[:, 2:3]], axis=0)
    curvature = jnp.concatenate([whole[:, 1:2], whole[:, 3:4]], axis=0)
    step = norm / (curvature + EPSILON)
    rim = from_across.shape[0]
    wide = jnp.broadcast_to(step, direction.shape[2:])
    step_length[...] = jnp.transpose(wide)[0:1]
    wide = wide[None]
    odd = parity()
    for q in range(rim):
        for c, part in (odd * rim + q, from_across), ((1 - odd) * rim + q, from_within):
            total = masked(image[c] + part[q].astype(jnp.float32))
            solution_next[c] = masked(solution[c] + wide * direction[c])
            residual_next[c] = masked(residual[c]) - wide * total


def swapped(across, within):
    count = lax.axis_size("orbit")
    assert count % 2 == 0
    outer = [(i, (i + 2 * (i % 2) - 1) % count) for i in range(count)]
    inner = [(i, i ^ 1) for i in range(count)]
    return lax.ppermute(across, "orbit", outer), lax.ppermute(within, "orbit", inner)


def local(
    solution, residual, direction, jacobian, crossing, tile_count, sightline_weight,
    length_class, smooth_weight,
):
    cols, species, probes, width = direction.shape
    assert REACH <= cols
    rim = cols // 2
    slots = crossing.shape[0]
    f32, bf16 = jnp.float32, jnp.bfloat16
    shape = jax.ShapeDtypeStruct
    column = (species, probes, width)
    elements = direction.size
    dot_flops = 2 * jacobian.size * probes
    near = shape((rim,) + column, bf16)
    whole = shape(direction.shape, f32)
    small = shape((probes, width), f32)

    across, within = call(
        rounding_kernel, (near, near), [VMEM()], 2 * elements, 6 * elements
    )(direction)
    from_across, from_within = swapped(across, within)

    begun, norm, curved, rows, jac = call(
        inner_kernel,
        (
            shape((2 * cols,) + column, f32), small, small,
            shape(sightline_weight.shape, f32), shape(jacobian.shape, bf16),
        ),
        [VMEM(), SMEM()] + [HBM()] * 5,
        60 * elements,
        4 * jacobian.size,
        [
            pltpu.VMEM(direction.shape, f32),
            pltpu.SMEM(length_class.shape, jnp.int32),
            pltpu.VMEM(smooth_weight.shape, f32),
            pltpu.VMEM(sightline_weight.shape, f32),
            pltpu.SemaphoreType.DMA((5,)),
        ],
    )(
        direction, tile_count,
        *map(in_hbm, (residual, length_class, smooth_weight, sightline_weight, jacobian)),
    )

    devices = lax.axis_size("orbit")
    weighted, own, sums = call(
        forward_kernel,
        (
            shape((slots, probes, width), bf16), whole,
            shape((devices, probes // 2, width), f32),
        ),
        [SMEM()] * 2 + [VMEM()] * 11,
        dot_flops,
        2 * jacobian.size,
        [pltpu.VMEM((2 * cols * species, probes, width), bf16)],
    )(
        crossing, length_class, rows, direction, smooth_weight,
        across, within, from_across, from_within, begun, norm, curved, jac,
    )
    sums = lax.all_to_all(sums, "orbit", 0, 0)

    image, across, within = call(
        backward_kernel,
        (whole, near, near),
        [SMEM()] + [VMEM()] * 4,
        dot_flops,
        2 * jacobian.size,
        [pltpu.VMEM((2 * cols * species, probes, width), f32)],
    )(crossing, weighted, jac, begun, own)
    from_across, from_within = swapped(across, within)

    solution_next, residual_next, step_length = call(
        final_kernel,
        (whole, whole, shape((1, probes), f32)),
        [VMEM()] * 7,
        8 * elements,
        28 * elements,
    )(solution, residual, direction, image, from_across, from_within, sums)
    return solution_next, residual_next, step_length.reshape(probes)


def solution(mesh):
    wide = P(("grp", "orbit"), None, None, None)
    placed = (
        wide, wide, wide, wide,
        P(("grp", "orbit"), None),
        P(("grp", "orbit")),
        P(("grp", "orbit"), None),
        P("grp"),
        P(),
    )
    return jax.shard_map(
        local, mesh=mesh, in_specs=placed, out_specs=(wide, wide, P("grp")), check_vma=False
    )
```

time: 34.7 us -> 30.2 us (0.87)
  waiting for transfers between devices: 13 us -> 0.01 us
  blocking collectives: 0 us -> 9.55 us
  starting transfers between devices: 10.1 us -> 8.94 us
    ppermute x8 -> x4, waiting for transfers between devices: 13 us -> 0.01 us  [the longest x2 0.01 us: swapped(): lax.ppermute(within, 'orbit', inner)]
    all_to_all x0 -> x1, blocking collectives: none -> 9.55 us  [local(): sums = lax.all_to_all(sums, 'orbit', 0, 0)]
    ppermute x8 -> x4, starting transfers between devices: 10.1 us -> 8.94 us  [the longest x2 8.93 us: swapped(): lax.ppermute(across, 'orbit', outer)]
    unnamed x16 -> x14, local copies, waits for them, and re-layouts: 1.07 us -> 1.07 us
  transfers between devices with their start and end apart: 8 -> 4, of which waited for: 4 -> 0; matrix products, arithmetic and copies ran while one was open for 0% -> 0% of each run, Pallas kernels for 9% -> 10%
where the time goes in v3:
time: 30.2 us; the launch traced here: 29.9 us
  blocking collectives  9.55 us (32%)
  Pallas kernels  8.97 us (30%)
  starting transfers between devices  8.94 us (30%)
  between operations  1.4 us (5%)
  local copies, waits for them, and re-layouts  1.07 us (4%)
    all_to_all x1, blocking collectives, local(): sums = lax.all_to_all(sums, 'orbit', 0, 0)  9.55 us
    ppermute x2, starting transfers between devices, swapped(): lax.ppermute(across, 'orbit', outer)  8.93 us
    pallas_call x1, Pallas kernels, local(): call(inner_kernel, (shape((2 * cols,) + column, f32), small, small, shape...  3.05 us
    pallas_call x1, Pallas kernels, local(): call(forward_kernel, (shape((slots, probes, width), bf16), whole, shape((...  2.84 us
    pallas_call x1, Pallas kernels, local(): call(backward_kernel, (whole, near, near), [SMEM()] + [VMEM()] * 4, dot_f...  1.8 us
    pallas_call x1, Pallas kernels, local(): call(final_kernel, (whole, whole, shape((1, probes), f32)), [VMEM()] * 7,...  1.25 us
    unnamed x14, local copies, waits for them, and re-layouts  1.07 us
  transfers between devices with their start and end apart: 4, of which 0 were waited for; matrix products, arithmetic and copies ran while one was open for 0% of the time, Pallas kernels for 10%

profile of v3, /device:TPU:0, one launch (start us, length us, event | category | flops | bytes accessed | tf_op | source)
XLA Modules:
  0.0 29.9 jit_solution(15024326233580752501)
XLA Ops:
  0.6 0.0 copy-start
  0.6 1.0 %copy-done = f32[8,8,16,128]{3,2,1,0:T(8,128)S(1)} copy-done((f32[8,8,16,128]{3,2,1,0:T(8,128)S(1)}, f32[8,8,16,128]{3,2,1,0:T(8,128)}, u32[]{:S(2)}) %copy-start) | copy-done | bytes 524312
  1.7 0.0 copy-start.4
  1.7 0.0 copy-start.5
  1.7 0.0 copy-start.6
  1.7 5.5 %collective-permute-start = (bf16[4,8,16,128]{3,2,1,0:T(8,128)(2,1)S(1)}, bf16[4,8,16,128]{3,2,1,0:T(8,128)(2,1)S(1)}, u32[]{:S(2)}, u32[]{:S(2)}) collective-permute-start(bf16[4,8,16,128]{3,2,1,0:T(8,128)(2,1)S(1)} %get-tuple-element.20.across), channel_id=1, source_target_pairs={{0,15},{1,2},{2,1},{3,4},{4,3},{5,6},{6,5},{7,8},{8,7},{9,10},{10,... | collective-permute-start | bytes 393224 | tf_op jit(solution)/shard_map/ppermute | solution.py:212
  7.2 0.0 collective-permute-start.1
  7.9 3.0 %shard_map.112 = (f32[16,8,16,128]{3,2,1,0:T(8,128)S(1)}, f32[16,128]{1,0:T(8,128)S(1)}, f32[16,128]{1,0:T(8,128)S(1)}, f32[8,128]{1,0:T(8,128)S(1)}, bf16[8,24,128,128]{3,2,1,0:T(8,128)(2,1)S(1)}) custom-call(f32[8,8,16,128]{3,2,1,0:T(8,128)S(1)} %copy-done, s32[1]{0:T(128)S(6)} %copy.12.count, f32[8,8,16,128]{3,2,1,0:T(8,128)} %residual.1, s32[128]{0:T(128)} %classes.1, ...), custom_call_target="tpu_custom_call" | custom-call | flops 7864320 | bytes 12582912 | tf_op jit(solution)/shard_map/pallas_call | solution.py:237
  10.9 0.0 collective-permute-done.from_across
  11.0 0.0 collective-permute-done.1.from_within
  11.0 0.0 copy-done.4
  11.0 0.0 copy-done.5
  11.0 0.0 copy-done.6
  11.0 0.0 copy-start.1
  11.0 0.0 copy-start.2
  11.0 0.0 copy-start.3
  11.0 2.8 %shard_map.114 = (bf16[8,16,128]{2,1,0:T(8,128)(2,1)S(1)}, f32[8,8,16,128]{3,2,1,0:T(8,128)S(1)}, f32[16,8,128]{2,1,0:T(8,128)S(1)}) custom-call(s32[8,24]{1,0:T(8,128)S(1)} %copy-done.4, s32[128]{0:T(128)S(1)} %copy-done.6, f32[8,128]{1,0:T(8,128)S(1)} %get-tuple-element.19.rows, f32[8,8,16,128]{3,2,1,0:T(8,128)S(1)} %copy-done, f32[8,128]{1,0:T(8,128)S(1)} %copy-done.5, ...), custom_call_target="tpu_custom_call" | custom-call | flops 100663296 | bytes 6291456 | tf_op jit(solution)/shard_map/pallas_call | solution.py:259
  13.9 1.8 %shard_map.115 = (f32[8,8,16,128]{3,2,1,0:T(8,128)S(1)}, bf16[4,8,16,128]{3,2,1,0:T(8,128)(2,1)S(1)}, bf16[4,8,16,128]{3,2,1,0:T(8,128)(2,1)S(1)}) custom-call(s32[8,24]{1,0:T(8,128)S(1)} %copy-done.4, bf16[8,16,128]{2,1,0:T(8,128)(2,1)S(1)} %get-tuple-element.26.weighted, bf16[8,24,128,128]{3,2,1,0:T(8,128)(2,1)S(1)} %get-tuple-element.25.jac, ...), custom_call_target="tpu_custom_call" | custom-call | flops 100663296 | bytes 6291456 | tf_op jit(solution)/shard_map/pallas_call | solution.py:275
  15.7 3.4 %collective-permute-start.2 = (bf16[4,8,16,128]{3,2,1,0:T(8,128)(2,1)S(1)}, bf16[4,8,16,128]{3,2,1,0:T(8,128)(2,1)S(1)}, u32[]{:S(2)}, u32[]{:S(2)}) collective-permute-start(bf16[4,8,16,128]{3,2,1,0:T(8,128)(2,1)S(1)} %get-tuple-element.29), channel_id=1, source_target_pairs={{0,15},{1,2},{2,1},{3,4},{4,3},{5,6},{6,5},{7,8},{8,7},{9,10},{10,... | collective-permute-start | bytes 393224 | tf_op jit(solution)/shard_map/ppermute | solution.py:212
  19.1 0.0 collective-permute-start.3
  19.1 9.5 %all_to_all.5.sums = f32[16,8,128]{2,1,0:T(8,128)S(1)} all-to-all(f32[16,8,128]{2,1,0:T(8,128)S(1)} %get-tuple-element.31), channel_id=1, replica_groups=mesh['grp'=2,'orbit'=16] {'orbit'}, dimensions={0} | all-to-all | bytes 131072 | tf_op jit(solution)/shard_map/all_to_all | solution.py:273
  28.6 0.0 collective-permute-done.2.from_across
  28.6 0.0 collective-permute-done.3.from_within
  28.7 0.0 copy-done.1
  28.7 0.0 copy-done.2
  28.7 0.0 copy-done.3
  28.7 1.2 %shard_map.116 = (f32[8,8,16,128]{3,2,1,0:T(8,128)}, f32[8,8,16,128]{3,2,1,0:T(8,128)}, f32[1,16]{1,0:T(1,128)}) custom-call(f32[8,8,16,128]{3,2,1,0:T(8,128)S(1)} %copy-done.3, f32[8,8,16,128]{3,2,1,0:T(8,128)S(1)} %copy-done.2, f32[8,8,16,128]{3,2,1,0:T(8,128)S(1)} %copy-done.1, f32[8,8,16,128]{3,2,1,0:T(8,128)S(1)} %get-tuple-element.28.image, ...), custom_call_target="tpu_custom_call" | custom-call | flops 1048576 | bytes 3670016 | tf_op jit(solution)/shard_map/pallas_call | solution.py:285
  (1 shorter events, 0.0 us)
Async XLA Ops:
  0.6 1.0 %copy-start = (f32[8,8,16,128]{3,2,1,0:T(8,128)S(1)}, f32[8,8,16,128]{3,2,1,0:T(8,128)}, u32[]{:S(2)}) copy-start(f32[8,8,16,128]{3,2,1,0:T(8,128)} %direction.7) | copy-start | bytes 1572868
  1.7 9.3 %copy-start.4 = (s32[8,24]{1,0:T(8,128)S(1)}, s32[8,24]{1,0:T(8,128)}, u32[]{:S(2)}) copy-start(s32[8,24]{1,0:T(8,128)} %crossing.3) | copy-start | bytes 2308
  1.7 9.3 %copy-start.5 = (f32[8,128]{1,0:T(8,128)S(1)}, f32[8,128]{1,0:T(8,128)}, u32[]{:S(2)}) copy-start(f32[8,128]{1,0:T(8,128)} %smooth.1) | copy-start | bytes 12292
  1.7 9.3 %copy-start.6 = (s32[128]{0:T(128)S(1)}, s32[128]{0:T(128)}, u32[]{:S(2)}) copy-start(s32[128]{0:T(128)} %classes.1) | copy-start | bytes 1540
  1.7 9.2 %collective-permute-start = (bf16[4,8,16,128]{3,2,1,0:T(8,128)(2,1)S(1)}, bf16[4,8,16,128]{3,2,1,0:T(8,128)(2,1)S(1)}, u32[]{:S(2)}, u32[]{:S(2)}) collective-permute-start(bf16[4,8,16,128]{3,2,1,0:T(8,128)(2,1)S(1)} %get-tuple-element.20.across), channel_id=1, source_target_pairs={{0,15},{1,2},{2,1},{3,4},{4,3},{5,6},{6,5},{7,8},{8,7},{9,10},{10,... | collective-permute-start | bytes 393224 | tf_op jit(solution)/shard_map/ppermute | solution.py:212
  7.2 3.7 %collective-permute-start.1 = (bf16[4,8,16,128]{3,2,1,0:T(8,128)(2,1)S(1)}, bf16[4,8,16,128]{3,2,1,0:T(8,128)(2,1)S(1)}, u32[]{:S(2)}, u32[]{:S(2)}) collective-permute-start(bf16[4,8,16,128]{3,2,1,0:T(8,128)(2,1)S(1)} %get-tuple-element.21.within), channel_id=1, source_target_pairs={{0,1},{1,0},{2,3},{3,2},{4,5},{5,4},{6,7},{7,6},{8,9},{9,8},{10,11... | collective-permute-start | bytes 393224 | tf_op jit(solution)/shard_map/ppermute | solution.py:212
  11.0 17.7 %copy-start.1 = (f32[8,8,16,128]{3,2,1,0:T(8,128)S(1)}, f32[8,8,16,128]{3,2,1,0:T(8,128)}, u32[]{:S(2)}) copy-start(f32[8,8,16,128]{3,2,1,0:T(8,128)} %direction.7) | copy-start | bytes 1572868
  11.0 17.7 %copy-start.2 = (f32[8,8,16,128]{3,2,1,0:T(8,128)S(1)}, f32[8,8,16,128]{3,2,1,0:T(8,128)}, u32[]{:S(2)}) copy-start(f32[8,8,16,128]{3,2,1,0:T(8,128)} %residual.1) | copy-start | bytes 1572868
  11.0 17.7 %copy-start.3 = (f32[8,8,16,128]{3,2,1,0:T(8,128)S(1)}, f32[8,8,16,128]{3,2,1,0:T(8,128)}, u32[]{:S(2)}) copy-start(f32[8,8,16,128]{3,2,1,0:T(8,128)} %solution.1) | copy-start | bytes 1572868
  15.7 13.0 %collective-permute-start.2 = (bf16[4,8,16,128]{3,2,1,0:T(8,128)(2,1)S(1)}, bf16[4,8,16,128]{3,2,1,0:T(8,128)(2,1)S(1)}, u32[]{:S(2)}, u32[]{:S(2)}) collective-permute-start(bf16[4,8,16,128]{3,2,1,0:T(8,128)(2,1)S(1)} %get-tuple-element.29), channel_id=1, source_target_pairs={{0,15},{1,2},{2,1},{3,4},{4,3},{5,6},{6,5},{7,8},{8,7},{9,10},{10,... | collective-permute-start | bytes 393224 | tf_op jit(solution)/shard_map/ppermute | solution.py:212
  19.1 9.6 %collective-permute-start.3 = (bf16[4,8,16,128]{3,2,1,0:T(8,128)(2,1)S(1)}, bf16[4,8,16,128]{3,2,1,0:T(8,128)(2,1)S(1)}, u32[]{:S(2)}, u32[]{:S(2)}) collective-permute-start(bf16[4,8,16,128]{3,2,1,0:T(8,128)(2,1)S(1)} %get-tuple-element.30), channel_id=1, source_target_pairs={{0,1},{1,0},{2,3},{3,2},{4,5},{5,4},{6,7},{7,6},{8,9},{9,8},{10,11... | collective-permute-start | bytes 393224 | tf_op jit(solution)/shard_map/ppermute | solution.py:212

commit v4 on v3

--- a/solution.py
+++ b/solution.py
@@ -154,14 +154,14 @@
         own[c] = begun[rim + c] + (from_before + from_after)
         edges = from_after if c < rim else from_after + from_before
         total = total + 2.0 * jnp.sum(masked(direction[c]) * edges, axis=0)
-    half = sums.shape[1]
+    half = sums.shape[0]
     parts = [jnp.sum(x, axis=1, keepdims=True) for x in (norm[...], total)]
     parts = [part[h * half : (h + 1) * half] for h in range(2) for part in parts]
-    lane = lax.broadcasted_iota(jnp.int32, sums.shape[1:], 1)
-    block = jnp.zeros(sums.shape[1:], jnp.float32)
+    lane = lax.broadcasted_iota(jnp.int32, sums.shape, 1)
+    block = jnp.zeros(sums.shape, jnp.float32)
     for k, part in enumerate(parts):
         block = jnp.where(lane == k, part, block)
-    sums[...] = jnp.broadcast_to(block[None], sums.shape)
+    sums[...] = block
 
 
 def backward_kernel(crossing, weighted, jac, begun, own, image, across, within, sums):
@@ -255,12 +255,11 @@
         *map(in_hbm, (residual, length_class, smooth_weight, sightline_weight, jacobian)),
     )
 
-    devices = lax.axis_size("orbit")
     weighted, own, sums = call(
         forward_kernel,
         (
             shape((slots, probes, width), bf16), whole,
-            shape((devices, probes // 2, width), f32),
+            shape((probes // 2, width), f32),
         ),
         [SMEM()] * 2 + [VMEM()] * 11,
         dot_flops,
@@ -270,7 +269,7 @@
         crossing, length_class, rows, direction, smooth_weight,
         across, within, from_across, from_within, begun, norm, curved, jac,
     )
-    sums = lax.all_to_all(sums, "orbit", 0, 0)
+    sums = lax.all_gather(sums, "orbit")
 
     image, across, within = call(
         backward_kernel,

time: 30.2 us -> 39.3 us (1.30)
  blocking collectives: 9.55 us -> 18.7 us
    all_gather x0 -> x1, blocking collectives: none -> 18.7 us  [local(): sums = lax.all_gather(sums, 'orbit')]
    all_to_all x1 -> x0, blocking collectives: 9.55 us -> none  [local(): sums = lax.all_to_all(sums, 'orbit', 0, 0)]
  transfers between devices with their start and end apart: 4 -> 4, of which waited for: 0 -> 0; matrix products, arithmetic and copies ran while one was open for 0% -> 0% of each run, Pallas kernels for 10% -> 8%
where the time goes in v4:
time: 39.3 us; the launch traced here: 39.1 us
  blocking collectives  18.7 us (48%)
  Pallas kernels  8.97 us (23%)
  starting transfers between devices  8.93 us (23%)
  between operations  1.4 us (4%)
  local copies, waits for them, and re-layouts  1.07 us (3%)
    all_gather x1, blocking collectives, local(): sums = lax.all_gather(sums, 'orbit')  18.7 us
    ppermute x2, starting transfers between devices, swapped(): lax.ppermute(across, 'orbit', outer)  8.93 us
    pallas_call x1, Pallas kernels, local(): call(inner_kernel, (shape((2 * cols,) + column, f32), small, small, shape...  3.05 us
    pallas_call x1, Pallas kernels, local(): call(forward_kernel, (shape((slots, probes, width), bf16), whole, shape((...  2.84 us
    pallas_call x1, Pallas kernels, local(): call(backward_kernel, (whole, near, near), [SMEM()] + [VMEM()] * 4, dot_f...  1.8 us
    pallas_call x1, Pallas kernels, local(): call(final_kernel, (whole, whole, shape((1, probes), f32)), [VMEM()] * 7,...  1.25 us
    unnamed x14, local copies, waits for them, and re-layouts  1.07 us
  transfers between devices with their start and end apart: 4, of which 0 were waited for; matrix products, arithmetic and copies ran while one was open for 0% of the time, Pallas kernels for 8%

profile of v4, /device:TPU:0, one launch (start us, length us, event | category | flops | bytes accessed | tf_op | source)
XLA Modules:
  0.0 39.1 jit_solution(13413379061597445951)
XLA Ops:
  0.6 0.0 copy-start
  0.6 1.0 %copy-done = f32[8,8,16,128]{3,2,1,0:T(8,128)S(1)} copy-done((f32[8,8,16,128]{3,2,1,0:T(8,128)S(1)}, f32[8,8,16,128]{3,2,1,0:T(8,128)}, u32[]{:S(2)}) %copy-start) | copy-done | bytes 524312
  1.7 0.0 copy-start.4
  1.7 0.0 copy-start.5
  1.7 0.0 copy-start.6
  1.7 5.5 %collective-permute-start = (bf16[4,8,16,128]{3,2,1,0:T(8,128)(2,1)S(1)}, bf16[4,8,16,128]{3,2,1,0:T(8,128)(2,1)S(1)}, u32[]{:S(2)}, u32[]{:S(2)}) collective-permute-start(bf16[4,8,16,128]{3,2,1,0:T(8,128)(2,1)S(1)} %get-tuple-element.20.across), channel_id=1, source_target_pairs={{0,15},{1,2},{2,1},{3,4},{4,3},{5,6},{6,5},{7,8},{8,7},{9,10},{10,... | collective-permute-start | bytes 393224 | tf_op jit(solution)/shard_map/ppermute | solution.py:212
  7.2 0.0 collective-permute-start.1
  7.9 3.0 %shard_map.112 = (f32[16,8,16,128]{3,2,1,0:T(8,128)S(1)}, f32[16,128]{1,0:T(8,128)S(1)}, f32[16,128]{1,0:T(8,128)S(1)}, f32[8,128]{1,0:T(8,128)S(1)}, bf16[8,24,128,128]{3,2,1,0:T(8,128)(2,1)S(1)}) custom-call(f32[8,8,16,128]{3,2,1,0:T(8,128)S(1)} %copy-done, s32[1]{0:T(128)S(6)} %copy.12.count, f32[8,8,16,128]{3,2,1,0:T(8,128)} %residual.1, s32[128]{0:T(128)} %classes.1, ...), custom_call_target="tpu_custom_call" | custom-call | flops 7864320 | bytes 12582912 | tf_op jit(solution)/shard_map/pallas_call | solution.py:237
  10.9 0.0 collective-permute-done.from_across
  11.0 0.0 collective-permute-done.1.from_within
  11.0 0.0 copy-done.4
  11.0 0.0 copy-done.5
  11.0 0.0 copy-done.6
  11.0 0.0 copy-start.1
  11.0 0.0 copy-start.2
  11.0 0.0 copy-start.3
  11.0 2.8 %shard_map.114 = (bf16[8,16,128]{2,1,0:T(8,128)(2,1)S(1)}, f32[8,8,16,128]{3,2,1,0:T(8,128)S(1)}, f32[8,128]{1,0:T(8,128)S(1)}) custom-call(s32[8,24]{1,0:T(8,128)S(1)} %copy-done.4, s32[128]{0:T(128)S(1)} %copy-done.6, f32[8,128]{1,0:T(8,128)S(1)} %get-tuple-element.19.rows, f32[8,8,16,128]{3,2,1,0:T(8,128)S(1)} %copy-done, f32[8,128]{1,0:T(8,128)S(1)} %copy-done.5, ...), custom_call_target="tpu_custom_call" | custom-call | flops 100663296 | bytes 6291456 | tf_op jit(solution)/shard_map/pallas_call | solution.py:258
  13.9 1.8 %shard_map.115 = (f32[8,8,16,128]{3,2,1,0:T(8,128)S(1)}, bf16[4,8,16,128]{3,2,1,0:T(8,128)(2,1)S(1)}, bf16[4,8,16,128]{3,2,1,0:T(8,128)(2,1)S(1)}) custom-call(s32[8,24]{1,0:T(8,128)S(1)} %copy-done.4, bf16[8,16,128]{2,1,0:T(8,128)(2,1)S(1)} %get-tuple-element.26.weighted, bf16[8,24,128,128]{3,2,1,0:T(8,128)(2,1)S(1)} %get-tuple-element.25.jac, ...), custom_call_target="tpu_custom_call" | custom-call | flops 100663296 | bytes 6291456 | tf_op jit(solution)/shard_map/pallas_call | solution.py:274
  15.7 3.4 %collective-permute-start.2 = (bf16[4,8,16,128]{3,2,1,0:T(8,128)(2,1)S(1)}, bf16[4,8,16,128]{3,2,1,0:T(8,128)(2,1)S(1)}, u32[]{:S(2)}, u32[]{:S(2)}) collective-permute-start(bf16[4,8,16,128]{3,2,1,0:T(8,128)(2,1)S(1)} %get-tuple-element.29), channel_id=1, source_target_pairs={{0,15},{1,2},{2,1},{3,4},{4,3},{5,6},{6,5},{7,8},{8,7},{9,10},{10,... | collective-permute-start | bytes 393224 | tf_op jit(solution)/shard_map/ppermute | solution.py:212
  19.1 0.0 collective-permute-start.3
  19.1 18.7 %all-gather = f32[128,128]{1,0:T(8,128)S(1)} all-gather(f32[8,128]{1,0:T(8,128)S(1)} %get-tuple-element.31), channel_id=2, replica_groups=mesh['grp'=2,'orbit'=16] {'orbit'}, dimensions={0}, use_global_device_ids=true | all-gather | bytes 69632 | tf_op jit(solution)/shard_map/all_gather | solution.py:272
  37.8 0.0 collective-permute-done.2.from_across
  37.8 0.0 collective-permute-done.3.from_within
  37.8 0.0 copy-done.1
  37.8 0.0 copy-done.2
  37.8 0.0 copy-done.3
  37.8 1.2 %shard_map.116 = (f32[8,8,16,128]{3,2,1,0:T(8,128)}, f32[8,8,16,128]{3,2,1,0:T(8,128)}, f32[1,16]{1,0:T(1,128)}) custom-call(f32[8,8,16,128]{3,2,1,0:T(8,128)S(1)} %copy-done.3, f32[8,8,16,128]{3,2,1,0:T(8,128)S(1)} %copy-done.2, f32[8,8,16,128]{3,2,1,0:T(8,128)S(1)} %copy-done.1, f32[8,8,16,128]{3,2,1,0:T(8,128)S(1)} %get-tuple-element.28.image, ...), custom_call_target="tpu_custom_call" | custom-call | flops 1048576 | bytes 3670016 | tf_op jit(solution)/shard_map/pallas_call | solution.py:284
  (1 shorter events, 0.0 us)
Async XLA Ops:
  0.6 1.0 %copy-start = (f32[8,8,16,128]{3,2,1,0:T(8,128)S(1)}, f32[8,8,16,128]{3,2,1,0:T(8,128)}, u32[]{:S(2)}) copy-start(f32[8,8,16,128]{3,2,1,0:T(8,128)} %direction.7) | copy-start | bytes 1572868
  1.7 9.3 %copy-start.4 = (s32[8,24]{1,0:T(8,128)S(1)}, s32[8,24]{1,0:T(8,128)}, u32[]{:S(2)}) copy-start(s32[8,24]{1,0:T(8,128)} %crossing.3) | copy-start | bytes 2308
  1.7 9.3 %copy-start.5 = (f32[8,128]{1,0:T(8,128)S(1)}, f32[8,128]{1,0:T(8,128)}, u32[]{:S(2)}) copy-start(f32[8,128]{1,0:T(8,128)} %smooth.1) | copy-start | bytes 12292
  1.7 9.3 %copy-start.6 = (s32[128]{0:T(128)S(1)}, s32[128]{0:T(128)}, u32[]{:S(2)}) copy-start(s32[128]{0:T(128)} %classes.1) | copy-start | bytes 1540
  1.7 9.2 %collective-permute-start = (bf16[4,8,16,128]{3,2,1,0:T(8,128)(2,1)S(1)}, bf16[4,8,16,128]{3,2,1,0:T(8,128)(2,1)S(1)}, u32[]{:S(2)}, u32[]{:S(2)}) collective-permute-start(bf16[4,8,16,128]{3,2,1,0:T(8,128)(2,1)S(1)} %get-tuple-element.20.across), channel_id=1, source_target_pairs={{0,15},{1,2},{2,1},{3,4},{4,3},{5,6},{6,5},{7,8},{8,7},{9,10},{10,... | collective-permute-start | bytes 393224 | tf_op jit(solution)/shard_map/ppermute | solution.py:212
  7.2 3.7 %collective-permute-start.1 = (bf16[4,8,16,128]{3,2,1,0:T(8,128)(2,1)S(1)}, bf16[4,8,16,128]{3,2,1,0:T(8,128)(2,1)S(1)}, u32[]{:S(2)}, u32[]{:S(2)}) collective-permute-start(bf16[4,8,16,128]{3,2,1,0:T(8,128)(2,1)S(1)} %get-tuple-element.21.within), channel_id=1, source_target_pairs={{0,1},{1,0},{2,3},{3,2},{4,5},{5,4},{6,7},{7,6},{8,9},{9,8},{10,11... | collective-permute-start | bytes 393224 | tf_op jit(solution)/shard_map/ppermute | solution.py:212
  11.0 26.8 %copy-start.1 = (f32[8,8,16,128]{3,2,1,0:T(8,128)S(1)}, f32[8,8,16,128]{3,2,1,0:T(8,128)}, u32[]{:S(2)}) copy-start(f32[8,8,16,128]{3,2,1,0:T(8,128)} %direction.7) | copy-start | bytes 1572868
  11.0 26.8 %copy-start.2 = (f32[8,8,16,128]{3,2,1,0:T(8,128)S(1)}, f32[8,8,16,128]{3,2,1,0:T(8,128)}, u32[]{:S(2)}) copy-start(f32[8,8,16,128]{3,2,1,0:T(8,128)} %residual.1) | copy-start | bytes 1572868
  11.0 26.8 %copy-start.3 = (f32[8,8,16,128]{3,2,1,0:T(8,128)S(1)}, f32[8,8,16,128]{3,2,1,0:T(8,128)}, u32[]{:S(2)}) copy-start(f32[8,8,16,128]{3,2,1,0:T(8,128)} %solution.1) | copy-start | bytes 1572868
  15.7 22.1 %collective-permute-start.2 = (bf16[4,8,16,128]{3,2,1,0:T(8,128)(2,1)S(1)}, bf16[4,8,16,128]{3,2,1,0:T(8,128)(2,1)S(1)}, u32[]{:S(2)}, u32[]{:S(2)}) collective-permute-start(bf16[4,8,16,128]{3,2,1,0:T(8,128)(2,1)S(1)} %get-tuple-element.29), channel_id=1, source_target_pairs={{0,15},{1,2},{2,1},{3,4},{4,3},{5,6},{6,5},{7,8},{8,7},{9,10},{10,... | collective-permute-start | bytes 393224 | tf_op jit(solution)/shard_map/ppermute | solution.py:212
  19.1 18.7 %collective-permute-start.3 = (bf16[4,8,16,128]{3,2,1,0:T(8,128)(2,1)S(1)}, bf16[4,8,16,128]{3,2,1,0:T(8,128)(2,1)S(1)}, u32[]{:S(2)}, u32[]{:S(2)}) collective-permute-start(bf16[4,8,16,128]{3,2,1,0:T(8,128)(2,1)S(1)} %get-tuple-element.30), channel_id=1, source_target_pairs={{0,1},{1,0},{2,3},{3,2},{4,5},{5,4},{6,7},{7,6},{8,9},{9,8},{10,11... | collective-permute-start | bytes 393224 | tf_op jit(solution)/shard_map/ppermute | solution.py:212

commit v5 on v4

--- a/solution.py
+++ b/solution.py
@@ -255,6 +255,8 @@
         *map(in_hbm, (residual, length_class, smooth_weight, sightline_weight, jacobian)),
     )
 
+    devices = lax.axis_size("orbit")
+    chips = devices // 2
     weighted, own, sums = call(
         forward_kernel,
         (
@@ -269,7 +271,7 @@
         crossing, length_class, rows, direction, smooth_weight,
         across, within, from_across, from_within, begun, norm, curved, jac,
     )
-    sums = lax.all_gather(sums, "orbit")
+    twin = lax.ppermute(sums, "orbit", [(i, i ^ 1) for i in range(devices)])
 
     image, across, within = call(
         backward_kernel,
@@ -279,7 +281,11 @@
         2 * jacobian.size,
         [pltpu.VMEM((2 * cols * species, probes, width), f32)],
     )(crossing, weighted, jac, begun, own)
+    across, within, twin = lax.optimization_barrier((across, within, twin))
     from_across, from_within = swapped(across, within)
+    alike = [[2 * i + core for i in range(chips)] for core in range(2)]
+    sums = jnp.broadcast_to((sums + twin)[None], (chips,) + sums.shape)
+    sums = lax.all_to_all(sums, "orbit", 0, 0, axis_index_groups=alike)
 
     solution_next, residual_next, step_length = call(
         final_kernel,

time: 39.3 us -> 30.3 us (0.77)
  blocking collectives: 18.7 us -> 9.72 us
    all_gather x1 -> x0, blocking collectives: 18.7 us -> none  [local(): sums = lax.all_gather(sums, 'orbit')]
    all_to_all x0 -> x1, blocking collectives: none -> 9.72 us  [local(): sums = lax.all_to_all(sums, 'orbit', 0, 0, axis_index_groups=alike)]
    ppermute x0 -> x1, starting transfers between devices: none -> 0.51 us  [local(): twin = lax.ppermute(sums, 'orbit', [(i, i ^ 1) for i in range(devices)])]
    ppermute x2, starting transfers between devices: 8.93 us -> 8.44 us  [swapped(): lax.ppermute(across, 'orbit', outer)]
  transfers between devices with their start and end apart: 4 -> 5, of which waited for: 0 -> 0; matrix products, arithmetic and copies ran while one was open for 0% -> 0% of each run, Pallas kernels for 8% -> 16%
where the time goes in v5:
time: 30.3 us; the launch traced here: 30.1 us
  blocking collectives  9.72 us (32%)
  Pallas kernels  8.95 us (30%)
  starting transfers between devices  8.95 us (30%)
  between operations  1.41 us (5%)
  local copies, waits for them, and re-layouts  1.07 us (4%)
    all_to_all x1, blocking collectives, local(): sums = lax.all_to_all(sums, 'orbit', 0, 0, axis_index_groups=alike)  9.72 us
    ppermute x2, starting transfers between devices, swapped(): lax.ppermute(across, 'orbit', outer)  8.44 us
    pallas_call x1, Pallas kernels, local(): call(inner_kernel, (shape((2 * cols,) + column, f32), small, small, shape...  3.05 us
    pallas_call x1, Pallas kernels, local(): call(forward_kernel, (shape((slots, probes, width), bf16), whole, shape((...  2.84 us
    pallas_call x1, Pallas kernels, local(): call(backward_kernel, (whole, near, near), [SMEM()] + [VMEM()] * 4, dot_f...  1.79 us
    pallas_call x1, Pallas kernels, local(): call(final_kernel, (whole, whole, shape((1, probes), f32)), [VMEM()] * 7,...  1.24 us
    unnamed x14, local copies, waits for them, and re-layouts  1.07 us
  transfers between devices with their start and end apart: 5, of which 0 were waited for; matrix products, arithmetic and copies ran while one was open for 0% of the time, Pallas kernels for 16%

profile of v5, /device:TPU:0, one launch (start us, length us, event | category | flops | bytes accessed | tf_op | source)
XLA Modules:
  0.0 30.1 jit_solution(2619515392675545038)
XLA Ops:
  0.6 0.0 copy-start
  0.6 1.0 %copy-done = f32[8,8,16,128]{3,2,1,0:T(8,128)S(1)} copy-done((f32[8,8,16,128]{3,2,1,0:T(8,128)S(1)}, f32[8,8,16,128]{3,2,1,0:T(8,128)}, u32[]{:S(2)}) %copy-start) | copy-done | bytes 524312
  1.7 0.0 copy-start.4
  1.7 0.0 copy-start.5
  1.7 0.0 copy-start.6
  1.7 5.5 %collective-permute-start = (bf16[4,8,16,128]{3,2,1,0:T(8,128)(2,1)S(1)}, bf16[4,8,16,128]{3,2,1,0:T(8,128)(2,1)S(1)}, u32[]{:S(2)}, u32[]{:S(2)}) collective-permute-start(bf16[4,8,16,128]{3,2,1,0:T(8,128)(2,1)S(1)} %get-tuple-element.23.across), channel_id=1, source_target_pairs={{0,15},{1,2},{2,1},{3,4},{4,3},{5,6},{6,5},{7,8},{8,7},{9,10},{10,... | collective-permute-start | bytes 393224 | tf_op jit(solution)/shard_map/ppermute | solution.py:212
  7.2 0.0 collective-permute-start.1
  7.9 3.0 %shard_map.112 = (f32[16,8,16,128]{3,2,1,0:T(8,128)S(1)}, f32[16,128]{1,0:T(8,128)S(1)}, f32[16,128]{1,0:T(8,128)S(1)}, f32[8,128]{1,0:T(8,128)S(1)}, bf16[8,24,128,128]{3,2,1,0:T(8,128)(2,1)S(1)}) custom-call(f32[8,8,16,128]{3,2,1,0:T(8,128)S(1)} %copy-done, s32[1]{0:T(128)S(6)} %copy.12.count, f32[8,8,16,128]{3,2,1,0:T(8,128)} %residual.1, s32[128]{0:T(128)} %classes.1, ...), custom_call_target="tpu_custom_call" | custom-call | flops 7864320 | bytes 12582912 | tf_op jit(solution)/shard_map/pallas_call | solution.py:237
  10.9 0.0 collective-permute-done.from_across
  11.0 0.0 collective-permute-done.1.from_within
  11.0 0.0 copy-done.4
  11.0 0.0 copy-done.5
  11.0 0.0 copy-done.6
  11.0 0.0 copy-start.1
  11.0 0.0 copy-start.2
  11.0 0.0 copy-start.3
  11.0 2.8 %shard_map.114 = (bf16[8,16,128]{2,1,0:T(8,128)(2,1)S(1)}, f32[8,8,16,128]{3,2,1,0:T(8,128)S(1)}, f32[8,128]{1,0:T(8,128)S(1)}) custom-call(s32[8,24]{1,0:T(8,128)S(1)} %copy-done.4, s32[128]{0:T(128)S(1)} %copy-done.6, f32[8,128]{1,0:T(8,128)S(1)} %get-tuple-element.22.rows, f32[8,8,16,128]{3,2,1,0:T(8,128)S(1)} %copy-done, f32[8,128]{1,0:T(8,128)S(1)} %copy-done.5, ...), custom_call_target="tpu_custom_call" | custom-call | flops 100663296 | bytes 6291456 | tf_op jit(solution)/shard_map/pallas_call | solution.py:260
  13.9 0.5 %collective-permute-start.2 = (f32[8,128]{1,0:T(8,128)S(1)}, f32[8,128]{1,0:T(8,128)S(1)}, u32[]{:S(2)}, u32[]{:S(2)}) collective-permute-start(f32[8,128]{1,0:T(8,128)S(1)} %get-tuple-element.34), channel_id=1, source_target_pairs={{0,1},{1,0},{2,3},{3,2},{4,5},{5,4},{6,7},{7,6},{8,9},{9,8},{10,11... | collective-permute-start | bytes 12296 | tf_op jit(solution)/shard_map/ppermute | solution.py:274
  14.4 1.8 %shard_map.115 = (f32[8,8,16,128]{3,2,1,0:T(8,128)S(1)}, bf16[4,8,16,128]{3,2,1,0:T(8,128)(2,1)S(1)}, bf16[4,8,16,128]{3,2,1,0:T(8,128)(2,1)S(1)}) custom-call(s32[8,24]{1,0:T(8,128)S(1)} %copy-done.4, bf16[8,16,128]{2,1,0:T(8,128)(2,1)S(1)} %get-tuple-element.29.weighted, bf16[8,24,128,128]{3,2,1,0:T(8,128)(2,1)S(1)} %get-tuple-element.28.jac, ...), custom_call_target="tpu_custom_call" | custom-call | flops 100663296 | bytes 6291456 | tf_op jit(solution)/shard_map/pallas_call | solution.py:276
  16.2 0.0 collective-permute-done.2
  16.2 2.9 %collective-permute-start.3 = (bf16[4,8,16,128]{3,2,1,0:T(8,128)(2,1)S(1)}, bf16[4,8,16,128]{3,2,1,0:T(8,128)(2,1)S(1)}, u32[]{:S(2)}, u32[]{:S(2)}) collective-permute-start(bf16[4,8,16,128]{3,2,1,0:T(8,128)(2,1)S(1)} %get-tuple-element.35), channel_id=1, source_target_pairs={{0,15},{1,2},{2,1},{3,4},{4,3},{5,6},{6,5},{7,8},{8,7},{9,10},{10,... | collective-permute-start | bytes 393224 | tf_op jit(solution)/shard_map/ppermute | solution.py:212
  19.1 0.0 collective-permute-start.4
  19.1 9.7 %all_to_all.5.sums = f32[8,8,128]{2,1,0:T(8,128)S(1)} all-to-all(f32[8,8,128]{2,1,0:T(8,128)S(1)} %broadcast_in_dim.2), channel_id=1, replica_groups={{0,2,4,6,8,10,12,14},{1,3,5,7,9,11,13,15},{16,18,20,22,24,26,28,30},{17..., dimensions={0} | all-to-all | bytes 65536 | tf_op jit(solution)/shard_map/all_to_all | solution.py:288
  28.8 0.0 collective-permute-done.3.from_across
  28.9 0.0 collective-permute-done.4.from_within
  28.9 0.0 copy-done.1
  28.9 0.0 copy-done.2
  28.9 0.0 copy-done.3
  28.9 1.2 %shard_map.116 = (f32[8,8,16,128]{3,2,1,0:T(8,128)}, f32[8,8,16,128]{3,2,1,0:T(8,128)}, f32[1,16]{1,0:T(1,128)}) custom-call(f32[8,8,16,128]{3,2,1,0:T(8,128)S(1)} %copy-done.3, f32[8,8,16,128]{3,2,1,0:T(8,128)S(1)} %copy-done.2, f32[8,8,16,128]{3,2,1,0:T(8,128)S(1)} %copy-done.1, f32[8,8,16,128]{3,2,1,0:T(8,128)S(1)} %get-tuple-element.31.image, ...), custom_call_target="tpu_custom_call" | custom-call | flops 1048576 | bytes 3670016 | tf_op jit(solution)/shard_map/pallas_call | solution.py:290
  (3 shorter events, 0.0 us)
Async XLA Ops:
  0.6 1.0 %copy-start = (f32[8,8,16,128]{3,2,1,0:T(8,128)S(1)}, f32[8,8,16,128]{3,2,1,0:T(8,128)}, u32[]{:S(2)}) copy-start(f32[8,8,16,128]{3,2,1,0:T(8,128)} %direction.7) | copy-start | bytes 1572868
  1.7 9.3 %copy-start.4 = (s32[8,24]{1,0:T(8,128)S(1)}, s32[8,24]{1,0:T(8,128)}, u32[]{:S(2)}) copy-start(s32[8,24]{1,0:T(8,128)} %crossing.3) | copy-start | bytes 2308
  1.7 9.3 %copy-start.5 = (f32[8,128]{1,0:T(8,128)S(1)}, f32[8,128]{1,0:T(8,128)}, u32[]{:S(2)}) copy-start(f32[8,128]{1,0:T(8,128)} %smooth.1) | copy-start | bytes 12292
  1.7 9.3 %copy-start.6 = (s32[128]{0:T(128)S(1)}, s32[128]{0:T(128)}, u32[]{:S(2)}) copy-start(s32[128]{0:T(128)} %classes.1) | copy-start | bytes 1540
  1.7 9.2 %collective-permute-start = (bf16[4,8,16,128]{3,2,1,0:T(8,128)(2,1)S(1)}, bf16[4,8,16,128]{3,2,1,0:T(8,128)(2,1)S(1)}, u32[]{:S(2)}, u32[]{:S(2)}) collective-permute-start(bf16[4,8,16,128]{3,2,1,0:T(8,128)(2,1)S(1)} %get-tuple-element.23.across), channel_id=1, source_target_pairs={{0,15},{1,2},{2,1},{3,4},{4,3},{5,6},{6,5},{7,8},{8,7},{9,10},{10,... | collective-permute-start | bytes 393224 | tf_op jit(solution)/shard_map/ppermute | solution.py:212
  7.2 3.7 %collective-permute-start.1 = (bf16[4,8,16,128]{3,2,1,0:T(8,128)(2,1)S(1)}, bf16[4,8,16,128]{3,2,1,0:T(8,128)(2,1)S(1)}, u32[]{:S(2)}, u32[]{:S(2)}) collective-permute-start(bf16[4,8,16,128]{3,2,1,0:T(8,128)(2,1)S(1)} %get-tuple-element.24.within), channel_id=1, source_target_pairs={{0,1},{1,0},{2,3},{3,2},{4,5},{5,4},{6,7},{7,6},{8,9},{9,8},{10,11... | collective-permute-start | bytes 393224 | tf_op jit(solution)/shard_map/ppermute | solution.py:212
  11.0 17.9 %copy-start.1 = (f32[8,8,16,128]{3,2,1,0:T(8,128)S(1)}, f32[8,8,16,128]{3,2,1,0:T(8,128)}, u32[]{:S(2)}) copy-start(f32[8,8,16,128]{3,2,1,0:T(8,128)} %direction.7) | copy-start | bytes 1572868
  11.0 17.9 %copy-start.2 = (f32[8,8,16,128]{3,2,1,0:T(8,128)S(1)}, f32[8,8,16,128]{3,2,1,0:T(8,128)}, u32[]{:S(2)}) copy-start(f32[8,8,16,128]{3,2,1,0:T(8,128)} %residual.1) | copy-start | bytes 1572868
  11.0 17.9 %copy-start.3 = (f32[8,8,16,128]{3,2,1,0:T(8,128)S(1)}, f32[8,8,16,128]{3,2,1,0:T(8,128)}, u32[]{:S(2)}) copy-start(f32[8,8,16,128]{3,2,1,0:T(8,128)} %solution.1) | copy-start | bytes 1572868
  13.9 2.3 %collective-permute-start.2 = (f32[8,128]{1,0:T(8,128)S(1)}, f32[8,128]{1,0:T(8,128)S(1)}, u32[]{:S(2)}, u32[]{:S(2)}) collective-permute-start(f32[8,128]{1,0:T(8,128)S(1)} %get-tuple-element.34), channel_id=1, source_target_pairs={{0,1},{1,0},{2,3},{3,2},{4,5},{5,4},{6,7},{7,6},{8,9},{9,8},{10,11... | collective-permute-start | bytes 12296 | tf_op jit(solution)/shard_map/ppermute | solution.py:274
  16.2 12.7 %collective-permute-start.3 = (bf16[4,8,16,128]{3,2,1,0:T(8,128)(2,1)S(1)}, bf16[4,8,16,128]{3,2,1,0:T(8,128)(2,1)S(1)}, u32[]{:S(2)}, u32[]{:S(2)}) collective-permute-start(bf16[4,8,16,128]{3,2,1,0:T(8,128)(2,1)S(1)} %get-tuple-element.35), channel_id=1, source_target_pairs={{0,15},{1,2},{2,1},{3,4},{4,3},{5,6},{6,5},{7,8},{8,7},{9,10},{10,... | collective-permute-start | bytes 393224 | tf_op jit(solution)/shard_map/ppermute | solution.py:212
  19.1 9.7 %collective-permute-start.4 = (bf16[4,8,16,128]{3,2,1,0:T(8,128)(2,1)S(1)}, bf16[4,8,16,128]{3,2,1,0:T(8,128)(2,1)S(1)}, u32[]{:S(2)}, u32[]{:S(2)}) collective-permute-start(bf16[4,8,16,128]{3,2,1,0:T(8,128)(2,1)S(1)} %get-tuple-element.36), channel_id=1, source_target_pairs={{0,1},{1,0},{2,3},{3,2},{4,5},{5,4},{6,7},{7,6},{8,9},{9,8},{10,11... | collective-permute-start | bytes 393224 | tf_op jit(solution)/shard_map/ppermute | solution.py:212

commit v6 on v5

--- a/solution.py
+++ b/solution.py
@@ -256,7 +256,7 @@
     )
 
     devices = lax.axis_size("orbit")
-    chips = devices // 2
+    peers = devices // 2
     weighted, own, sums = call(
         forward_kernel,
         (
@@ -271,7 +271,8 @@
         crossing, length_class, rows, direction, smooth_weight,
         across, within, from_across, from_within, begun, norm, curved, jac,
     )
-    twin = lax.ppermute(sums, "orbit", [(i, i ^ 1) for i in range(devices)])
+    assert devices % 4 == 0
+    twin = lax.ppermute(sums, "orbit", [(i, i ^ 2) for i in range(devices)])
 
     image, across, within = call(
         backward_kernel,
@@ -283,8 +284,8 @@
     )(crossing, weighted, jac, begun, own)
     across, within, twin = lax.optimization_barrier((across, within, twin))
     from_across, from_within = swapped(across, within)
-    alike = [[2 * i + core for i in range(chips)] for core in range(2)]
-    sums = jnp.broadcast_to((sums + twin)[None], (chips,) + sums.shape)
+    alike = [[i for i in range(devices) if i & 2 == side] for side in (0, 2)]
+    sums = jnp.broadcast_to((sums + twin)[None], (peers,) + sums.shape)
     sums = lax.all_to_all(sums, "orbit", 0, 0, axis_index_groups=alike)
 
     solution_next, residual_next, step_length = call(

time: 30.3 us -> 29.3 us (0.967)
  waiting for transfers between devices: 0.01 us -> 1.81 us
  blocking collectives: 9.72 us -> 8.11 us
  starting transfers between devices: 8.95 us -> 7.72 us
    ppermute x1, waiting for transfers between devices: 0.01 us -> 1.8 us  [local(): twin = lax.ppermute(sums, 'orbit', [(i, i ^ 2) for i in range(devices)])]
    all_to_all x1, blocking collectives: 9.72 us -> 8.11 us  [local(): sums = lax.all_to_all(sums, 'orbit', 0, 0, axis_index_groups=alike)]
    ppermute x2, starting transfers between devices: 8.44 us -> 7.71 us  [swapped(): lax.ppermute(across, 'orbit', outer)]
    ppermute x1, starting transfers between devices: 0.51 us -> 0.01 us  [local(): twin = lax.ppermute(sums, 'orbit', [(i, i ^ 2) for i in range(devices)])]
  transfers between devices with their start and end apart: 5 -> 5, of which waited for: 0 -> 1; matrix products, arithmetic and copies ran while one was open for 0% -> 0% of each run, Pallas kernels for 16% -> 17%
where the time goes in v6:
time: 29.3 us; the launch traced here: 29.1 us
  Pallas kernels  8.95 us (31%)
  blocking collectives  8.11 us (28%)
  starting transfers between devices  7.72 us (26%)
  waiting for transfers between devices  1.81 us (6%)
  between operations  1.41 us (5%)
  local copies, waits for them, and re-layouts  1.07 us (4%)
    all_to_all x1, blocking collectives, local(): sums = lax.all_to_all(sums, 'orbit', 0, 0, axis_index_groups=alike)  8.11 us
    ppermute x2, starting transfers between devices, swapped(): lax.ppermute(across, 'orbit', outer)  7.71 us
    pallas_call x1, Pallas kernels, local(): call(inner_kernel, (shape((2 * cols,) + column, f32), small, small, shape...  3.05 us
    pallas_call x1, Pallas kernels, local(): call(forward_kernel, (shape((slots, probes, width), bf16), whole, shape((...  2.84 us
    ppermute x1, waiting for transfers between devices, local(): twin = lax.ppermute(sums, 'orbit', [(i, i ^ 2) for i in range(devices)])  1.8 us
    pallas_call x1, Pallas kernels, local(): call(backward_kernel, (whole, near, near), [SMEM()] + [VMEM()] * 4, dot_f...  1.8 us
    pallas_call x1, Pallas kernels, local(): call(final_kernel, (whole, whole, shape((1, probes), f32)), [VMEM()] * 7,...  1.24 us
    unnamed x14, local copies, waits for them, and re-layouts  1.07 us
  transfers between devices with their start and end apart: 5, of which 1 were waited for; matrix products, arithmetic and copies ran while one was open for 0% of the time, Pallas kernels for 17%

profile of v6, /device:TPU:0, one launch (start us, length us, event | category | flops | bytes accessed | tf_op | source)
XLA Modules:
  0.0 29.1 jit_solution(16129791226991466928)
XLA Ops:
  0.6 0.0 copy-start
  0.6 1.0 %copy-done = f32[8,8,16,128]{3,2,1,0:T(8,128)S(1)} copy-done((f32[8,8,16,128]{3,2,1,0:T(8,128)S(1)}, f32[8,8,16,128]{3,2,1,0:T(8,128)}, u32[]{:S(2)}) %copy-start) | copy-done | bytes 524312
  1.7 0.0 copy-start.4
  1.7 0.0 copy-start.5
  1.7 0.0 copy-start.6
  1.7 5.5 %collective-permute-start = (bf16[4,8,16,128]{3,2,1,0:T(8,128)(2,1)S(1)}, bf16[4,8,16,128]{3,2,1,0:T(8,128)(2,1)S(1)}, u32[]{:S(2)}, u32[]{:S(2)}) collective-permute-start(bf16[4,8,16,128]{3,2,1,0:T(8,128)(2,1)S(1)} %get-tuple-element.23.across), channel_id=1, source_target_pairs={{0,15},{1,2},{2,1},{3,4},{4,3},{5,6},{6,5},{7,8},{8,7},{9,10},{10,... | collective-permute-start | bytes 393224 | tf_op jit(solution)/shard_map/ppermute | solution.py:212
  7.2 0.0 collective-permute-start.1
  7.9 3.0 %shard_map.112 = (f32[16,8,16,128]{3,2,1,0:T(8,128)S(1)}, f32[16,128]{1,0:T(8,128)S(1)}, f32[16,128]{1,0:T(8,128)S(1)}, f32[8,128]{1,0:T(8,128)S(1)}, bf16[8,24,128,128]{3,2,1,0:T(8,128)(2,1)S(1)}) custom-call(f32[8,8,16,128]{3,2,1,0:T(8,128)S(1)} %copy-done, s32[1]{0:T(128)S(6)} %copy.12.count, f32[8,8,16,128]{3,2,1,0:T(8,128)} %residual.1, s32[128]{0:T(128)} %classes.1, ...), custom_call_target="tpu_custom_call" | custom-call | flops 7864320 | bytes 12582912 | tf_op jit(solution)/shard_map/pallas_call | solution.py:237
  10.9 0.0 collective-permute-done.from_across
  11.0 0.0 collective-permute-done.1.from_within
  11.0 0.0 copy-done.4
  11.0 0.0 copy-done.5
  11.0 0.0 copy-done.6
  11.0 0.0 copy-start.1
  11.0 0.0 copy-start.2
  11.0 0.0 copy-start.3
  11.0 2.8 %shard_map.114 = (bf16[8,16,128]{2,1,0:T(8,128)(2,1)S(1)}, f32[8,8,16,128]{3,2,1,0:T(8,128)S(1)}, f32[8,128]{1,0:T(8,128)S(1)}) custom-call(s32[8,24]{1,0:T(8,128)S(1)} %copy-done.4, s32[128]{0:T(128)S(1)} %copy-done.6, f32[8,128]{1,0:T(8,128)S(1)} %get-tuple-element.22.rows, f32[8,8,16,128]{3,2,1,0:T(8,128)S(1)} %copy-done, f32[8,128]{1,0:T(8,128)S(1)} %copy-done.5, ...), custom_call_target="tpu_custom_call" | custom-call | flops 100663296 | bytes 6291456 | tf_op jit(solution)/shard_map/pallas_call | solution.py:260
  13.9 0.0 collective-permute-start.2
  13.9 1.8 %shard_map.115 = (f32[8,8,16,128]{3,2,1,0:T(8,128)S(1)}, bf16[4,8,16,128]{3,2,1,0:T(8,128)(2,1)S(1)}, bf16[4,8,16,128]{3,2,1,0:T(8,128)(2,1)S(1)}) custom-call(s32[8,24]{1,0:T(8,128)S(1)} %copy-done.4, bf16[8,16,128]{2,1,0:T(8,128)(2,1)S(1)} %get-tuple-element.29.weighted, bf16[8,24,128,128]{3,2,1,0:T(8,128)(2,1)S(1)} %get-tuple-element.28.jac, ...), custom_call_target="tpu_custom_call" | custom-call | flops 100663296 | bytes 6291456 | tf_op jit(solution)/shard_map/pallas_call | solution.py:277
  15.7 1.8 %collective-permute-done.2 = f32[8,128]{1,0:T(8,128)S(1)} collective-permute-done((f32[8,128]{1,0:T(8,128)S(1)}, f32[8,128]{1,0:T(8,128)S(1)}, u32[]{:S(2)}, u32[]{:S(2)}) %collective-permute-start.2) | collective-permute-done | bytes 4128 | tf_op jit(solution)/shard_map/ppermute | solution.py:275
  17.5 2.2 %collective-permute-start.3 = (bf16[4,8,16,128]{3,2,1,0:T(8,128)(2,1)S(1)}, bf16[4,8,16,128]{3,2,1,0:T(8,128)(2,1)S(1)}, u32[]{:S(2)}, u32[]{:S(2)}) collective-permute-start(bf16[4,8,16,128]{3,2,1,0:T(8,128)(2,1)S(1)} %get-tuple-element.35), channel_id=1, source_target_pairs={{0,15},{1,2},{2,1},{3,4},{4,3},{5,6},{6,5},{7,8},{8,7},{9,10},{10,... | collective-permute-start | bytes 393224 | tf_op jit(solution)/shard_map/ppermute | solution.py:212
  19.7 0.0 collective-permute-start.4
  19.7 8.1 %all_to_all.5.sums = f32[8,8,128]{2,1,0:T(8,128)S(1)} all-to-all(f32[8,8,128]{2,1,0:T(8,128)S(1)} %broadcast_in_dim.2), channel_id=1, replica_groups={{0,1,4,5,8,9,12,13},{2,3,6,7,10,11,14,15},{16,17,20,21,24,25,28,29},{18..., dimensions={0} | all-to-all | bytes 65536 | tf_op jit(solution)/shard_map/all_to_all | solution.py:289
  27.8 0.0 collective-permute-done.3.from_across
  27.8 0.0 collective-permute-done.4.from_within
  27.8 0.0 copy-done.1
  27.8 0.0 copy-done.2
  27.8 0.0 copy-done.3
  27.8 1.2 %shard_map.116 = (f32[8,8,16,128]{3,2,1,0:T(8,128)}, f32[8,8,16,128]{3,2,1,0:T(8,128)}, f32[1,16]{1,0:T(1,128)}) custom-call(f32[8,8,16,128]{3,2,1,0:T(8,128)S(1)} %copy-done.3, f32[8,8,16,128]{3,2,1,0:T(8,128)S(1)} %copy-done.2, f32[8,8,16,128]{3,2,1,0:T(8,128)S(1)} %copy-done.1, f32[8,8,16,128]{3,2,1,0:T(8,128)S(1)} %get-tuple-element.31.image, ...), custom_call_target="tpu_custom_call" | custom-call | flops 1048576 | bytes 3670016 | tf_op jit(solution)/shard_map/pallas_call | solution.py:291
  (3 shorter events, 0.0 us)
Async XLA Ops:
  0.6 1.0 %copy-start = (f32[8,8,16,128]{3,2,1,0:T(8,128)S(1)}, f32[8,8,16,128]{3,2,1,0:T(8,128)}, u32[]{:S(2)}) copy-start(f32[8,8,16,128]{3,2,1,0:T(8,128)} %direction.7) | copy-start | bytes 1572868
  1.7 9.3 %copy-start.4 = (s32[8,24]{1,0:T(8,128)S(1)}, s32[8,24]{1,0:T(8,128)}, u32[]{:S(2)}) copy-start(s32[8,24]{1,0:T(8,128)} %crossing.3) | copy-start | bytes 2308
  1.7 9.3 %copy-start.5 = (f32[8,128]{1,0:T(8,128)S(1)}, f32[8,128]{1,0:T(8,128)}, u32[]{:S(2)}) copy-start(f32[8,128]{1,0:T(8,128)} %smooth.1) | copy-start | bytes 12292
  1.7 9.3 %copy-start.6 = (s32[128]{0:T(128)S(1)}, s32[128]{0:T(128)}, u32[]{:S(2)}) copy-start(s32[128]{0:T(128)} %classes.1) | copy-start | bytes 1540
  1.7 9.2 %collective-permute-start = (bf16[4,8,16,128]{3,2,1,0:T(8,128)(2,1)S(1)}, bf16[4,8,16,128]{3,2,1,0:T(8,128)(2,1)S(1)}, u32[]{:S(2)}, u32[]{:S(2)}) collective-permute-start(bf16[4,8,16,128]{3,2,1,0:T(8,128)(2,1)S(1)} %get-tuple-element.23.across), channel_id=1, source_target_pairs={{0,15},{1,2},{2,1},{3,4},{4,3},{5,6},{6,5},{7,8},{8,7},{9,10},{10,... | collective-permute-start | bytes 393224 | tf_op jit(solution)/shard_map/ppermute | solution.py:212
  7.2 3.7 %collective-permute-start.1 = (bf16[4,8,16,128]{3,2,1,0:T(8,128)(2,1)S(1)}, bf16[4,8,16,128]{3,2,1,0:T(8,128)(2,1)S(1)}, u32[]{:S(2)}, u32[]{:S(2)}) collective-permute-start(bf16[4,8,16,128]{3,2,1,0:T(8,128)(2,1)S(1)} %get-tuple-element.24.within), channel_id=1, source_target_pairs={{0,1},{1,0},{2,3},{3,2},{4,5},{5,4},{6,7},{7,6},{8,9},{9,8},{10,11... | collective-permute-start | bytes 393224 | tf_op jit(solution)/shard_map/ppermute | solution.py:212
  11.0 16.8 %copy-start.1 = (f32[8,8,16,128]{3,2,1,0:T(8,128)S(1)}, f32[8,8,16,128]{3,2,1,0:T(8,128)}, u32[]{:S(2)}) copy-start(f32[8,8,16,128]{3,2,1,0:T(8,128)} %direction.7) | copy-start | bytes 1572868
  11.0 16.8 %copy-start.2 = (f32[8,8,16,128]{3,2,1,0:T(8,128)S(1)}, f32[8,8,16,128]{3,2,1,0:T(8,128)}, u32[]{:S(2)}) copy-start(f32[8,8,16,128]{3,2,1,0:T(8,128)} %residual.1) | copy-start | bytes 1572868
  11.0 16.8 %copy-start.3 = (f32[8,8,16,128]{3,2,1,0:T(8,128)S(1)}, f32[8,8,16,128]{3,2,1,0:T(8,128)}, u32[]{:S(2)}) copy-start(f32[8,8,16,128]{3,2,1,0:T(8,128)} %solution.1) | copy-start | bytes 1572868
  13.9 3.6 %collective-permute-start.2 = (f32[8,128]{1,0:T(8,128)S(1)}, f32[8,128]{1,0:T(8,128)S(1)}, u32[]{:S(2)}, u32[]{:S(2)}) collective-permute-start(f32[8,128]{1,0:T(8,128)S(1)} %get-tuple-element.34), channel_id=1, source_target_pairs={{0,2},{1,3},{2,0},{3,1},{4,6},{5,7},{6,4},{7,5},{8,10},{9,11},{10,... | collective-permute-start | bytes 12296 | tf_op jit(solution)/shard_map/ppermute | solution.py:275
  17.5 10.3 %collective-permute-start.3 = (bf16[4,8,16,128]{3,2,1,0:T(8,128)(2,1)S(1)}, bf16[4,8,16,128]{3,2,1,0:T(8,128)(2,1)S(1)}, u32[]{:S(2)}, u32[]{:S(2)}) collective-permute-start(bf16[4,8,16,128]{3,2,1,0:T(8,128)(2,1)S(1)} %get-tuple-element.35), channel_id=1, source_target_pairs={{0,15},{1,2},{2,1},{3,4},{4,3},{5,6},{6,5},{7,8},{8,7},{9,10},{10,... | collective-permute-start | bytes 393224 | tf_op jit(solution)/shard_map/ppermute | solution.py:212
  19.7 8.1 %collective-permute-start.4 = (bf16[4,8,16,128]{3,2,1,0:T(8,128)(2,1)S(1)}, bf16[4,8,16,128]{3,2,1,0:T(8,128)(2,1)S(1)}, u32[]{:S(2)}, u32[]{:S(2)}) collective-permute-start(bf16[4,8,16,128]{3,2,1,0:T(8,128)(2,1)S(1)} %get-tuple-element.36), channel_id=1, source_target_pairs={{0,1},{1,0},{2,3},{3,2},{4,5},{5,4},{6,7},{7,6},{8,9},{9,8},{10,11... | collective-permute-start | bytes 393224 | tf_op jit(solution)/shard_map/ppermute | solution.py:212

commit v7 on v6

--- a/solution.py
+++ b/solution.py
@@ -30,12 +30,12 @@
     return jnp.where(live_lanes(values.shape), values, 0.0)
 
 
-def call(kernel, out_shape, in_specs, flops, moved, scratch=()):
+def call(kernel, out_shape, in_specs, flops, moved, scratch=(), out_specs=None):
     return pl.pallas_call(
         kernel,
         out_shape=out_shape,
         in_specs=in_specs,
-        out_specs=jax.tree.map(lambda _: VMEM(), out_shape),
+        out_specs=tuple(out_specs or [VMEM()] * len(out_shape)),
         scratch_shapes=list(scratch),
         compiler_params=pltpu.CompilerParams(vmem_limit_bytes=VMEM_LIMIT),
         cost_estimate=pl.CostEstimate(flops=flops, bytes_accessed=moved, transcendentals=0),
@@ -74,33 +74,77 @@
     return -result
 
 
-def inner_kernel(
-    direction, count, residual_hbm, classes_hbm, smooth_hbm, sight_hbm, jac_hbm,
-    begun, norm, curved, rows, jac, residual, classes, smooth, sight, sems,
+def side_pulls(table, values, on_left, cols):
+    rim = len(values)
+    for c in range(cols):
+        result = None
+        for q, value in enumerate(values):
+            before, after = c - q + rim, q + cols - c
+            left = table[q - rim, before] if before <= REACH else jnp.float32(0.0)
+            right = table[c, after] if after <= REACH else jnp.float32(0.0)
+            term = jnp.where(on_left, left, right) * value
+            result = term if result is None else result + term
+        counted = jnp.where(on_left, jnp.float32(0.0 if c < rim else 2.0), jnp.float32(2.0))
+        yield c, -result, counted
+
+
+def early_positions(crossings):
+    return 2 * (crossings * 7 // 24)
+
+
+def shadow_kernel(
+    count, direction, across, within, from_within,
+    residual_hbm, classes_hbm, smooth_hbm, sight_hbm, crossing_hbm, jac_hbm,
+    begun, norm, curved, rows, jac, partial, order,
+    residual, classes, smooth, sight, crossing, window, sems,
 ):
+    slots, crossings = crossing.shape
     pairs = (
-        (classes_hbm, classes), (smooth_hbm, smooth), (sight_hbm, sight),
-        (residual_hbm, residual), (jac_hbm, jac),
+        (classes_hbm, classes), (smooth_hbm, smooth), (sight_hbm, sight), (residual_hbm, residual),
+        (crossing_hbm, crossing),
     )
     copies = [pltpu.make_async_copy(*pair, sems.at[i]) for i, pair in enumerate(pairs)]
-    for copy in copies:
+    loads = [
+        pltpu.make_async_copy(jac_hbm.at[i], jac.at[i], sems.at[len(pairs) + i]) for i in range(slots)
+    ]
+    for copy in copies + loads:
         copy.start()
+    cols, species = direction.shape[:2]
+    rim = cols // 2
+    span = rim * species
+    odd = parity()
+
+    for place, part in (1 + odd, across), (2 - odd, within), (3 - 3 * odd, from_within):
+        window[pl.ds(place * span, span)] = part[...].reshape(span, *part.shape[2:])
+    window[4 * span] = jnp.zeros(window.shape[1:], window.dtype)
+
+    copies[4].wait()
+    known_from = (1 - odd) * span
+    for i in range(slots):
+        head, tail = jnp.int32(0), jnp.int32(crossings - 1)
+        for j in range(crossings):
+            tile = crossing[i, j]
+            known = (tile >= known_from) & (tile < known_from + 3 * span)
+            order[i, jnp.where(known, head, tail)] = j
+            step = known.astype(jnp.int32)
+            head, tail = head + step, tail + step - 1
+        order[i, crossings] = head
+
     copies[0].wait()
     copies[1].wait()
-    cols = direction.shape[0]
-    rim = cols // 2
     table = coupling(classes, cols, range(-REACH, cols))
     weight = smooth[...][:, None, :]
     total = jnp.zeros(norm.shape, jnp.float32)
     values = {c: masked(direction[c]) for c in range(cols)}
     rests = {c: v - v.astype(jnp.bfloat16).astype(jnp.float32) for c, v in values.items()}
-    for c in range(cols):
+    beside = [from_within[q].astype(jnp.float32) for q in range(rim)]
+    for c, side, counted in side_pulls(table, beside, odd == 1, cols):
         centre = jnp.float32(1.0)
         for k in range(1, REACH + 1):
             centre = centre + (table[c, k] + table[c - k, k])
-        result = weight * (centre * values[c] + pull(table, c, values))
-        begun[rim + c] = result
-        total = total + jnp.sum(values[c] * result, axis=0)
+        inner = centre * values[c] + pull(table, c, values)
+        begun[rim + c] = weight * (inner + side)
+        total = total + jnp.sum(values[c] * (weight * (inner + counted * side)), axis=0)
     for q in range(rim):
         to_left = {c: values[c] if c >= rim else rests[c] for c in range(cols)}
         to_right = {c: values[c] if c < rim else rests[c] for c in range(cols)}
@@ -116,14 +160,31 @@
         mres = masked(residual[c])
         squares = squares + jnp.sum(mres * mres, axis=0)
     norm[...] = squares
-    copies[4].wait()
+
+    for i in range(slots):
+        loads[i].wait()
+        picked, tiles = [], []
+        for place in range(early_positions(crossings)):
+            j = order[i, place]
+            here = place < order[i, crossings]
+            picked.append(window[jnp.where(here, crossing[i, j], 4 * span)])
+            tiles.append(jac[i, j])
+        partial[i] = jnp.transpose(project(tiles, picked))
+
+
+def project(tiles, picked):
+    return lax.dot_general(
+        jnp.concatenate(tiles, axis=1), jnp.concatenate(picked, axis=1),
+        (((1,), (1,)), ((), ())), preferred_element_type=jnp.float32,
+    )
 
 
 def forward_kernel(
-    crossing, classes, rows, direction, smooth, across, within, from_across, from_within,
-    begun, norm, curved, jac, weighted, own, sums, window,
+    crossing, order, classes, rows, direction, smooth, across, within, from_across, from_within,
+    begun, norm, curved, jac, partial, weighted, own, sums, window, integrals,
 ):
     slots, crossings = crossing.shape
+    early = early_positions(crossings)
     cols, species = direction.shape[:2]
     rim = across.shape[0]
     span = rim * species
@@ -131,29 +192,38 @@
     places = (1 + odd, across), (2 - odd, within), (3 * odd, from_across), (3 - 3 * odd, from_within)
     for place, part in places:
         window[pl.ds(place * span, span)] = part[...].reshape(span, *part.shape[2:])
+    for i in range(slots):
+        picked, tiles = [], []
+        for place in range(early, crossings):
+            j = order[i, place]
+            picked.append(window[crossing[i, j]])
+            tiles.append(jac[i, j])
+        integrals[i] = partial[i] + jnp.transpose(project(tiles, picked))
+
+    fewest = order[0, crossings]
+    for i in range(1, slots):
+        fewest = jnp.minimum(fewest, order[i, crossings])
+
+    @pl.when(fewest < early)
+    def _():
+        for i in range(slots):
+            @pl.loop(order[i, crossings], early)
+            def _(place):
+                j = order[i, place]
+                integrals[i] += jnp.transpose(project([jac[i, j]], [window[crossing[i, j]]]))
+
     total = curved[...]
     for i in range(slots):
-        picked = jnp.concatenate([window[crossing[i, j]] for j in range(crossings)], axis=1)
-        tiles = jnp.concatenate([jac[i, j] for j in range(crossings)], axis=1)
-        integrals = lax.dot_general(
-            tiles, picked, (((1,), (1,)), ((), ())), preferred_element_type=jnp.float32
-        )
-        integrals = jnp.transpose(integrals)
-        product = (rows[pl.ds(i, 1), :] * integrals).astype(jnp.bfloat16)
+        product = (rows[pl.ds(i, 1), :] * integrals[i]).astype(jnp.bfloat16)
         weighted[i] = product
-        total = total + product.astype(jnp.float32) * integrals
+        total = total + product.astype(jnp.float32) * integrals[i]
     table = coupling(classes, cols, range(-rim, cols))
     weight = smooth[...][:, None, :]
-    before, after = {}, {}
-    for c in range(rim):
-        before[c - rim] = window[pl.ds(c * species, species)].astype(jnp.float32)
-        after[c + cols] = window[pl.ds(3 * span + c * species, species)].astype(jnp.float32)
-    for c in range(cols):
-        from_before = weight * pull(table, c, before)
-        from_after = weight * pull(table, c, after)
-        own[c] = begun[rim + c] + (from_before + from_after)
-        edges = from_after if c < rim else from_after + from_before
-        total = total + 2.0 * jnp.sum(masked(direction[c]) * edges, axis=0)
+    beside = [from_across[q].astype(jnp.float32) for q in range(rim)]
+    for c, side, counted in side_pulls(table, beside, odd == 0, cols):
+        side = weight * side
+        own[c] = begun[rim + c] + side
+        total = total + counted * jnp.sum(masked(direction[c]) * side, axis=0)
     half = sums.shape[0]
     parts = [jnp.sum(x, axis=1, keepdims=True) for x in (norm[...], total)]
     parts = [part[h * half : (h + 1) * half] for h in range(2) for part in parts]
@@ -209,7 +279,8 @@
     assert count % 2 == 0
     outer = [(i, (i + 2 * (i % 2) - 1) % count) for i in range(count)]
     inner = [(i, i ^ 1) for i in range(count)]
-    return lax.ppermute(across, "orbit", outer), lax.ppermute(within, "orbit", inner)
+    from_within = lax.ppermute(within, "orbit", inner)
+    return lax.ppermute(across, "orbit", outer), from_within
 
 
 def local(
@@ -219,7 +290,7 @@
     cols, species, probes, width = direction.shape
     assert REACH <= cols
     rim = cols // 2
-    slots = crossing.shape[0]
+    slots, crossings = crossing.shape
     f32, bf16 = jnp.float32, jnp.bfloat16
     shape = jax.ShapeDtypeStruct
     column = (species, probes, width)
@@ -234,25 +305,31 @@
     )(direction)
     from_across, from_within = swapped(across, within)
 
-    begun, norm, curved, rows, jac = call(
-        inner_kernel,
+    begun, norm, curved, rows, jac, partial, order = call(
+        shadow_kernel,
         (
             shape((2 * cols,) + column, f32), small, small,
             shape(sightline_weight.shape, f32), shape(jacobian.shape, bf16),
+            shape((slots, probes, width), f32), shape((slots, crossings + 1), jnp.int32),
         ),
-        [VMEM(), SMEM()] + [HBM()] * 5,
-        60 * elements,
+        [SMEM()] + [VMEM()] * 4 + [HBM()] * 6,
+        dot_flops,
         4 * jacobian.size,
         [
             pltpu.VMEM(direction.shape, f32),
             pltpu.SMEM(length_class.shape, jnp.int32),
             pltpu.VMEM(smooth_weight.shape, f32),
             pltpu.VMEM(sightline_weight.shape, f32),
-            pltpu.SemaphoreType.DMA((5,)),
+            pltpu.SMEM(crossing.shape, jnp.int32),
+            pltpu.VMEM((2 * cols * species + 1, probes, width), bf16),
+            pltpu.SemaphoreType.DMA((5 + slots,)),
         ],
+        [VMEM()] * 6 + [SMEM()],
     )(
-        direction, tile_count,
-        *map(in_hbm, (residual, length_class, smooth_weight, sightline_weight, jacobian)),
+        tile_count, direction, across, within, from_within,
+        *map(in_hbm, (
+            residual, length_class, smooth_weight, sightline_weight, crossing, jacobian,
+        )),
     )
 
     devices = lax.axis_size("orbit")
@@ -263,13 +340,16 @@
             shape((slots, probes, width), bf16), whole,
             shape((probes // 2, width), f32),
         ),
-        [SMEM()] * 2 + [VMEM()] * 11,
+        [SMEM()] * 3 + [VMEM()] * 12,
         dot_flops,
         2 * jacobian.size,
-        [pltpu.VMEM((2 * cols * species, probes, width), bf16)],
+        [
+            pltpu.VMEM((2 * cols * species, probes, width), bf16),
+            pltpu.VMEM((slots, probes, width), f32),
+        ],
     )(
-        crossing, length_class, rows, direction, smooth_weight,
-        across, within, from_across, from_within, begun, norm, curved, jac,
+        crossing, order, length_class, rows, direction, smooth_weight,
+        across, within, from_across, from_within, begun, norm, curved, jac, partial,
     )
     assert devices % 4 == 0
     twin = lax.ppermute(sums, "orbit", [(i, i ^ 2) for i in range(devices)])

time: 29.3 us -> 31.5 us (1.075)
  the two profiles are of different devices: /device:TPU:0 before, /device:TPU:6 now
where the time goes in v7:
time: 31.5 us; the launch traced here: 31.2 us
  Pallas kernels  12 us (38%)
  blocking collectives  11.8 us (37%)
  starting transfers between devices  4.74 us (15%)
  between operations  1.44 us (5%)
  local copies, waits for them, and re-layouts  1.07 us (3%)
    all_to_all x1, blocking collectives, local(): sums = lax.all_to_all(sums, 'orbit', 0, 0, axis_index_groups=alike)  11.8 us
    pallas_call x1, Pallas kernels, local(): call(shadow_kernel, (shape((2 * cols,) + column, f32), small, small, shap...  6.37 us
    ppermute x1, starting transfers between devices, local(): twin = lax.ppermute(sums, 'orbit', [(i, i ^ 2) for i in range(devices)])  3.92 us
    pallas_call x1, Pallas kernels, local(): call(forward_kernel, (shape((slots, probes, width), bf16), whole, shape((...  2.6 us
    pallas_call x1, Pallas kernels, local(): call(backward_kernel, (whole, near, near), [SMEM()] + [VMEM()] * 4, dot_f...  1.79 us
    pallas_call x1, Pallas kernels, local(): call(final_kernel, (whole, whole, shape((1, probes), f32)), [VMEM()] * 7,...  1.24 us
    unnamed x14, local copies, waits for them, and re-layouts  1.07 us
    ppermute x2, starting transfers between devices, swapped(): return (lax.ppermute(across, 'orbit', outer), from_within)  0.68 us
  transfers between devices with their start and end apart: 5, of which 1 were waited for; matrix products, arithmetic and copies ran while one was open for 0% of the time, Pallas kernels for 26%

profile of v7, /device:TPU:6, one launch (start us, length us, event | category | flops | bytes accessed | tf_op | source)
XLA Modules:
  0.0 31.2 jit_solution(14710572758656082237)
XLA Ops:
  0.6 0.0 copy-start
  0.6 1.0 %copy-done = f32[8,8,16,128]{3,2,1,0:T(8,128)S(1)} copy-done((f32[8,8,16,128]{3,2,1,0:T(8,128)S(1)}, f32[8,8,16,128]{3,2,1,0:T(8,128)}, u32[]{:S(2)}) %copy-start) | copy-done | bytes 524312
  1.7 0.0 copy-start.4
  1.7 0.0 copy-start.5
  1.7 0.0 copy-start.6
  1.7 0.1 collective-permute-start
  1.8 0.6 %collective-permute-start.1 = (bf16[4,8,16,128]{3,2,1,0:T(8,128)(2,1)S(1)}, bf16[4,8,16,128]{3,2,1,0:T(8,128)(2,1)S(1)}, u32[]{:S(2)}, u32[]{:S(2)}) collective-permute-start(bf16[4,8,16,128]{3,2,1,0:T(8,128)(2,1)S(1)} %get-tuple-element.24.across), channel_id=1, source_target_pairs={{0,15},{1,2},{2,1},{3,4},{4,3},{5,6},{6,5},{7,8},{8,7},{9,10},{10,... | collective-permute-start | bytes 393224 | tf_op jit(solution)/shard_map/ppermute | solution.py:283
  3.1 0.1 collective-permute-done.from_within
  3.1 6.4 %shard_map.113 = (f32[16,8,16,128]{3,2,1,0:T(8,128)S(1)}, f32[16,128]{1,0:T(8,128)S(1)}, f32[16,128]{1,0:T(8,128)S(1)}, f32[8,128]{1,0:T(8,128)S(1)}, bf16[8,24,...) custom-call(s32[1]{0:T(128)S(6)} %copy.12.count, f32[8,8,16,128]{3,2,1,0:T(8,128)S(1)} %copy-done, ...), custom_call_target="tpu_custom_call" | custom-call | flops 100663296 | bytes 12582912 | tf_op jit(solution)/shard_map/pallas_call | solution.py:308
  9.5 0.0 collective-permute-done.1.from_across
  9.5 0.0 copy-done.4
  9.5 0.0 copy-done.5
  9.5 0.0 copy-done.6
  9.6 0.0 copy-start.1
  9.6 0.0 copy-start.2
  9.6 0.0 copy-start.3
  9.6 2.6 %shard_map.114 = (bf16[8,16,128]{2,1,0:T(8,128)(2,1)S(1)}, f32[8,8,16,128]{3,2,1,0:T(8,128)S(1)}, f32[8,128]{1,0:T(8,128)S(1)}) custom-call(s32[8,24]{1,0:T(8,128)S(1)} %copy-done.4, s32[8,25]{1,0:T(8,128)S(1)} %get-tuple-element.26.order, s32[128]{0:T(128)S(1)} %copy-done.6, f32[8,128]{1,0:T(8,128)S(1)} %get-tuple-element.27.rows, ...), custom_call_target="tpu_custom_call" | custom-call | flops 100663296 | bytes 6291456 | tf_op jit(solution)/shard_map/pallas_call | solution.py:337
  12.2 3.9 %collective-permute-start.2 = (f32[8,128]{1,0:T(8,128)S(1)}, f32[8,128]{1,0:T(8,128)S(1)}, u32[]{:S(2)}, u32[]{:S(2)}) collective-permute-start(f32[8,128]{1,0:T(8,128)S(1)} %get-tuple-element.38), channel_id=1, source_target_pairs={{0,2},{1,3},{2,0},{3,1},{4,6},{5,7},{6,4},{7,5},{8,10},{9,11},{10,... | collective-permute-start | bytes 12296 | tf_op jit(solution)/shard_map/ppermute | solution.py:355
  16.1 1.8 %shard_map.115 = (f32[8,8,16,128]{3,2,1,0:T(8,128)S(1)}, bf16[4,8,16,128]{3,2,1,0:T(8,128)(2,1)S(1)}, bf16[4,8,16,128]{3,2,1,0:T(8,128)(2,1)S(1)}) custom-call(s32[8,24]{1,0:T(8,128)S(1)} %copy-done.4, bf16[8,16,128]{2,1,0:T(8,128)(2,1)S(1)} %get-tuple-element.33.weighted, bf16[8,24,128,128]{3,2,1,0:T(8,128)(2,1)S(1)} %get-tuple-element.31.jac, ...), custom_call_target="tpu_custom_call" | custom-call | flops 100663296 | bytes 6291456 | tf_op jit(solution)/shard_map/pallas_call | solution.py:357
  17.9 0.0 collective-permute-done.2
  17.9 0.1 collective-permute-start.3
  18.0 0.1 collective-permute-start.4
  18.1 11.8 %all_to_all.5.sums = f32[8,8,128]{2,1,0:T(8,128)S(1)} all-to-all(f32[8,8,128]{2,1,0:T(8,128)S(1)} %broadcast_in_dim.2), channel_id=1, replica_groups={{0,1,4,5,8,9,12,13},{2,3,6,7,10,11,14,15},{16,17,20,21,24,25,28,29},{18..., dimensions={0} | all-to-all | bytes 65536 | tf_op jit(solution)/shard_map/all_to_all | solution.py:369
  29.9 0.0 collective-permute-done.3.from_across
  29.9 0.0 collective-permute-done.4.from_within
  29.9 0.0 copy-done.1
  29.9 0.0 copy-done.2
  29.9 0.0 copy-done.3
  29.9 1.2 %shard_map.116 = (f32[8,8,16,128]{3,2,1,0:T(8,128)}, f32[8,8,16,128]{3,2,1,0:T(8,128)}, f32[1,16]{1,0:T(1,128)}) custom-call(f32[8,8,16,128]{3,2,1,0:T(8,128)S(1)} %copy-done.3, f32[8,8,16,128]{3,2,1,0:T(8,128)S(1)} %copy-done.2, f32[8,8,16,128]{3,2,1,0:T(8,128)S(1)} %copy-done.1, f32[8,8,16,128]{3,2,1,0:T(8,128)S(1)} %get-tuple-element.35.image, ...), custom_call_target="tpu_custom_call" | custom-call | flops 1048576 | bytes 3670016 | tf_op jit(solution)/shard_map/pallas_call | solution.py:371
  (3 shorter events, 0.0 us)
Async XLA Ops:
  0.6 1.0 %copy-start = (f32[8,8,16,128]{3,2,1,0:T(8,128)S(1)}, f32[8,8,16,128]{3,2,1,0:T(8,128)}, u32[]{:S(2)}) copy-start(f32[8,8,16,128]{3,2,1,0:T(8,128)} %direction.7) | copy-start | bytes 1572868
  1.7 7.9 %copy-start.4 = (s32[8,24]{1,0:T(8,128)S(1)}, s32[8,24]{1,0:T(8,128)}, u32[]{:S(2)}) copy-start(s32[8,24]{1,0:T(8,128)} %crossing.3) | copy-start | bytes 2308
  1.7 7.9 %copy-start.5 = (f32[8,128]{1,0:T(8,128)S(1)}, f32[8,128]{1,0:T(8,128)}, u32[]{:S(2)}) copy-start(f32[8,128]{1,0:T(8,128)} %smooth.1) | copy-start | bytes 12292
  1.7 7.9 %copy-start.6 = (s32[128]{0:T(128)S(1)}, s32[128]{0:T(128)}, u32[]{:S(2)}) copy-start(s32[128]{0:T(128)} %classes.1) | copy-start | bytes 1540
  1.7 1.4 %collective-permute-start = (bf16[4,8,16,128]{3,2,1,0:T(8,128)(2,1)S(1)}, bf16[4,8,16,128]{3,2,1,0:T(8,128)(2,1)S(1)}, u32[]{:S(2)}, u32[]{:S(2)}) collective-permute-start(bf16[4,8,16,128]{3,2,1,0:T(8,128)(2,1)S(1)} %get-tuple-element.25.within), channel_id=1, source_target_pairs={{0,1},{1,0},{2,3},{3,2},{4,5},{5,4},{6,7},{7,6},{8,9},{9,8},{10,11... | collective-permute-start | bytes 393224 | tf_op jit(solution)/shard_map/ppermute | solution.py:282
  1.8 7.7 %collective-permute-start.1 = (bf16[4,8,16,128]{3,2,1,0:T(8,128)(2,1)S(1)}, bf16[4,8,16,128]{3,2,1,0:T(8,128)(2,1)S(1)}, u32[]{:S(2)}, u32[]{:S(2)}) collective-permute-start(bf16[4,8,16,128]{3,2,1,0:T(8,128)(2,1)S(1)} %get-tuple-element.24.across), channel_id=1, source_target_pairs={{0,15},{1,2},{2,1},{3,4},{4,3},{5,6},{6,5},{7,8},{8,7},{9,10},{10,... | collective-permute-start | bytes 393224 | tf_op jit(solution)/shard_map/ppermute | solution.py:283
  9.6 20.4 %copy-start.1 = (f32[8,8,16,128]{3,2,1,0:T(8,128)S(1)}, f32[8,8,16,128]{3,2,1,0:T(8,128)}, u32[]{:S(2)}) copy-start(f32[8,8,16,128]{3,2,1,0:T(8,128)} %direction.7) | copy-start | bytes 1572868
  9.6 20.4 %copy-start.2 = (f32[8,8,16,128]{3,2,1,0:T(8,128)S(1)}, f32[8,8,16,128]{3,2,1,0:T(8,128)}, u32[]{:S(2)}) copy-start(f32[8,8,16,128]{3,2,1,0:T(8,128)} %residual.1) | copy-start | bytes 1572868
  9.6 20.4 %copy-start.3 = (f32[8,8,16,128]{3,2,1,0:T(8,128)S(1)}, f32[8,8,16,128]{3,2,1,0:T(8,128)}, u32[]{:S(2)}) copy-start(f32[8,8,16,128]{3,2,1,0:T(8,128)} %solution.1) | copy-start | bytes 1572868
  12.2 5.7 %collective-permute-start.2 = (f32[8,128]{1,0:T(8,128)S(1)}, f32[8,128]{1,0:T(8,128)S(1)}, u32[]{:S(2)}, u32[]{:S(2)}) collective-permute-start(f32[8,128]{1,0:T(8,128)S(1)} %get-tuple-element.38), channel_id=1, source_target_pairs={{0,2},{1,3},{2,0},{3,1},{4,6},{5,7},{6,4},{7,5},{8,10},{9,11},{10,... | collective-permute-start | bytes 12296 | tf_op jit(solution)/shard_map/ppermute | solution.py:355
  17.9 12.0 %collective-permute-start.3 = (bf16[4,8,16,128]{3,2,1,0:T(8,128)(2,1)S(1)}, bf16[4,8,16,128]{3,2,1,0:T(8,128)(2,1)S(1)}, u32[]{:S(2)}, u32[]{:S(2)}) collective-permute-start(bf16[4,8,16,128]{3,2,1,0:T(8,128)(2,1)S(1)} %get-tuple-element.39), channel_id=1, source_target_pairs={{0,15},{1,2},{2,1},{3,4},{4,3},{5,6},{6,5},{7,8},{8,7},{9,10},{10,... | collective-permute-start | bytes 393224 | tf_op jit(solution)/shard_map/ppermute | solution.py:283
  18.0 11.9 %collective-permute-start.4 = (bf16[4,8,16,128]{3,2,1,0:T(8,128)(2,1)S(1)}, bf16[4,8,16,128]{3,2,1,0:T(8,128)(2,1)S(1)}, u32[]{:S(2)}, u32[]{:S(2)}) collective-permute-start(bf16[4,8,16,128]{3,2,1,0:T(8,128)(2,1)S(1)} %get-tuple-element.40), channel_id=1, source_target_pairs={{0,1},{1,0},{2,3},{3,2},{4,5},{5,4},{6,7},{7,6},{8,9},{9,8},{10,11... | collective-permute-start | bytes 393224 | tf_op jit(solution)/shard_map/ppermute | solution.py:282

commit v8 on v6

--- a/solution.py
+++ b/solution.py
@@ -30,12 +30,12 @@
     return jnp.where(live_lanes(values.shape), values, 0.0)
 
 
-def call(kernel, out_shape, in_specs, flops, moved, scratch=()):
+def call(kernel, out_shape, in_specs, flops, moved, scratch=(), out_specs=None):
     return pl.pallas_call(
         kernel,
         out_shape=out_shape,
         in_specs=in_specs,
-        out_specs=jax.tree.map(lambda _: VMEM(), out_shape),
+        out_specs=tuple(out_specs or [VMEM()] * len(out_shape)),
         scratch_shapes=list(scratch),
         compiler_params=pltpu.CompilerParams(vmem_limit_bytes=VMEM_LIMIT),
         cost_estimate=pl.CostEstimate(flops=flops, bytes_accessed=moved, transcendentals=0),
@@ -71,12 +71,12 @@
         if c != to and abs(c - to) <= REACH:
             term = table[min(c, to), abs(c - to)] * value
             result = term if result is None else result + term
-    return -result
+    return 0.0 if result is None else -result
 
 
 def inner_kernel(
     direction, count, residual_hbm, classes_hbm, smooth_hbm, sight_hbm, jac_hbm,
-    begun, norm, curved, rows, jac, residual, classes, smooth, sight, sems,
+    begun, faced, norm, curved, rows, jac, residual, classes, smooth, sight, sems,
 ):
     pairs = (
         (classes_hbm, classes), (smooth_hbm, smooth), (sight_hbm, sight),
@@ -101,11 +101,17 @@
         result = weight * (centre * values[c] + pull(table, c, values))
         begun[rim + c] = result
         total = total + jnp.sum(values[c] * result, axis=0)
+    low = {c: values[c] for c in range(rim)}
+    high = {c: values[c] for c in range(rim, cols)}
+    low_rests = {c: rests[c] for c in range(rim)}
+    high_rests = {c: rests[c] for c in range(rim, cols)}
     for q in range(rim):
-        to_left = {c: values[c] if c >= rim else rests[c] for c in range(cols)}
-        to_right = {c: values[c] if c < rim else rests[c] for c in range(cols)}
-        begun[q] = weight * pull(table, q - rim, to_left)
-        begun[rim + cols + q] = weight * pull(table, q + cols, to_right)
+        facing = weight * pull(table, q - rim, high)
+        faced[0, q] = facing
+        begun[q] = facing + weight * pull(table, q - rim, low_rests)
+        facing = weight * pull(table, q + cols, low)
+        faced[1, q] = facing + weight * pull(table, q + cols, high)
+        begun[rim + cols + q] = facing + weight * pull(table, q + cols, high_rests)
     curved[...] = total
     copies[2].wait()
     slot = lax.broadcasted_iota(jnp.int32, rows.shape, 0)
@@ -120,18 +126,20 @@
 
 
 def forward_kernel(
-    crossing, classes, rows, direction, smooth, across, within, from_across, from_within,
-    begun, norm, curved, jac, weighted, own, sums, window,
+    crossing, rows, across, within, from_across, from_within, faced, norm, curved, jac,
+    weighted, sums, window,
 ):
     slots, crossings = crossing.shape
-    cols, species = direction.shape[:2]
-    rim = across.shape[0]
+    rim, species = across.shape[:2]
     span = rim * species
     odd = parity()
     places = (1 + odd, across), (2 - odd, within), (3 * odd, from_across), (3 - 3 * odd, from_within)
     for place, part in places:
         window[pl.ds(place * span, span)] = part[...].reshape(span, *part.shape[2:])
     total = curved[...]
+    for q in range(rim):
+        for side, part in (odd, from_across), (1 - odd, from_within):
+            total = total + 2.0 * jnp.sum(faced[side, q] * part[q].astype(jnp.float32), axis=0)
     for i in range(slots):
         picked = jnp.concatenate([window[crossing[i, j]] for j in range(crossings)], axis=1)
         tiles = jnp.concatenate([jac[i, j] for j in range(crossings)], axis=1)
@@ -142,18 +150,6 @@
         product = (rows[pl.ds(i, 1), :] * integrals).astype(jnp.bfloat16)
         weighted[i] = product
         total = total + product.astype(jnp.float32) * integrals
-    table = coupling(classes, cols, range(-rim, cols))
-    weight = smooth[...][:, None, :]
-    before, after = {}, {}
-    for c in range(rim):
-        before[c - rim] = window[pl.ds(c * species, species)].astype(jnp.float32)
-        after[c + cols] = window[pl.ds(3 * span + c * species, species)].astype(jnp.float32)
-    for c in range(cols):
-        from_before = weight * pull(table, c, before)
-        from_after = weight * pull(table, c, after)
-        own[c] = begun[rim + c] + (from_before + from_after)
-        edges = from_after if c < rim else from_after + from_before
-        total = total + 2.0 * jnp.sum(masked(direction[c]) * edges, axis=0)
     half = sums.shape[0]
     parts = [jnp.sum(x, axis=1, keepdims=True) for x in (norm[...], total)]
     parts = [part[h * half : (h + 1) * half] for h in range(2) for part in parts]
@@ -164,29 +160,38 @@
     sums[...] = block
 
 
-def backward_kernel(crossing, weighted, jac, begun, own, image, across, within, sums):
+def backward_kernel(
+    crossing, classes, smooth, weighted, jac, begun, from_across, from_within,
+    image, across, within, sums, near,
+):
     slots, crossings = crossing.shape
-    cols, species, probes, tile = own.shape
+    cols, species, probes, tile = image.shape
     rim = across.shape[0]
     span = rim * species
-    middle = pl.ds(span, 2 * span)
+    odd = parity()
+    near[odd] = from_across[...].astype(jnp.float32)
+    near[1 - odd] = from_within[...].astype(jnp.float32)
+    table = coupling(classes, cols, range(-rim, cols))
+    weight = smooth[...][:, None, :]
+    beside = {q - rim: near[0, q] for q in range(rim)} | {q + cols: near[1, q] for q in range(rim)}
+    for c in range(cols):
+        place = pl.ds(span + c * species, species)
+        sums[place] = begun[rim + c] + weight * pull(table, c, beside)
     sums[pl.ds(0, span)] = begun[pl.ds(0, rim)].reshape(span, probes, tile)
-    sums[middle] = own[...].reshape(2 * span, probes, tile)
     sums[pl.ds(3 * span, span)] = begun[pl.ds(rim + cols, rim)].reshape(span, probes, tile)
     for i in range(slots):
         tiles = jnp.concatenate([jac[i, j] for j in range(crossings)], axis=1)
         terms = jnp.dot(weighted[i], tiles, preferred_element_type=jnp.float32)
         for j in range(crossings):
             sums[crossing[i, j]] += terms[:, j * tile : (j + 1) * tile]
-    odd = parity()
     for part, place in (across, 3 * odd), (within, 3 - 3 * odd):
         part[...] = sums[pl.ds(place * span, span)].astype(part.dtype).reshape(part.shape)
-    image[...] = sums[middle].reshape(image.shape)
+    image[...] = sums[pl.ds(span, 2 * span)].reshape(image.shape)
 
 
 def final_kernel(
     solution, residual, direction, image, from_across, from_within, sums,
-    solution_next, residual_next, step_length,
+    solution_next, residual_next, step_length, made, sems,
 ):
     whole = jnp.sum(sums[...], axis=0)
     norm = jnp.concatenate([whole[:, 0:1], whole[:, 2:3]], axis=0)
@@ -197,11 +202,18 @@
     step_length[...] = jnp.transpose(wide)[0:1]
     wide = wide[None]
     odd = parity()
+    copies = []
     for q in range(rim):
         for c, part in (odd * rim + q, from_across), ((1 - odd) * rim + q, from_within):
-            total = masked(image[c] + part[q].astype(jnp.float32))
-            solution_next[c] = masked(solution[c] + wide * direction[c])
-            residual_next[c] = masked(residual[c]) - wide * total
+            k = len(copies) // 2
+            made[0, k] = masked(solution[c] + wide * direction[c])
+            made[1, k] = masked(residual[c]) - wide * masked(image[c] + part[q].astype(jnp.float32))
+            for half, out in enumerate((solution_next, residual_next)):
+                copy = pltpu.make_async_copy(made.at[half, k], out.at[c], sems.at[half, k])
+                copy.start()
+                copies.append(copy)
+    for copy in copies:
+        copy.wait()
 
 
 def swapped(across, within):
@@ -234,10 +246,10 @@
     )(direction)
     from_across, from_within = swapped(across, within)
 
-    begun, norm, curved, rows, jac = call(
+    begun, faced, norm, curved, rows, jac = call(
         inner_kernel,
         (
-            shape((2 * cols,) + column, f32), small, small,
+            shape((2 * cols,) + column, f32), shape((2, rim) + column, f32), small, small,
             shape(sightline_weight.shape, f32), shape(jacobian.shape, bf16),
         ),
         [VMEM(), SMEM()] + [HBM()] * 5,
@@ -257,31 +269,28 @@
 
     devices = lax.axis_size("orbit")
     peers = devices // 2
-    weighted, own, sums = call(
+    weighted, sums = call(
         forward_kernel,
-        (
-            shape((slots, probes, width), bf16), whole,
-            shape((probes // 2, width), f32),
-        ),
-        [SMEM()] * 2 + [VMEM()] * 11,
+        (shape((slots, probes, width), bf16), shape((probes // 2, width), f32)),
+        [SMEM()] + [VMEM()] * 9,
         dot_flops,
         2 * jacobian.size,
         [pltpu.VMEM((2 * cols * species, probes, width), bf16)],
-    )(
-        crossing, length_class, rows, direction, smooth_weight,
-        across, within, from_across, from_within, begun, norm, curved, jac,
-    )
+    )(crossing, rows, across, within, from_across, from_within, faced, norm, curved, jac)
     assert devices % 4 == 0
     twin = lax.ppermute(sums, "orbit", [(i, i ^ 2) for i in range(devices)])
 
     image, across, within = call(
         backward_kernel,
         (whole, near, near),
-        [SMEM()] + [VMEM()] * 4,
+        [SMEM()] * 2 + [VMEM()] * 6,
         dot_flops,
         2 * jacobian.size,
-        [pltpu.VMEM((2 * cols * species, probes, width), f32)],
-    )(crossing, weighted, jac, begun, own)
+        [
+            pltpu.VMEM((2 * cols * species, probes, width), f32),
+            pltpu.VMEM((2, rim) + column, f32),
+        ],
+    )(crossing, length_class, smooth_weight, weighted, jac, begun, from_across, from_within)
     across, within, twin = lax.optimization_barrier((across, within, twin))
     from_across, from_within = swapped(across, within)
     alike = [[i for i in range(devices) if i & 2 == side] for side in (0, 2)]
@@ -294,6 +303,8 @@
         [VMEM()] * 7,
         8 * elements,
         28 * elements,
+        [pltpu.VMEM((2,) + direction.shape, f32), pltpu.SemaphoreType.DMA((2, cols))],
+        [HBM()] * 2 + [VMEM()],
     )(solution, residual, direction, image, from_across, from_within, sums)
     return solution_next, residual_next, step_length.reshape(probes)
 

time: 29.3 us -> 29.6 us (1.010)
  Pallas kernels: 8.95 us -> 9.52 us
  waiting for transfers between devices: 1.81 us -> 1.46 us
    pallas_call x1, Pallas kernels: 1.24 us -> 1.83 us  [local(): call(final_kernel, (whole, whole, shape((1, probes), f32)), [VMEM()] * 7,...]
    ppermute x1, waiting for transfers between devices: 1.8 us -> 1.45 us  [local(): twin = lax.ppermute(sums, 'orbit', [(i, i ^ 2) for i in range(devices)])]
  transfers between devices with their start and end apart: 5 -> 5, of which waited for: 1 -> 1; matrix products, arithmetic and copies ran while one was open for 0% -> 0% of each run, Pallas kernels for 17% -> 18%
where the time goes in v8:
time: 29.6 us; the launch traced here: 29.3 us
  Pallas kernels  9.52 us (32%)
  blocking collectives  8.11 us (27%)
  starting transfers between devices  7.75 us (26%)
  waiting for transfers between devices  1.46 us (5%)
  between operations  1.42 us (5%)
  local copies, waits for them, and re-layouts  1.08 us (4%)
    all_to_all x1, blocking collectives, local(): sums = lax.all_to_all(sums, 'orbit', 0, 0, axis_index_groups=alike)  8.11 us
    ppermute x2, starting transfers between devices, swapped(): lax.ppermute(across, 'orbit', outer)  7.69 us
    pallas_call x1, Pallas kernels, local(): call(inner_kernel, (shape((2 * cols,) + column, f32), shape((2, rim) + co...  3.05 us
    pallas_call x1, Pallas kernels, local(): call(forward_kernel, (shape((slots, probes, width), bf16), shape((probes...  2.48 us
    pallas_call x1, Pallas kernels, local(): call(backward_kernel, (whole, near, near), [SMEM()] * 2 + [VMEM()] * 6, d...  2.13 us
    pallas_call x1, Pallas kernels, local(): call(final_kernel, (whole, whole, shape((1, probes), f32)), [VMEM()] * 7,...  1.83 us
    ppermute x1, waiting for transfers between devices, local(): twin = lax.ppermute(sums, 'orbit', [(i, i ^ 2) for i in range(devices)])  1.45 us
    unnamed x14, local copies, waits for them, and re-layouts  1.07 us
  transfers between devices with their start and end apart: 5, of which 1 were waited for; matrix products, arithmetic and copies ran while one was open for 0% of the time, Pallas kernels for 18%

profile of v8, /device:TPU:0, one launch (start us, length us, event | category | flops | bytes accessed | tf_op | source)
XLA Modules:
  0.0 29.3 jit_solution(18107285218319275665)
XLA Ops:
  0.6 0.0 copy-start
  0.6 1.0 %copy-done = f32[8,8,16,128]{3,2,1,0:T(8,128)S(1)} copy-done((f32[8,8,16,128]{3,2,1,0:T(8,128)S(1)}, f32[8,8,16,128]{3,2,1,0:T(8,128)}, u32[]{:S(2)}) %copy-start) | copy-done | bytes 524312
  1.7 0.0 copy-start.4
  1.7 5.5 %collective-permute-start = (bf16[4,8,16,128]{3,2,1,0:T(8,128)(2,1)S(1)}, bf16[4,8,16,128]{3,2,1,0:T(8,128)(2,1)S(1)}, u32[]{:S(2)}, u32[]{:S(2)}) collective-permute-start(bf16[4,8,16,128]{3,2,1,0:T(8,128)(2,1)S(1)} %get-tuple-element.23.across), channel_id=1, source_target_pairs={{0,15},{1,2},{2,1},{3,4},{4,3},{5,6},{6,5},{7,8},{8,7},{9,10},{10,... | collective-permute-start | bytes 393224 | tf_op jit(solution)/shard_map/ppermute | solution.py:224
  7.2 0.0 collective-permute-start.1
  7.9 0.0 copy-start.5
  7.9 0.0 copy-start.6
  7.9 3.0 %shard_map.112 = (f32[16,8,16,128]{3,2,1,0:T(8,128)S(1)}, f32[2,4,8,16,128]{4,3,2,1,0:T(8,128)S(1)}, f32[16,128]{1,0:T(8,128)S(1)}, f32[16,128]{1,0:T(8,128)S(1)...) custom-call(f32[8,8,16,128]{3,2,1,0:T(8,128)S(1)} %copy-done, s32[1]{0:T(128)S(6)} %copy.12.count, ...), custom_call_target="tpu_custom_call" | custom-call | flops 7864320 | bytes 12582912 | tf_op jit(solution)/shard_map/pallas_call | solution.py:249
  11.0 0.0 collective-permute-done.from_across
  11.0 0.0 collective-permute-done.1.from_within
  11.0 0.0 copy-done.4
  11.0 0.0 copy-start.1
  11.0 0.0 copy-start.2
  11.0 0.0 copy-start.3
  11.0 2.5 %shard_map.114 = (bf16[8,16,128]{2,1,0:T(8,128)(2,1)S(1)}, f32[8,128]{1,0:T(8,128)S(1)}) custom-call(s32[8,24]{1,0:T(8,128)S(1)} %copy-done.4, f32[8,128]{1,0:T(8,128)S(1)} %get-tuple-element.22.rows, bf16[4,8,16,128]{3,2,1,0:T(8,128)(2,1)S(1)} %get-tuple-element.23.across, bf16[4,8,16,128]{3,2,1,0:T(8,128)(2,1)S(1)} %get-tuple-element.24.within, ...), custom_call_target="tpu_custom_call" | custom-call | flops 100663296 | bytes 6291456 | tf_op jit(solution)/shard_map/pallas_call | solution.py:272
  13.5 0.1 collective-permute-start.2
  13.6 0.0 copy-done.5
  13.6 0.0 copy-done.6
  13.6 2.1 %shard_map.115 = (f32[8,8,16,128]{3,2,1,0:T(8,128)S(1)}, bf16[4,8,16,128]{3,2,1,0:T(8,128)(2,1)S(1)}, bf16[4,8,16,128]{3,2,1,0:T(8,128)(2,1)S(1)}) custom-call(s32[8,24]{1,0:T(8,128)S(1)} %copy-done.4, s32[128]{0:T(128)S(1)} %copy-done.6, f32[8,128]{1,0:T(8,128)S(1)} %copy-done.5, bf16[8,16,128]{2,1,0:T(8,128)(2,1)S(1)} %get-tuple-element.29.weighted, ...), custom_call_target="tpu_custom_call" | custom-call | flops 100663296 | bytes 6291456 | tf_op jit(solution)/shard_map/pallas_call | solution.py:283
  15.7 1.4 %collective-permute-done.2 = f32[8,128]{1,0:T(8,128)S(1)} collective-permute-done((f32[8,128]{1,0:T(8,128)S(1)}, f32[8,128]{1,0:T(8,128)S(1)}, u32[]{:S(2)}, u32[]{:S(2)}) %collective-permute-start.2) | collective-permute-done | bytes 4128 | tf_op jit(solution)/shard_map/ppermute | solution.py:281
  17.2 2.2 %collective-permute-start.3 = (bf16[4,8,16,128]{3,2,1,0:T(8,128)(2,1)S(1)}, bf16[4,8,16,128]{3,2,1,0:T(8,128)(2,1)S(1)}, u32[]{:S(2)}, u32[]{:S(2)}) collective-permute-start(bf16[4,8,16,128]{3,2,1,0:T(8,128)(2,1)S(1)} %get-tuple-element.35), channel_id=1, source_target_pairs={{0,15},{1,2},{2,1},{3,4},{4,3},{5,6},{6,5},{7,8},{8,7},{9,10},{10,... | collective-permute-start | bytes 393224 | tf_op jit(solution)/shard_map/ppermute | solution.py:224
  19.3 0.0 collective-permute-start.4
  19.4 8.1 %all_to_all.5.sums = f32[8,8,128]{2,1,0:T(8,128)S(1)} all-to-all(f32[8,8,128]{2,1,0:T(8,128)S(1)} %broadcast_in_dim.2), channel_id=1, replica_groups={{0,1,4,5,8,9,12,13},{2,3,6,7,10,11,14,15},{16,17,20,21,24,25,28,29},{18..., dimensions={0} | all-to-all | bytes 65536 | tf_op jit(solution)/shard_map/all_to_all | solution.py:298
  27.5 0.0 collective-permute-done.3.from_across
  27.5 0.0 collective-permute-done.4.from_within
  27.5 0.0 copy-done.1
  27.5 0.0 copy-done.2
  27.5 0.0 copy-done.3
  27.5 1.8 %shard_map.116 = (f32[8,8,16,128]{3,2,1,0:T(8,128)}, f32[8,8,16,128]{3,2,1,0:T(8,128)}, f32[1,16]{1,0:T(1,128)}) custom-call(f32[8,8,16,128]{3,2,1,0:T(8,128)S(1)} %copy-done.3, f32[8,8,16,128]{3,2,1,0:T(8,128)S(1)} %copy-done.2, f32[8,8,16,128]{3,2,1,0:T(8,128)S(1)} %copy-done.1, f32[8,8,16,128]{3,2,1,0:T(8,128)S(1)} %get-tuple-element.31.image, ...), custom_call_target="tpu_custom_call" | custom-call | flops 1048576 | bytes 3670016 | tf_op jit(solution)/shard_map/pallas_call | solution.py:300
  (3 shorter events, 0.0 us)
Async XLA Ops:
  0.6 1.0 %copy-start = (f32[8,8,16,128]{3,2,1,0:T(8,128)S(1)}, f32[8,8,16,128]{3,2,1,0:T(8,128)}, u32[]{:S(2)}) copy-start(f32[8,8,16,128]{3,2,1,0:T(8,128)} %direction.5) | copy-start | bytes 1572868
  1.7 9.3 %copy-start.4 = (s32[8,24]{1,0:T(8,128)S(1)}, s32[8,24]{1,0:T(8,128)}, u32[]{:S(2)}) copy-start(s32[8,24]{1,0:T(8,128)} %crossing.3) | copy-start | bytes 2308
  1.7 9.2 %collective-permute-start = (bf16[4,8,16,128]{3,2,1,0:T(8,128)(2,1)S(1)}, bf16[4,8,16,128]{3,2,1,0:T(8,128)(2,1)S(1)}, u32[]{:S(2)}, u32[]{:S(2)}) collective-permute-start(bf16[4,8,16,128]{3,2,1,0:T(8,128)(2,1)S(1)} %get-tuple-element.23.across), channel_id=1, source_target_pairs={{0,15},{1,2},{2,1},{3,4},{4,3},{5,6},{6,5},{7,8},{8,7},{9,10},{10,... | collective-permute-start | bytes 393224 | tf_op jit(solution)/shard_map/ppermute | solution.py:224
  7.2 3.7 %collective-permute-start.1 = (bf16[4,8,16,128]{3,2,1,0:T(8,128)(2,1)S(1)}, bf16[4,8,16,128]{3,2,1,0:T(8,128)(2,1)S(1)}, u32[]{:S(2)}, u32[]{:S(2)}) collective-permute-start(bf16[4,8,16,128]{3,2,1,0:T(8,128)(2,1)S(1)} %get-tuple-element.24.within), channel_id=1, source_target_pairs={{0,1},{1,0},{2,3},{3,2},{4,5},{5,4},{6,7},{7,6},{8,9},{9,8},{10,11... | collective-permute-start | bytes 393224 | tf_op jit(solution)/shard_map/ppermute | solution.py:224
  7.9 5.7 %copy-start.5 = (f32[8,128]{1,0:T(8,128)S(1)}, f32[8,128]{1,0:T(8,128)}, u32[]{:S(2)}) copy-start(f32[8,128]{1,0:T(8,128)} %smooth.1) | copy-start | bytes 12292
  7.9 5.7 %copy-start.6 = (s32[128]{0:T(128)S(1)}, s32[128]{0:T(128)}, u32[]{:S(2)}) copy-start(s32[128]{0:T(128)} %classes.1) | copy-start | bytes 1540
  11.0 16.5 %copy-start.1 = (f32[8,8,16,128]{3,2,1,0:T(8,128)S(1)}, f32[8,8,16,128]{3,2,1,0:T(8,128)}, u32[]{:S(2)}) copy-start(f32[8,8,16,128]{3,2,1,0:T(8,128)} %direction.5) | copy-start | bytes 1572868
  11.0 16.5 %copy-start.2 = (f32[8,8,16,128]{3,2,1,0:T(8,128)S(1)}, f32[8,8,16,128]{3,2,1,0:T(8,128)}, u32[]{:S(2)}) copy-start(f32[8,8,16,128]{3,2,1,0:T(8,128)} %residual.1) | copy-start | bytes 1572868
  11.0 16.5 %copy-start.3 = (f32[8,8,16,128]{3,2,1,0:T(8,128)S(1)}, f32[8,8,16,128]{3,2,1,0:T(8,128)}, u32[]{:S(2)}) copy-start(f32[8,8,16,128]{3,2,1,0:T(8,128)} %solution.1) | copy-start | bytes 1572868
  13.5 3.7 %collective-permute-start.2 = (f32[8,128]{1,0:T(8,128)S(1)}, f32[8,128]{1,0:T(8,128)S(1)}, u32[]{:S(2)}, u32[]{:S(2)}) collective-permute-start(f32[8,128]{1,0:T(8,128)S(1)} %get-tuple-element.34), channel_id=1, source_target_pairs={{0,2},{1,3},{2,0},{3,1},{4,6},{5,7},{6,4},{7,5},{8,10},{9,11},{10,... | collective-permute-start | bytes 12296 | tf_op jit(solution)/shard_map/ppermute | solution.py:281
  17.2 10.3 %collective-permute-start.3 = (bf16[4,8,16,128]{3,2,1,0:T(8,128)(2,1)S(1)}, bf16[4,8,16,128]{3,2,1,0:T(8,128)(2,1)S(1)}, u32[]{:S(2)}, u32[]{:S(2)}) collective-permute-start(bf16[4,8,16,128]{3,2,1,0:T(8,128)(2,1)S(1)} %get-tuple-element.35), channel_id=1, source_target_pairs={{0,15},{1,2},{2,1},{3,4},{4,3},{5,6},{6,5},{7,8},{8,7},{9,10},{10,... | collective-permute-start | bytes 393224 | tf_op jit(solution)/shard_map/ppermute | solution.py:224
  19.3 8.1 %collective-permute-start.4 = (bf16[4,8,16,128]{3,2,1,0:T(8,128)(2,1)S(1)}, bf16[4,8,16,128]{3,2,1,0:T(8,128)(2,1)S(1)}, u32[]{:S(2)}, u32[]{:S(2)}) collective-permute-start(bf16[4,8,16,128]{3,2,1,0:T(8,128)(2,1)S(1)} %get-tuple-element.36), channel_id=1, source_target_pairs={{0,1},{1,0},{2,3},{3,2},{4,5},{5,4},{6,7},{7,6},{8,9},{9,8},{10,11... | collective-permute-start | bytes 393224 | tf_op jit(solution)/shard_map/ppermute | solution.py:224

commit v9 on v8

--- a/solution.py
+++ b/solution.py
@@ -75,12 +75,12 @@
 
 
 def inner_kernel(
-    direction, count, residual_hbm, classes_hbm, smooth_hbm, sight_hbm, jac_hbm,
-    begun, faced, norm, curved, rows, jac, residual, classes, smooth, sight, sems,
+    direction, count, residual_hbm, classes_hbm, smooth_hbm, sight_hbm, crossing_hbm, jac_hbm,
+    begun, faced, norm, curved, rows, jac, crossing, classes, residual, smooth, sight, sems,
 ):
     pairs = (
         (classes_hbm, classes), (smooth_hbm, smooth), (sight_hbm, sight),
-        (residual_hbm, residual), (jac_hbm, jac),
+        (residual_hbm, residual), (crossing_hbm, crossing), (jac_hbm, jac),
     )
     copies = [pltpu.make_async_copy(*pair, sems.at[i]) for i, pair in enumerate(pairs)]
     for copy in copies:
@@ -123,6 +123,7 @@
         squares = squares + jnp.sum(mres * mres, axis=0)
     norm[...] = squares
     copies[4].wait()
+    copies[5].wait()
 
 
 def forward_kernel(
@@ -191,7 +192,7 @@
 
 def final_kernel(
     solution, residual, direction, image, from_across, from_within, sums,
-    solution_next, residual_next, step_length, made, sems,
+    solution_next, residual_next, step_length,
 ):
     whole = jnp.sum(sums[...], axis=0)
     norm = jnp.concatenate([whole[:, 0:1], whole[:, 2:3]], axis=0)
@@ -202,18 +203,11 @@
     step_length[...] = jnp.transpose(wide)[0:1]
     wide = wide[None]
     odd = parity()
-    copies = []
     for q in range(rim):
         for c, part in (odd * rim + q, from_across), ((1 - odd) * rim + q, from_within):
-            k = len(copies) // 2
-            made[0, k] = masked(solution[c] + wide * direction[c])
-            made[1, k] = masked(residual[c]) - wide * masked(image[c] + part[q].astype(jnp.float32))
-            for half, out in enumerate((solution_next, residual_next)):
-                copy = pltpu.make_async_copy(made.at[half, k], out.at[c], sems.at[half, k])
-                copy.start()
-                copies.append(copy)
-    for copy in copies:
-        copy.wait()
+            total = masked(image[c] + part[q].astype(jnp.float32))
+            solution_next[c] = masked(solution[c] + wide * direction[c])
+            residual_next[c] = masked(residual[c]) - wide * total
 
 
 def swapped(across, within):
@@ -246,25 +240,28 @@
     )(direction)
     from_across, from_within = swapped(across, within)
 
-    begun, faced, norm, curved, rows, jac = call(
+    begun, faced, norm, curved, rows, jac, crossing, length_class = call(
         inner_kernel,
         (
             shape((2 * cols,) + column, f32), shape((2, rim) + column, f32), small, small,
             shape(sightline_weight.shape, f32), shape(jacobian.shape, bf16),
+            pltpu.SMEM(crossing.shape, jnp.int32), pltpu.SMEM(length_class.shape, jnp.int32),
         ),
-        [VMEM(), SMEM()] + [HBM()] * 5,
+        [VMEM(), SMEM()] + [HBM()] * 6,
         60 * elements,
         4 * jacobian.size,
         [
             pltpu.VMEM(direction.shape, f32),
-            pltpu.SMEM(length_class.shape, jnp.int32),
             pltpu.VMEM(smooth_weight.shape, f32),
             pltpu.VMEM(sightline_weight.shape, f32),
-            pltpu.SemaphoreType.DMA((5,)),
+            pltpu.SemaphoreType.DMA((6,)),
         ],
+        [VMEM()] * 6 + [SMEM()] * 2,
     )(
         direction, tile_count,
-        *map(in_hbm, (residual, length_class, smooth_weight, sightline_weight, jacobian)),
+        *map(in_hbm, (
+            residual, length_class, smooth_weight, sightline_weight, crossing, jacobian,
+        )),
     )
 
     devices = lax.axis_size("orbit")
@@ -291,7 +288,7 @@
             pltpu.VMEM((2, rim) + column, f32),
         ],
     )(crossing, length_class, smooth_weight, weighted, jac, begun, from_across, from_within)
-    across, within, twin = lax.optimization_barrier((across, within, twin))
+    within, twin = lax.optimization_barrier((within, twin))
     from_across, from_within = swapped(across, within)
     alike = [[i for i in range(devices) if i & 2 == side] for side in (0, 2)]
     sums = jnp.broadcast_to((sums + twin)[None], (peers,) + sums.shape)
@@ -303,8 +300,6 @@
         [VMEM()] * 7,
         8 * elements,
         28 * elements,
-        [pltpu.VMEM((2,) + direction.shape, f32), pltpu.SemaphoreType.DMA((2, cols))],
-        [HBM()] * 2 + [VMEM()],
     )(solution, residual, direction, image, from_across, from_within, sums)
     return solution_next, residual_next, step_length.reshape(probes)
 

time: 29.6 us -> 27.5 us (0.929)
  Pallas kernels: 9.52 us -> 7.73 us
  waiting for transfers between devices: 1.46 us -> 0.01 us
  starting transfers between devices: 7.75 us -> 8.95 us
    ppermute x1, waiting for transfers between devices: 1.45 us -> 0.01 us  [local(): twin = lax.ppermute(sums, 'orbit', [(i, i ^ 2) for i in range(devices)])]
    ppermute x2, starting transfers between devices: 7.69 us -> 8.9 us  [swapped(): lax.ppermute(across, 'orbit', outer)]
    pallas_call x1, Pallas kernels: 2.13 us -> 1.52 us  [local(): call(backward_kernel, (whole, near, near), [SMEM()] * 2 + [VMEM()] * 6, d...]
    pallas_call x1, Pallas kernels: 2.48 us -> 1.88 us  [local(): call(forward_kernel, (shape((slots, probes, width), bf16), shape((probes...]
    pallas_call x1, Pallas kernels: 1.83 us -> 1.24 us  [local(): call(final_kernel, (whole, whole, shape((1, probes), f32)), [VMEM()] * 7,...]
    unnamed x14 -> x10, local copies, waits for them, and re-layouts: 1.07 us -> 1.06 us
  transfers between devices with their start and end apart: 5 -> 5, of which waited for: 1 -> 0; matrix products, arithmetic and copies ran while one was open for 0% -> 0% of each run, Pallas kernels for 18% -> 17%
where the time goes in v9:
time: 27.5 us; the launch traced here: 27.3 us
  starting transfers between devices  8.95 us (33%)
  blocking collectives  8.12 us (30%)
  Pallas kernels  7.73 us (28%)
  between operations  1.41 us (5%)
  local copies, waits for them, and re-layouts  1.07 us (4%)
    ppermute x2, starting transfers between devices, swapped(): lax.ppermute(across, 'orbit', outer)  8.9 us
    all_to_all x1, blocking collectives, local(): sums = lax.all_to_all(sums, 'orbit', 0, 0, axis_index_groups=alike)  8.12 us
    pallas_call x1, Pallas kernels, local(): call(inner_kernel, (shape((2 * cols,) + column, f32), shape((2, rim) + co...  3.06 us
    pallas_call x1, Pallas kernels, local(): call(forward_kernel, (shape((slots, probes, width), bf16), shape((probes...  1.88 us
    pallas_call x1, Pallas kernels, local(): call(backward_kernel, (whole, near, near), [SMEM()] * 2 + [VMEM()] * 6, d...  1.52 us
    pallas_call x1, Pallas kernels, local(): call(final_kernel, (whole, whole, shape((1, probes), f32)), [VMEM()] * 7,...  1.24 us
    unnamed x10, local copies, waits for them, and re-layouts  1.06 us
  transfers between devices with their start and end apart: 5, of which 0 were waited for; matrix products, arithmetic and copies ran while one was open for 0% of the time, Pallas kernels for 17%

profile of v9, /device:TPU:0, one launch (start us, length us, event | category | flops | bytes accessed | tf_op | source)
XLA Modules:
  0.0 27.3 jit_solution(3115773833528378987)
XLA Ops:
  0.6 0.0 copy-start
  0.6 1.0 %copy-done = f32[8,8,16,128]{3,2,1,0:T(8,128)S(1)} copy-done((f32[8,8,16,128]{3,2,1,0:T(8,128)S(1)}, f32[8,8,16,128]{3,2,1,0:T(8,128)}, u32[]{:S(2)}) %copy-start) | copy-done | bytes 524312
  1.7 5.5 %collective-permute-start = (bf16[4,8,16,128]{3,2,1,0:T(8,128)(2,1)S(1)}, bf16[4,8,16,128]{3,2,1,0:T(8,128)(2,1)S(1)}, u32[]{:S(2)}, u32[]{:S(2)}) collective-permute-start(bf16[4,8,16,128]{3,2,1,0:T(8,128)(2,1)S(1)} %get-tuple-element.26.across), channel_id=1, source_target_pairs={{0,15},{1,2},{2,1},{3,4},{4,3},{5,6},{6,5},{7,8},{8,7},{9,10},{10,... | collective-permute-start | bytes 393224 | tf_op jit(solution)/shard_map/ppermute | solution.py:218
  7.2 0.0 collective-permute-start.1
  7.9 0.0 copy-start.4
  7.9 3.1 %shard_map.112 = (f32[16,8,16,128]{3,2,1,0:T(8,128)S(1)}, f32[2,4,8,16,128]{4,3,2,1,0:T(8,128)S(1)}, f32[16,128]{1,0:T(8,128)S(1)}, f32[16,128]{1,0:T(8,128)S(1)...) custom-call(f32[8,8,16,128]{3,2,1,0:T(8,128)S(1)} %copy-done, ...), custom_call_target="tpu_custom_call" | custom-call | flops 7864320 | bytes 12582912 | tf_op jit(solution)/shard_map/pallas_call | solution.py:243
  11.0 0.0 collective-permute-done.from_across
  11.0 0.0 collective-permute-done.1.from_within
  11.0 0.0 copy-start.1
  11.0 0.0 copy-start.2
  11.0 0.0 copy-start.3
  11.0 1.9 %shard_map.114 = (bf16[8,16,128]{2,1,0:T(8,128)(2,1)S(1)}, f32[8,128]{1,0:T(8,128)S(1)}) custom-call(s32[8,24]{1,0:T(8,128)S(4)} %get-tuple-element.23.crossing, f32[8,128]{1,0:T(8,128)S(1)} %get-tuple-element.25.rows, bf16[4,8,16,128]{3,2,1,0:T(8,128)(2,1)S(1)} %get-tuple-element.26.across, bf16[4,8,16,128]{3,2,1,0:T(8,128)(2,1)S(1)} %get-tuple-element.27.within, ...), custom_call_target="tpu_custom_call" | custom-call | flops 100663296 | bytes 6291456 | tf_op jit(solution)/shard_map/pallas_call | solution.py:269
  12.9 0.1 collective-permute-start.3
  13.0 0.0 copy-done.4
  13.0 1.5 %shard_map.115 = (f32[8,8,16,128]{3,2,1,0:T(8,128)S(1)}, bf16[4,8,16,128]{3,2,1,0:T(8,128)(2,1)S(1)}, bf16[4,8,16,128]{3,2,1,0:T(8,128)(2,1)S(1)}) custom-call(s32[8,24]{1,0:T(8,128)S(4)} %get-tuple-element.23.crossing, s32[128]{0:T(128)S(4)} %get-tuple-element.24.classes, f32[8,128]{1,0:T(8,128)S(1)} %copy-done.4, ...), custom_call_target="tpu_custom_call" | custom-call | flops 100663296 | bytes 6291456 | tf_op jit(solution)/shard_map/pallas_call | solution.py:280
  14.5 3.4 %collective-permute-start.2 = (bf16[4,8,16,128]{3,2,1,0:T(8,128)(2,1)S(1)}, bf16[4,8,16,128]{3,2,1,0:T(8,128)(2,1)S(1)}, u32[]{:S(2)}, u32[]{:S(2)}) collective-permute-start(bf16[4,8,16,128]{3,2,1,0:T(8,128)(2,1)S(1)} %get-tuple-element.35), channel_id=1, source_target_pairs={{0,15},{1,2},{2,1},{3,4},{4,3},{5,6},{6,5},{7,8},{8,7},{9,10},{10,... | collective-permute-start | bytes 393224 | tf_op jit(solution)/shard_map/ppermute | solution.py:218
  17.9 0.0 collective-permute-done.3
  17.9 0.0 collective-permute-start.4
  17.9 8.1 %all_to_all.5.sums = f32[8,8,128]{2,1,0:T(8,128)S(1)} all-to-all(f32[8,8,128]{2,1,0:T(8,128)S(1)} %broadcast_in_dim.2), channel_id=1, replica_groups={{0,1,4,5,8,9,12,13},{2,3,6,7,10,11,14,15},{16,17,20,21,24,25,28,29},{18..., dimensions={0} | all-to-all | bytes 65536 | tf_op jit(solution)/shard_map/all_to_all | solution.py:295
  26.0 0.0 collective-permute-done.2.from_across
  26.0 0.0 collective-permute-done.4.from_within
  26.0 0.0 copy-done.1
  26.0 0.0 copy-done.2
  26.0 0.0 copy-done.3
  26.0 1.2 %shard_map.116 = (f32[8,8,16,128]{3,2,1,0:T(8,128)}, f32[8,8,16,128]{3,2,1,0:T(8,128)}, f32[1,16]{1,0:T(1,128)}) custom-call(f32[8,8,16,128]{3,2,1,0:T(8,128)S(1)} %copy-done.3, f32[8,8,16,128]{3,2,1,0:T(8,128)S(1)} %copy-done.2, f32[8,8,16,128]{3,2,1,0:T(8,128)S(1)} %copy-done.1, f32[8,8,16,128]{3,2,1,0:T(8,128)S(1)} %get-tuple-element.34.image, ...), custom_call_target="tpu_custom_call" | custom-call | flops 1048576 | bytes 3670016 | tf_op jit(solution)/shard_map/pallas_call | solution.py:297
  (3 shorter events, 0.0 us)
Async XLA Ops:
  0.6 1.0 %copy-start = (f32[8,8,16,128]{3,2,1,0:T(8,128)S(1)}, f32[8,8,16,128]{3,2,1,0:T(8,128)}, u32[]{:S(2)}) copy-start(f32[8,8,16,128]{3,2,1,0:T(8,128)} %direction.5) | copy-start | bytes 1572868
  1.7 9.2 %collective-permute-start = (bf16[4,8,16,128]{3,2,1,0:T(8,128)(2,1)S(1)}, bf16[4,8,16,128]{3,2,1,0:T(8,128)(2,1)S(1)}, u32[]{:S(2)}, u32[]{:S(2)}) collective-permute-start(bf16[4,8,16,128]{3,2,1,0:T(8,128)(2,1)S(1)} %get-tuple-element.26.across), channel_id=1, source_target_pairs={{0,15},{1,2},{2,1},{3,4},{4,3},{5,6},{6,5},{7,8},{8,7},{9,10},{10,... | collective-permute-start | bytes 393224 | tf_op jit(solution)/shard_map/ppermute | solution.py:218
  7.2 3.7 %collective-permute-start.1 = (bf16[4,8,16,128]{3,2,1,0:T(8,128)(2,1)S(1)}, bf16[4,8,16,128]{3,2,1,0:T(8,128)(2,1)S(1)}, u32[]{:S(2)}, u32[]{:S(2)}) collective-permute-start(bf16[4,8,16,128]{3,2,1,0:T(8,128)(2,1)S(1)} %get-tuple-element.27.within), channel_id=1, source_target_pairs={{0,1},{1,0},{2,3},{3,2},{4,5},{5,4},{6,7},{7,6},{8,9},{9,8},{10,11... | collective-permute-start | bytes 393224 | tf_op jit(solution)/shard_map/ppermute | solution.py:218
  7.9 5.1 %copy-start.4 = (f32[8,128]{1,0:T(8,128)S(1)}, f32[8,128]{1,0:T(8,128)}, u32[]{:S(2)}) copy-start(f32[8,128]{1,0:T(8,128)} %smooth.1) | copy-start | bytes 12292
  11.0 15.1 %copy-start.1 = (f32[8,8,16,128]{3,2,1,0:T(8,128)S(1)}, f32[8,8,16,128]{3,2,1,0:T(8,128)}, u32[]{:S(2)}) copy-start(f32[8,8,16,128]{3,2,1,0:T(8,128)} %direction.5) | copy-start | bytes 1572868
  11.0 15.0 %copy-start.2 = (f32[8,8,16,128]{3,2,1,0:T(8,128)S(1)}, f32[8,8,16,128]{3,2,1,0:T(8,128)}, u32[]{:S(2)}) copy-start(f32[8,8,16,128]{3,2,1,0:T(8,128)} %residual.1) | copy-start | bytes 1572868
  11.0 15.0 %copy-start.3 = (f32[8,8,16,128]{3,2,1,0:T(8,128)S(1)}, f32[8,8,16,128]{3,2,1,0:T(8,128)}, u32[]{:S(2)}) copy-start(f32[8,8,16,128]{3,2,1,0:T(8,128)} %solution.1) | copy-start | bytes 1572868
  12.9 5.0 %collective-permute-start.3 = (f32[8,128]{1,0:T(8,128)S(1)}, f32[8,128]{1,0:T(8,128)S(1)}, u32[]{:S(2)}, u32[]{:S(2)}) collective-permute-start(f32[8,128]{1,0:T(8,128)S(1)} %get-tuple-element.37), channel_id=1, source_target_pairs={{0,2},{1,3},{2,0},{3,1},{4,6},{5,7},{6,4},{7,5},{8,10},{9,11},{10,... | collective-permute-start | bytes 12296 | tf_op jit(solution)/shard_map/ppermute | solution.py:278
  14.5 11.5 %collective-permute-start.2 = (bf16[4,8,16,128]{3,2,1,0:T(8,128)(2,1)S(1)}, bf16[4,8,16,128]{3,2,1,0:T(8,128)(2,1)S(1)}, u32[]{:S(2)}, u32[]{:S(2)}) collective-permute-start(bf16[4,8,16,128]{3,2,1,0:T(8,128)(2,1)S(1)} %get-tuple-element.35), channel_id=1, source_target_pairs={{0,15},{1,2},{2,1},{3,4},{4,3},{5,6},{6,5},{7,8},{8,7},{9,10},{10,... | collective-permute-start | bytes 393224 | tf_op jit(solution)/shard_map/ppermute | solution.py:218
  17.9 8.1 %collective-permute-start.4 = (bf16[4,8,16,128]{3,2,1,0:T(8,128)(2,1)S(1)}, bf16[4,8,16,128]{3,2,1,0:T(8,128)(2,1)S(1)}, u32[]{:S(2)}, u32[]{:S(2)}) collective-permute-start(bf16[4,8,16,128]{3,2,1,0:T(8,128)(2,1)S(1)} %get-tuple-element.38), channel_id=1, source_target_pairs={{0,1},{1,0},{2,3},{3,2},{4,5},{5,4},{6,7},{7,6},{8,9},{9,8},{10,11... | collective-permute-start | bytes 393224 | tf_op jit(solution)/shard_map/ppermute | solution.py:218

commit v10 on v9

--- a/solution.py
+++ b/solution.py
@@ -191,10 +191,10 @@
 
 
 def final_kernel(
-    solution, residual, direction, image, from_across, from_within, sums,
-    solution_next, residual_next, step_length,
-):
-    whole = jnp.sum(sums[...], axis=0)
+    solution, residual, direction, image, from_across, from_within, *rest
+):
+    *held, solution_next, residual_next, step_length = rest
+    whole = tree_sum([part[...] for part in held])
     norm = jnp.concatenate([whole[:, 0:1], whole[:, 2:3]], axis=0)
     curvature = jnp.concatenate([whole[:, 1:2], whole[:, 3:4]], axis=0)
     step = norm / (curvature + EPSILON)
@@ -216,6 +216,27 @@
     outer = [(i, (i + 2 * (i % 2) - 1) % count) for i in range(count)]
     inner = [(i, i ^ 1) for i in range(count)]
     return lax.ppermute(across, "orbit", outer), lax.ppermute(within, "orbit", inner)
+
+
+def sum_steps(devices):
+    assert devices & (devices - 1) == 0
+    bits = [1 << b for b in range(devices.bit_length() - 1)]
+    return [bits[k : k + 2] for k in range(0, len(bits), 2)]
+
+
+def partners(array, bits):
+    devices = range(lax.axis_size("orbit"))
+    masks = [sum(bit for k, bit in enumerate(bits) if m >> k & 1) for m in range(1, 1 << len(bits))]
+    found = {
+        mask: lax.ppermute(array, "orbit", [(i, i ^ mask) for i in devices]) for mask in masks[::-1]
+    }
+    return [found[mask] for mask in masks]
+
+
+def tree_sum(parts):
+    while len(parts) > 1:
+        parts = [parts[k] + parts[k + 1] for k in range(0, len(parts), 2)]
+    return parts[0]
 
 
 def local(
@@ -274,8 +295,8 @@
         2 * jacobian.size,
         [pltpu.VMEM((2 * cols * species, probes, width), bf16)],
     )(crossing, rows, across, within, from_across, from_within, faced, norm, curved, jac)
-    assert devices % 4 == 0
-    twin = lax.ppermute(sums, "orbit", [(i, i ^ 2) for i in range(devices)])
+    steps = sum_steps(devices)
+    held = [sums] + partners(sums, steps[0])
 
     image, across, within = call(
         backward_kernel,
@@ -288,19 +309,19 @@
             pltpu.VMEM((2, rim) + column, f32),
         ],
     )(crossing, length_class, smooth_weight, weighted, jac, begun, from_across, from_within)
-    within, twin = lax.optimization_barrier((within, twin))
+    within, *held = lax.optimization_barrier((within, *held))
     from_across, from_within = swapped(across, within)
-    alike = [[i for i in range(devices) if i & 2 == side] for side in (0, 2)]
-    sums = jnp.broadcast_to((sums + twin)[None], (peers,) + sums.shape)
-    sums = lax.all_to_all(sums, "orbit", 0, 0, axis_index_groups=alike)
+    for step in steps[1:]:
+        sums = tree_sum(held)
+        held = [sums] + partners(sums, step)
 
     solution_next, residual_next, step_length = call(
         final_kernel,
         (whole, whole, shape((1, probes), f32)),
-        [VMEM()] * 7,
+        [VMEM()] * (6 + len(held)),
         8 * elements,
         28 * elements,
-    )(solution, residual, direction, image, from_across, from_within, sums)
+    )(solution, residual, direction, image, from_across, from_within, *held)
     return solution_next, residual_next, step_length.reshape(probes)
 
 

time: 27.5 us -> 27.6 us (level)
  blocking collectives: 8.12 us -> 0 us
  starting transfers between devices: 8.95 us -> 15.6 us
  waiting for transfers between devices: 0.01 us -> 1.6 us
    all_to_all x1 -> x0, blocking collectives: 8.12 us -> none  [local(): sums = lax.all_to_all(sums, 'orbit', 0, 0, axis_index_groups=alike)]
    ppermute x1 -> x6, starting transfers between devices: 0.05 us -> 6.65 us  [partners(): lax.ppermute(array, 'orbit', [(i, i ^ mask) for i in devices])]
    ppermute x1 -> x6, waiting for transfers between devices: 0.01 us -> 1.59 us  [partners(): lax.ppermute(array, 'orbit', [(i, i ^ mask) for i in devices])]
  transfers between devices with their start and end apart: 5 -> 10, of which waited for: 0 -> 2; matrix products, arithmetic and copies ran while one was open for 0% -> 0% of each run, Pallas kernels for 17% -> 17%
where the time goes in v10:
time: 27.6 us; the launch traced here: 27.4 us
  starting transfers between devices  15.6 us (57%)
  Pallas kernels  7.72 us (28%)
  waiting for transfers between devices  1.6 us (6%)
  between operations  1.41 us (5%)
  local copies, waits for them, and re-layouts  1.06 us (4%)
    ppermute x2, starting transfers between devices, swapped(): lax.ppermute(across, 'orbit', outer)  8.88 us
    ppermute x6, starting transfers between devices, partners(): lax.ppermute(array, 'orbit', [(i, i ^ mask) for i in devices])  6.65 us
    pallas_call x1, Pallas kernels, local(): call(inner_kernel, (shape((2 * cols,) + column, f32), shape((2, rim) + co...  3.06 us
    pallas_call x1, Pallas kernels, local(): call(forward_kernel, (shape((slots, probes, width), bf16), shape((probes...  1.88 us
    ppermute x6, waiting for transfers between devices, partners(): lax.ppermute(array, 'orbit', [(i, i ^ mask) for i in devices])  1.59 us
    pallas_call x1, Pallas kernels, local(): call(backward_kernel, (whole, near, near), [SMEM()] * 2 + [VMEM()] * 6, d...  1.51 us
    pallas_call x1, Pallas kernels, local(): call(final_kernel, (whole, whole, shape((1, probes), f32)), [VMEM()] * (6...  1.24 us
    unnamed x10, local copies, waits for them, and re-layouts  1.06 us
  transfers between devices with their start and end apart: 10, of which 2 were waited for; matrix products, arithmetic and copies ran while one was open for 0% of the time, Pallas kernels for 17%

profile of v10, /device:TPU:0, one launch (start us, length us, event | category | flops | bytes accessed | tf_op | source)
XLA Modules:
  0.0 27.4 jit_solution(11696945736236596900)
XLA Ops:
  0.6 0.0 copy-start
  0.6 1.0 %copy-done = f32[8,8,16,128]{3,2,1,0:T(8,128)S(1)} copy-done((f32[8,8,16,128]{3,2,1,0:T(8,128)S(1)}, f32[8,8,16,128]{3,2,1,0:T(8,128)}, u32[]{:S(2)}) %copy-start) | copy-done | bytes 524312
  1.7 5.5 %collective-permute-start = (bf16[4,8,16,128]{3,2,1,0:T(8,128)(2,1)S(1)}, bf16[4,8,16,128]{3,2,1,0:T(8,128)(2,1)S(1)}, u32[]{:S(2)}, u32[]{:S(2)}) collective-permute-start(bf16[4,8,16,128]{3,2,1,0:T(8,128)(2,1)S(1)} %get-tuple-element.29.across), channel_id=1, source_target_pairs={{0,15},{1,2},{2,1},{3,4},{4,3},{5,6},{6,5},{7,8},{8,7},{9,10},{10,... | collective-permute-start | bytes 393224 | tf_op jit(solution)/shard_map/ppermute | solution.py:218
  7.2 0.0 collective-permute-start.1
  7.9 0.0 copy-start.4
  7.9 3.1 %shard_map.112 = (f32[16,8,16,128]{3,2,1,0:T(8,128)S(1)}, f32[2,4,8,16,128]{4,3,2,1,0:T(8,128)S(1)}, f32[16,128]{1,0:T(8,128)S(1)}, f32[16,128]{1,0:T(8,128)S(1)...) custom-call(f32[8,8,16,128]{3,2,1,0:T(8,128)S(1)} %copy-done, ...), custom_call_target="tpu_custom_call" | custom-call | flops 7864320 | bytes 12582912 | tf_op jit(solution)/shard_map/pallas_call | solution.py:264
  11.0 0.0 collective-permute-done.from_across
  11.0 0.0 collective-permute-done.1.from_within
  11.0 0.0 copy-start.1
  11.0 0.0 copy-start.2
  11.0 0.0 copy-start.3
  11.0 1.9 %shard_map.114 = (bf16[8,16,128]{2,1,0:T(8,128)(2,1)S(1)}, f32[8,128]{1,0:T(8,128)S(1)}) custom-call(s32[8,24]{1,0:T(8,128)S(4)} %get-tuple-element.26.crossing, f32[8,128]{1,0:T(8,128)S(1)} %get-tuple-element.28.rows, bf16[4,8,16,128]{3,2,1,0:T(8,128)(2,1)S(1)} %get-tuple-element.29.across, bf16[4,8,16,128]{3,2,1,0:T(8,128)(2,1)S(1)} %get-tuple-element.30.within, ...), custom_call_target="tpu_custom_call" | custom-call | flops 100663296 | bytes 6291456 | tf_op jit(solution)/shard_map/pallas_call | solution.py:290
  12.9 0.1 collective-permute-start.5
  13.0 2.1 %collective-permute-start.4 = (f32[8,128]{1,0:T(8,128)S(1)}, f32[8,128]{1,0:T(8,128)S(1)}, u32[]{:S(2)}, u32[]{:S(2)}) collective-permute-start(f32[8,128]{1,0:T(8,128)S(1)} %get-tuple-element.42), channel_id=1, source_target_pairs={{0,2},{1,3},{2,0},{3,1},{4,6},{5,7},{6,4},{7,5},{8,10},{9,11},{10,... | collective-permute-start | bytes 12296 | tf_op jit(solution)/shard_map/ppermute | solution.py:231
  15.1 0.0 collective-permute-start.3
  15.1 0.0 copy-done.4
  15.1 1.5 %shard_map.115 = (f32[8,8,16,128]{3,2,1,0:T(8,128)S(1)}, bf16[4,8,16,128]{3,2,1,0:T(8,128)(2,1)S(1)}, bf16[4,8,16,128]{3,2,1,0:T(8,128)(2,1)S(1)}) custom-call(s32[8,24]{1,0:T(8,128)S(4)} %get-tuple-element.26.crossing, s32[128]{0:T(128)S(4)} %get-tuple-element.27.classes, f32[8,128]{1,0:T(8,128)S(1)} %copy-done.4, ...), custom_call_target="tpu_custom_call" | custom-call | flops 100663296 | bytes 6291456 | tf_op jit(solution)/shard_map/pallas_call | solution.py:301
  16.6 3.4 %collective-permute-start.2 = (bf16[4,8,16,128]{3,2,1,0:T(8,128)(2,1)S(1)}, bf16[4,8,16,128]{3,2,1,0:T(8,128)(2,1)S(1)}, u32[]{:S(2)}, u32[]{:S(2)}) collective-permute-start(bf16[4,8,16,128]{3,2,1,0:T(8,128)(2,1)S(1)} %get-tuple-element.38), channel_id=1, source_target_pairs={{0,15},{1,2},{2,1},{3,4},{4,3},{5,6},{6,5},{7,8},{8,7},{9,10},{10,... | collective-permute-start | bytes 393224 | tf_op jit(solution)/shard_map/ppermute | solution.py:218
  20.0 0.0 collective-permute-done.5
  20.0 0.0 collective-permute-done.4
  20.0 0.0 collective-permute-done.3
  20.0 0.1 collective-permute-start.6
  20.1 0.5 %collective-permute-start.9 = (f32[8,128]{1,0:T(8,128)S(1)}, f32[8,128]{1,0:T(8,128)S(1)}, u32[]{:S(2)}, u32[]{:S(2)}) collective-permute-start(f32[8,128]{1,0:T(8,128)S(1)} %add_add_fusion.rest_0_), channel_id=1, source_target_pairs={{0,12},{1,13},{2,14},{3,15},{4,8},{5,9},{6,10},{7,11},{8,4},{9,5},... | collective-permute-start | bytes 12296 | tf_op jit(solution)/shard_map/ppermute | solution.py:231
  20.6 0.0 collective-permute-start.8
  20.6 3.9 %collective-permute-start.7 = (f32[8,128]{1,0:T(8,128)S(1)}, f32[8,128]{1,0:T(8,128)S(1)}, u32[]{:S(2)}, u32[]{:S(2)}) collective-permute-start(f32[8,128]{1,0:T(8,128)S(1)} %add_add_fusion.rest_0_), channel_id=1, source_target_pairs={{0,4},{1,5},{2,6},{3,7},{4,0},{5,1},{6,2},{7,3},{8,12},{9,13},{10,... | collective-permute-start | bytes 12296 | tf_op jit(solution)/shard_map/ppermute | solution.py:231
  24.6 1.0 %collective-permute-done.9.rest_3_ = f32[8,128]{1,0:T(8,128)S(1)} collective-permute-done((f32[8,128]{1,0:T(8,128)S(1)}, f32[8,128]{1,0:T(8,128)S(1)}, u32[]{:S(2)}, u32[]{:S(2)}) %collective-permute-start.9) | collective-permute-done | bytes 4128 | tf_op jit(solution)/shard_map/ppermute | solution.py:231
  25.6 0.0 collective-permute-done.8.rest_2_
  25.6 0.6 %collective-permute-done.7.rest_1_ = f32[8,128]{1,0:T(8,128)S(1)} collective-permute-done((f32[8,128]{1,0:T(8,128)S(1)}, f32[8,128]{1,0:T(8,128)S(1)}, u32[]{:S(2)}, u32[]{:S(2)}) %collective-permute-start.7) | collective-permute-done | bytes 4128 | tf_op jit(solution)/shard_map/ppermute | solution.py:231
  26.1 0.0 collective-permute-done.2.from_across
  26.1 0.0 collective-permute-done.6.from_within
  26.1 0.0 copy-done.1
  26.2 1.2 %shard_map.116 = (f32[8,8,16,128]{3,2,1,0:T(8,128)}, f32[8,8,16,128]{3,2,1,0:T(8,128)}, f32[1,16]{1,0:T(1,128)}) custom-call(f32[8,8,16,128]{3,2,1,0:T(8,128)S(1)} %copy-done.3, f32[8,8,16,128]{3,2,1,0:T(8,128)S(1)} %copy-done.2, f32[8,8,16,128]{3,2,1,0:T(8,128)S(1)} %copy-done.1, f32[8,8,16,128]{3,2,1,0:T(8,128)S(1)} %get-tuple-element.37.image, ...), custom_call_target="tpu_custom_call" | custom-call | flops 1048576 | bytes 3670016 | tf_op jit(solution)/shard_map/pallas_call | solution.py:318
  (4 shorter events, 0.0 us)
Async XLA Ops:
  0.6 1.0 %copy-start = (f32[8,8,16,128]{3,2,1,0:T(8,128)S(1)}, f32[8,8,16,128]{3,2,1,0:T(8,128)}, u32[]{:S(2)}) copy-start(f32[8,8,16,128]{3,2,1,0:T(8,128)} %direction.5) | copy-start | bytes 1572868
  1.7 9.2 %collective-permute-start = (bf16[4,8,16,128]{3,2,1,0:T(8,128)(2,1)S(1)}, bf16[4,8,16,128]{3,2,1,0:T(8,128)(2,1)S(1)}, u32[]{:S(2)}, u32[]{:S(2)}) collective-permute-start(bf16[4,8,16,128]{3,2,1,0:T(8,128)(2,1)S(1)} %get-tuple-element.29.across), channel_id=1, source_target_pairs={{0,15},{1,2},{2,1},{3,4},{4,3},{5,6},{6,5},{7,8},{8,7},{9,10},{10,... | collective-permute-start | bytes 393224 | tf_op jit(solution)/shard_map/ppermute | solution.py:218
  7.2 3.7 %collective-permute-start.1 = (bf16[4,8,16,128]{3,2,1,0:T(8,128)(2,1)S(1)}, bf16[4,8,16,128]{3,2,1,0:T(8,128)(2,1)S(1)}, u32[]{:S(2)}, u32[]{:S(2)}) collective-permute-start(bf16[4,8,16,128]{3,2,1,0:T(8,128)(2,1)S(1)} %get-tuple-element.30.within), channel_id=1, source_target_pairs={{0,1},{1,0},{2,3},{3,2},{4,5},{5,4},{6,7},{7,6},{8,9},{9,8},{10,11... | collective-permute-start | bytes 393224 | tf_op jit(solution)/shard_map/ppermute | solution.py:218
  7.9 7.2 %copy-start.4 = (f32[8,128]{1,0:T(8,128)S(1)}, f32[8,128]{1,0:T(8,128)}, u32[]{:S(2)}) copy-start(f32[8,128]{1,0:T(8,128)} %smooth.1) | copy-start | bytes 12292
  11.0 15.2 %copy-start.1 = (f32[8,8,16,128]{3,2,1,0:T(8,128)S(1)}, f32[8,8,16,128]{3,2,1,0:T(8,128)}, u32[]{:S(2)}) copy-start(f32[8,8,16,128]{3,2,1,0:T(8,128)} %direction.5) | copy-start | bytes 1572868
  11.0 15.2 %copy-start.2 = (f32[8,8,16,128]{3,2,1,0:T(8,128)S(1)}, f32[8,8,16,128]{3,2,1,0:T(8,128)}, u32[]{:S(2)}) copy-start(f32[8,8,16,128]{3,2,1,0:T(8,128)} %residual.1) | copy-start | bytes 1572868
  11.0 15.2 %copy-start.3 = (f32[8,8,16,128]{3,2,1,0:T(8,128)S(1)}, f32[8,8,16,128]{3,2,1,0:T(8,128)}, u32[]{:S(2)}) copy-start(f32[8,8,16,128]{3,2,1,0:T(8,128)} %solution.1) | copy-start | bytes 1572868
  12.9 7.1 %collective-permute-start.5 = (f32[8,128]{1,0:T(8,128)S(1)}, f32[8,128]{1,0:T(8,128)S(1)}, u32[]{:S(2)}, u32[]{:S(2)}) collective-permute-start(f32[8,128]{1,0:T(8,128)S(1)} %get-tuple-element.42), channel_id=1, source_target_pairs={{0,3},{1,2},{2,1},{3,0},{4,7},{5,6},{6,5},{7,4},{8,11},{9,10},{10,... | collective-permute-start | bytes 12296 | tf_op jit(solution)/shard_map/ppermute | solution.py:231
  13.0 7.0 %collective-permute-start.4 = (f32[8,128]{1,0:T(8,128)S(1)}, f32[8,128]{1,0:T(8,128)S(1)}, u32[]{:S(2)}, u32[]{:S(2)}) collective-permute-start(f32[8,128]{1,0:T(8,128)S(1)} %get-tuple-element.42), channel_id=1, source_target_pairs={{0,2},{1,3},{2,0},{3,1},{4,6},{5,7},{6,4},{7,5},{8,10},{9,11},{10,... | collective-permute-start | bytes 12296 | tf_op jit(solution)/shard_map/ppermute | solution.py:231
  15.1 4.9 %collective-permute-start.3 = (f32[8,128]{1,0:T(8,128)S(1)}, f32[8,128]{1,0:T(8,128)S(1)}, u32[]{:S(2)}, u32[]{:S(2)}) collective-permute-start(f32[8,128]{1,0:T(8,128)S(1)} %get-tuple-element.42), channel_id=1, source_target_pairs={{0,1},{1,0},{2,3},{3,2},{4,5},{5,4},{6,7},{7,6},{8,9},{9,8},{10,11... | collective-permute-start | bytes 12296 | tf_op jit(solution)/shard_map/ppermute | solution.py:231
  16.6 9.5 %collective-permute-start.2 = (bf16[4,8,16,128]{3,2,1,0:T(8,128)(2,1)S(1)}, bf16[4,8,16,128]{3,2,1,0:T(8,128)(2,1)S(1)}, u32[]{:S(2)}, u32[]{:S(2)}) collective-permute-start(bf16[4,8,16,128]{3,2,1,0:T(8,128)(2,1)S(1)} %get-tuple-element.38), channel_id=1, source_target_pairs={{0,15},{1,2},{2,1},{3,4},{4,3},{5,6},{6,5},{7,8},{8,7},{9,10},{10,... | collective-permute-start | bytes 393224 | tf_op jit(solution)/shard_map/ppermute | solution.py:218
  20.0 6.1 %collective-permute-start.6 = (bf16[4,8,16,128]{3,2,1,0:T(8,128)(2,1)S(1)}, bf16[4,8,16,128]{3,2,1,0:T(8,128)(2,1)S(1)}, u32[]{:S(2)}, u32[]{:S(2)}) collective-permute-start(bf16[4,8,16,128]{3,2,1,0:T(8,128)(2,1)S(1)} %get-tuple-element.41), channel_id=1, source_target_pairs={{0,1},{1,0},{2,3},{3,2},{4,5},{5,4},{6,7},{7,6},{8,9},{9,8},{10,11... | collective-permute-start | bytes 393224 | tf_op jit(solution)/shard_map/ppermute | solution.py:218
  20.1 5.5 %collective-permute-start.9 = (f32[8,128]{1,0:T(8,128)S(1)}, f32[8,128]{1,0:T(8,128)S(1)}, u32[]{:S(2)}, u32[]{:S(2)}) collective-permute-start(f32[8,128]{1,0:T(8,128)S(1)} %add_add_fusion.rest_0_), channel_id=1, source_target_pairs={{0,12},{1,13},{2,14},{3,15},{4,8},{5,9},{6,10},{7,11},{8,4},{9,5},... | collective-permute-start | bytes 12296 | tf_op jit(solution)/shard_map/ppermute | solution.py:231
  20.6 4.9 %collective-permute-start.8 = (f32[8,128]{1,0:T(8,128)S(1)}, f32[8,128]{1,0:T(8,128)S(1)}, u32[]{:S(2)}, u32[]{:S(2)}) collective-permute-start(f32[8,128]{1,0:T(8,128)S(1)} %add_add_fusion.rest_0_), channel_id=1, source_target_pairs={{0,8},{1,9},{2,10},{3,11},{4,12},{5,13},{6,14},{7,15},{8,0},{9,1},... | collective-permute-start | bytes 12296 | tf_op jit(solution)/shard_map/ppermute | solution.py:231
  20.6 5.5 %collective-permute-start.7 = (f32[8,128]{1,0:T(8,128)S(1)}, f32[8,128]{1,0:T(8,128)S(1)}, u32[]{:S(2)}, u32[]{:S(2)}) collective-permute-start(f32[8,128]{1,0:T(8,128)S(1)} %add_add_fusion.rest_0_), channel_id=1, source_target_pairs={{0,4},{1,5},{2,6},{3,7},{4,0},{5,1},{6,2},{7,3},{8,12},{9,13},{10,... | collective-permute-start | bytes 12296 | tf_op jit(solution)/shard_map/ppermute | solution.py:231

commit v11 on v9

--- a/solution.py
+++ b/solution.py
@@ -46,12 +46,21 @@
     return lax.rem(lax.axis_index("orbit"), 2)
 
 
-def rounding_kernel(direction, across, within):
+def rounding_kernel(direction_hbm, direction, across, within, sems):
     rim = across.shape[0]
     odd = parity()
-    for c in range(rim):
-        across[c] = masked(direction[odd * rim + c]).astype(jnp.bfloat16)
-        within[c] = masked(direction[(1 - odd) * rim + c]).astype(jnp.bfloat16)
+    halves = ((odd, across), (1 - odd, within))
+    copies = []
+    for k, (place, _) in enumerate(halves):
+        half = pl.ds(place * rim, rim)
+        copies.append(
+            pltpu.make_async_copy(direction_hbm.at[half], direction.at[half], sems.at[k])
+        )
+        copies[-1].start()
+    for copy, (place, half) in zip(copies, halves):
+        copy.wait()
+        for c in range(rim):
+            half[c] = masked(direction[place * rim + c]).astype(jnp.bfloat16)
 
 
 def coupling(classes, cols, columns):
@@ -145,9 +154,8 @@
         picked = jnp.concatenate([window[crossing[i, j]] for j in range(crossings)], axis=1)
         tiles = jnp.concatenate([jac[i, j] for j in range(crossings)], axis=1)
         integrals = lax.dot_general(
-            tiles, picked, (((1,), (1,)), ((), ())), preferred_element_type=jnp.float32
+            picked, tiles, (((1,), (1,)), ((), ())), preferred_element_type=jnp.float32
         )
-        integrals = jnp.transpose(integrals)
         product = (rows[pl.ds(i, 1), :] * integrals).astype(jnp.bfloat16)
         weighted[i] = product
         total = total + product.astype(jnp.float32) * integrals
@@ -235,9 +243,14 @@
     whole = shape(direction.shape, f32)
     small = shape((probes, width), f32)
 
-    across, within = call(
-        rounding_kernel, (near, near), [VMEM()], 2 * elements, 6 * elements
-    )(direction)
+    held, across, within = call(
+        rounding_kernel,
+        (whole, near, near),
+        [HBM()],
+        2 * elements,
+        10 * elements,
+        [pltpu.SemaphoreType.DMA((2,))],
+    )(in_hbm(direction))
     from_across, from_within = swapped(across, within)
 
     begun, faced, norm, curved, rows, jac, crossing, length_class = call(
@@ -258,7 +271,7 @@
         ],
         [VMEM()] * 6 + [SMEM()] * 2,
     )(
-        direction, tile_count,
+        held, tile_count,
         *map(in_hbm, (
             residual, length_class, smooth_weight, sightline_weight, crossing, jacobian,
         )),

time: 27.5 us -> 27.4 us (level)
  local copies, waits for them, and re-layouts: 1.07 us -> 0.03 us
  Pallas kernels: 7.73 us -> 8.71 us
    pallas_call x1, Pallas kernels: 0.03 us -> 1.07 us  [local(): call(rounding_kernel, (whole, near, near), [HBM()], 2 * elements, 10 * el...]
    unnamed x10 -> x8, local copies, waits for them, and re-layouts: 1.06 us -> 0.03 us
where the time goes in v11:
time: 27.4 us; the launch traced here: 27.2 us
  starting transfers between devices  8.93 us (33%)
  Pallas kernels  8.71 us (32%)
  blocking collectives  8.12 us (30%)
  between operations  1.4 us (5%)
    ppermute x2, starting transfers between devices, swapped(): lax.ppermute(across, 'orbit', outer)  8.89 us
    all_to_all x1, blocking collectives, local(): sums = lax.all_to_all(sums, 'orbit', 0, 0, axis_index_groups=alike)  8.12 us
    pallas_call x1, Pallas kernels, local(): call(inner_kernel, (shape((2 * cols,) + column, f32), shape((2, rim) + co...  3.06 us
    pallas_call x1, Pallas kernels, local(): call(forward_kernel, (shape((slots, probes, width), bf16), shape((probes...  1.83 us
    pallas_call x1, Pallas kernels, local(): call(backward_kernel, (whole, near, near), [SMEM()] * 2 + [VMEM()] * 6, d...  1.52 us
    pallas_call x1, Pallas kernels, local(): call(final_kernel, (whole, whole, shape((1, probes), f32)), [VMEM()] * 7,...  1.24 us
    pallas_call x1, Pallas kernels, local(): call(rounding_kernel, (whole, near, near), [HBM()], 2 * elements, 10 * el...  1.07 us
  transfers between devices with their start and end apart: 5, of which 0 were waited for; matrix products, arithmetic and copies ran while one was open for 0% of the time, Pallas kernels for 17%

profile of v11, /device:TPU:0, one launch (start us, length us, event | category | flops | bytes accessed | tf_op | source)
XLA Modules:
  0.0 27.2 jit_solution(4694890285610395358)
XLA Ops:
  0.6 1.1 %shard_map.112 = (f32[8,8,16,128]{3,2,1,0:T(8,128)S(1)}, bf16[4,8,16,128]{3,2,1,0:T(8,128)(2,1)S(1)}, bf16[4,8,16,128]{3,2,1,0:T(8,128)(2,1)S(1)}) custom-call(f32[8,8,16,128]{3,2,1,0:T(8,128)} %direction.1), custom_call_target="tpu_custom_call" | custom-call | flops 262144 | bytes 1310720 | tf_op jit(solution)/shard_map/pallas_call | solution.py:246
  1.7 5.5 %collective-permute-start = (bf16[4,8,16,128]{3,2,1,0:T(8,128)(2,1)S(1)}, bf16[4,8,16,128]{3,2,1,0:T(8,128)(2,1)S(1)}, u32[]{:S(2)}, u32[]{:S(2)}) collective-permute-start(bf16[4,8,16,128]{3,2,1,0:T(8,128)(2,1)S(1)} %get-tuple-element.28.across), channel_id=1, source_target_pairs={{0,15},{1,2},{2,1},{3,4},{4,3},{5,6},{6,5},{7,8},{8,7},{9,10},{10,... | collective-permute-start | bytes 393224 | tf_op jit(solution)/shard_map/ppermute | solution.py:226
  7.2 0.0 collective-permute-start.1
  7.9 0.0 copy-start.3
  7.9 3.1 %shard_map.113 = (f32[16,8,16,128]{3,2,1,0:T(8,128)S(1)}, f32[2,4,8,16,128]{4,3,2,1,0:T(8,128)S(1)}, f32[16,128]{1,0:T(8,128)S(1)}, f32[16,128]{1,0:T(8,128)S(1)...) custom-call(f32[8,8,16,128]{3,2,1,0:T(8,128)S(1)} %get-tuple-element.24.d, ...), custom_call_target="tpu_custom_call" | custom-call | flops 7864320 | bytes 12582912 | tf_op jit(solution)/shard_map/pallas_call | solution.py:256
  11.0 0.0 collective-permute-done.from_across
  11.0 0.0 collective-permute-done.1.from_within
  11.0 0.0 copy-start
  11.0 0.0 copy-start.1
  11.0 0.0 copy-start.2
  11.0 1.8 %shard_map.114 = (bf16[8,16,128]{2,1,0:T(8,128)(2,1)S(1)}, f32[8,128]{1,0:T(8,128)S(1)}) custom-call(s32[8,24]{1,0:T(8,128)S(4)} %get-tuple-element.25.crossing, f32[8,128]{1,0:T(8,128)S(1)} %get-tuple-element.27.rows, bf16[4,8,16,128]{3,2,1,0:T(8,128)(2,1)S(1)} %get-tuple-element.28.across, bf16[4,8,16,128]{3,2,1,0:T(8,128)(2,1)S(1)} %get-tuple-element.29.within, ...), custom_call_target="tpu_custom_call" | custom-call | flops 100663296 | bytes 6291456 | tf_op jit(solution)/shard_map/pallas_call | solution.py:282
  12.8 0.0 collective-permute-start.3
  12.9 0.0 copy-done.3
  12.9 1.5 %shard_map.115 = (f32[8,8,16,128]{3,2,1,0:T(8,128)S(1)}, bf16[4,8,16,128]{3,2,1,0:T(8,128)(2,1)S(1)}, bf16[4,8,16,128]{3,2,1,0:T(8,128)(2,1)S(1)}) custom-call(s32[8,24]{1,0:T(8,128)S(4)} %get-tuple-element.25.crossing, s32[128]{0:T(128)S(4)} %get-tuple-element.26.classes, f32[8,128]{1,0:T(8,128)S(1)} %copy-done.3, ...), custom_call_target="tpu_custom_call" | custom-call | flops 100663296 | bytes 6291456 | tf_op jit(solution)/shard_map/pallas_call | solution.py:293
  14.4 3.4 %collective-permute-start.2 = (bf16[4,8,16,128]{3,2,1,0:T(8,128)(2,1)S(1)}, bf16[4,8,16,128]{3,2,1,0:T(8,128)(2,1)S(1)}, u32[]{:S(2)}, u32[]{:S(2)}) collective-permute-start(bf16[4,8,16,128]{3,2,1,0:T(8,128)(2,1)S(1)} %get-tuple-element.37), channel_id=1, source_target_pairs={{0,15},{1,2},{2,1},{3,4},{4,3},{5,6},{6,5},{7,8},{8,7},{9,10},{10,... | collective-permute-start | bytes 393224 | tf_op jit(solution)/shard_map/ppermute | solution.py:226
  17.8 0.0 collective-permute-done.3
  17.8 0.0 collective-permute-start.4
  17.8 8.1 %all_to_all.5.sums = f32[8,8,128]{2,1,0:T(8,128)S(1)} all-to-all(f32[8,8,128]{2,1,0:T(8,128)S(1)} %broadcast_in_dim.2), channel_id=1, replica_groups={{0,1,4,5,8,9,12,13},{2,3,6,7,10,11,14,15},{16,17,20,21,24,25,28,29},{18..., dimensions={0} | all-to-all | bytes 65536 | tf_op jit(solution)/shard_map/all_to_all | solution.py:308
  25.9 0.0 collective-permute-done.2.from_across
  25.9 0.0 collective-permute-done.4.from_within
  25.9 0.0 copy-done
  25.9 0.0 copy-done.1
  26.0 0.0 copy-done.2
  26.0 1.2 %shard_map.116 = (f32[8,8,16,128]{3,2,1,0:T(8,128)}, f32[8,8,16,128]{3,2,1,0:T(8,128)}, f32[1,16]{1,0:T(1,128)}) custom-call(f32[8,8,16,128]{3,2,1,0:T(8,128)S(1)} %copy-done.2, f32[8,8,16,128]{3,2,1,0:T(8,128)S(1)} %copy-done.1, f32[8,8,16,128]{3,2,1,0:T(8,128)S(1)} %copy-done, f32[8,8,16,128]{3,2,1,0:T(8,128)S(1)} %get-tuple-element.36.image, ...), custom_call_target="tpu_custom_call" | custom-call | flops 1048576 | bytes 3670016 | tf_op jit(solution)/shard_map/pallas_call | solution.py:310
  (2 shorter events, 0.0 us)
Async XLA Ops:
  1.7 9.2 %collective-permute-start = (bf16[4,8,16,128]{3,2,1,0:T(8,128)(2,1)S(1)}, bf16[4,8,16,128]{3,2,1,0:T(8,128)(2,1)S(1)}, u32[]{:S(2)}, u32[]{:S(2)}) collective-permute-start(bf16[4,8,16,128]{3,2,1,0:T(8,128)(2,1)S(1)} %get-tuple-element.28.across), channel_id=1, source_target_pairs={{0,15},{1,2},{2,1},{3,4},{4,3},{5,6},{6,5},{7,8},{8,7},{9,10},{10,... | collective-permute-start | bytes 393224 | tf_op jit(solution)/shard_map/ppermute | solution.py:226
  7.2 3.7 %collective-permute-start.1 = (bf16[4,8,16,128]{3,2,1,0:T(8,128)(2,1)S(1)}, bf16[4,8,16,128]{3,2,1,0:T(8,128)(2,1)S(1)}, u32[]{:S(2)}, u32[]{:S(2)}) collective-permute-start(bf16[4,8,16,128]{3,2,1,0:T(8,128)(2,1)S(1)} %get-tuple-element.29.within), channel_id=1, source_target_pairs={{0,1},{1,0},{2,3},{3,2},{4,5},{5,4},{6,7},{7,6},{8,9},{9,8},{10,11... | collective-permute-start | bytes 393224 | tf_op jit(solution)/shard_map/ppermute | solution.py:226
  7.9 5.0 %copy-start.3 = (f32[8,128]{1,0:T(8,128)S(1)}, f32[8,128]{1,0:T(8,128)}, u32[]{:S(2)}) copy-start(f32[8,128]{1,0:T(8,128)} %smooth.1) | copy-start | bytes 12292
  11.0 15.0 %copy-start = (f32[8,8,16,128]{3,2,1,0:T(8,128)S(1)}, f32[8,8,16,128]{3,2,1,0:T(8,128)}, u32[]{:S(2)}) copy-start(f32[8,8,16,128]{3,2,1,0:T(8,128)} %direction.1) | copy-start | bytes 1572868
  11.0 15.0 %copy-start.1 = (f32[8,8,16,128]{3,2,1,0:T(8,128)S(1)}, f32[8,8,16,128]{3,2,1,0:T(8,128)}, u32[]{:S(2)}) copy-start(f32[8,8,16,128]{3,2,1,0:T(8,128)} %residual.1) | copy-start | bytes 1572868
  11.0 15.0 %copy-start.2 = (f32[8,8,16,128]{3,2,1,0:T(8,128)S(1)}, f32[8,8,16,128]{3,2,1,0:T(8,128)}, u32[]{:S(2)}) copy-start(f32[8,8,16,128]{3,2,1,0:T(8,128)} %solution.1) | copy-start | bytes 1572868
  12.8 5.0 %collective-permute-start.3 = (f32[8,128]{1,0:T(8,128)S(1)}, f32[8,128]{1,0:T(8,128)S(1)}, u32[]{:S(2)}, u32[]{:S(2)}) collective-permute-start(f32[8,128]{1,0:T(8,128)S(1)} %get-tuple-element.39), channel_id=1, source_target_pairs={{0,2},{1,3},{2,0},{3,1},{4,6},{5,7},{6,4},{7,5},{8,10},{9,11},{10,... | collective-permute-start | bytes 12296 | tf_op jit(solution)/shard_map/ppermute | solution.py:291
  14.4 11.5 %collective-permute-start.2 = (bf16[4,8,16,128]{3,2,1,0:T(8,128)(2,1)S(1)}, bf16[4,8,16,128]{3,2,1,0:T(8,128)(2,1)S(1)}, u32[]{:S(2)}, u32[]{:S(2)}) collective-permute-start(bf16[4,8,16,128]{3,2,1,0:T(8,128)(2,1)S(1)} %get-tuple-element.37), channel_id=1, source_target_pairs={{0,15},{1,2},{2,1},{3,4},{4,3},{5,6},{6,5},{7,8},{8,7},{9,10},{10,... | collective-permute-start | bytes 393224 | tf_op jit(solution)/shard_map/ppermute | solution.py:226
  17.8 8.1 %collective-permute-start.4 = (bf16[4,8,16,128]{3,2,1,0:T(8,128)(2,1)S(1)}, bf16[4,8,16,128]{3,2,1,0:T(8,128)(2,1)S(1)}, u32[]{:S(2)}, u32[]{:S(2)}) collective-permute-start(bf16[4,8,16,128]{3,2,1,0:T(8,128)(2,1)S(1)} %get-tuple-element.40), channel_id=1, source_target_pairs={{0,1},{1,0},{2,3},{3,2},{4,5},{5,4},{6,7},{7,6},{8,9},{9,8},{10,11... | collective-permute-start | bytes 393224 | tf_op jit(solution)/shard_map/ppermute | solution.py:226
